TPU v7x, 32 devices: a whole 2x2x4 slice. The times are simulated.
32 devices in a mesh: side: 2 (over x), seq: 4 (over y, core), head: 4 (over z).
Axes of the slice: x: 2, y: 2, z: 4, core: 2. Of those that a mesh axis runs over, the one named last changes fastest.
Arguments:
- cached_hidden: bfloat16 [8, 3072, 8192], P('side', ('seq', 'head')), may hold values from -240 to 240
- page_order: int32 [8, 192], P('side', ('seq', 'head')), may hold values from 0 to 11, as said below
- lengths: int32 [8], P('side'), may hold values from 768 to 3072, as said below
- new_ids: int32 [8, 4], replicated, may hold values from 0 to 64511
- embedding: bfloat16 [64512, 8192], P('side', ('seq', 'head')), may hold values from -128 to 128
- query_proj: bfloat16 [8192, 8192], P(('seq', 'head')), may hold values from -0.15625 to 0.15625
- down_proj: bfloat16 [8192, 1024], P(('seq', 'head')), may hold values from -0.0625 to 0.0625
- key_up: bfloat16 [8, 64, 128], P('head'), may hold values from -0.75 to 0.75
- value_up: bfloat16 [8, 64, 128], P('head'), may hold values from -1.5 to 1.5
- out_proj: bfloat16 [8192, 8192], P('head', 'seq'), may hold values from -0.0625 to 0.0625
Outputs:
- attended: bfloat16 [8, 4, 8192], P('side', None, 'seq')
Inputs may be any that keep to these rules, and one draw needn't show every extreme that they name: `lengths`: each request's number of cached tokens; in every draw some request has exactly 3072. `page_order`: in each row every aligned run of 12 entries holds each number once; entry j of run b names the page of run b's 192 positions in which the request's logical page j of that run is stored.
All inputs are finite; a program needn't handle non-finite values.
Results may differ from a plain program's by a relative error of at most 0.012.
The roundings to bfloat16 on the way count: a program that leaves them out, or rounds other values in their place, can miss the bound.
Values may be sent and summed in bfloat16 or wider, within the bound.
No kernel may reach another device: no remote copies, remote signals or barrier semaphores. Data moves between devices by JAX's collectives and lax.ppermute only.
A program may use at most 128 MiB of HBM per device.

v0:
```python
import math

import jax
import jax.numpy as jnp
from jax import lax
from jax.sharding import PartitionSpec as P

D = 8192
HQ = 64
KVH = 8
HD = 128
PAGE = 16


rope_base = 500000.0
masked_score = -1e30


def combined_all(value, axis, join):
    pieces = jax.tree.map(lambda part: lax.all_gather(part, axis), value)
    head = jax.tree.map(lambda part: part[0], pieces)
    tail = jax.tree.map(lambda part: part[1:], pieces)
    subtotal, _ = lax.scan(lambda subtotal, section: (join(subtotal, section), None), head, tail)
    return subtotal


def rotate(values, positions):
    half_width = values.shape[-1] // 2
    frequency = 1.0 / rope_base ** (
        jnp.arange(half_width, dtype=jnp.float32) * 2.0 / values.shape[-1]
    )
    angles = positions.astype(jnp.float32)[..., None] * frequency
    cosine = jnp.cos(angles)
    sines = jnp.sin(angles)
    lower_half = values[..., :half_width]
    upper_half = values[..., half_width:]
    return jnp.concatenate(
        [lower_half * cosine - upper_half * sines, upper_half * cosine + lower_half * sines],
        axis=-1,
    )


def rebuild(latent, positions, key_up, value_up):
    latent_rank = key_up.shape[1]
    rebuilt_keys = jnp.einsum(
        "...gc,gcd->...gd", latent[..., :latent_rank], key_up, preferred_element_type=jnp.float32
    )
    rebuilt_keys = rotate(rebuilt_keys, positions[..., None]).astype(jnp.bfloat16)
    rebuilt_values = jnp.einsum(
        "...gc,gcd->...gd", latent[..., latent_rank:], value_up, preferred_element_type=jnp.float32
    )
    return (rebuilt_keys, rebuilt_values.astype(jnp.bfloat16))


def combine(earlier, latter):
    peak_early, total_early, summed_early = earlier
    peak_late, total_late, summed_late = latter
    joint_peak = jnp.maximum(peak_early, peak_late)
    weight_early = jnp.exp(peak_early - joint_peak)
    weight_late = jnp.exp(peak_late - joint_peak)
    joint_total = total_early * weight_early + total_late * weight_late
    joint_summed = summed_early * weight_early[..., None] + summed_late * weight_late[..., None]
    return (joint_peak, joint_total, joint_summed)


def local(
    cached_hidden,
    page_order,
    lengths,
    new_ids,
    embedding,
    query_proj,
    down_proj,
    key_up,
    value_up,
    out_proj,
):
    req_side, len_dev, model_width = cached_hidden.shape
    vocab_half = embedding.shape[0]
    side_index = lax.axis_index("side")
    seq_index = lax.axis_index("seq")
    head_index = lax.axis_index("head")
    head_count = lax.axis_size("head")
    requests, steps = new_ids.shape
    local_ids = new_ids.reshape(-1) - side_index * vocab_half
    inside = (local_ids >= 0) & (local_ids < vocab_half)
    picked = jnp.take(embedding, jnp.clip(local_ids, 0, vocab_half - 1), axis=0)
    picked = jnp.where(inside[:, None], picked, jnp.zeros_like(picked))
    query_part = jnp.dot(picked, query_proj, preferred_element_type=jnp.float32).reshape(
        requests, steps, -1
    )
    latent_part = jnp.dot(picked, down_proj, preferred_element_type=jnp.float32).reshape(
        requests, steps, -1
    )
    widened = picked.astype(jnp.float32)
    square_part = jnp.sum(widened * widened, axis=-1).reshape(requests, steps)
    query_all, latent_all, square_all = lax.psum(
        (query_part, latent_part, square_part), ("side", "seq", "head")
    )
    first_request = side_index * req_side
    query_sum = lax.dynamic_slice_in_dim(query_all, first_request, req_side, 0)
    latent_sum = lax.dynamic_slice_in_dim(latent_all, first_request, req_side, 0)
    square_sum = lax.dynamic_slice_in_dim(square_all, first_request, req_side, 0)
    inv_rms = lax.rsqrt(square_sum / D + 1e-05)
    local_heads = HQ // head_count
    local_groups = key_up.shape[0]
    latent_width = down_proj.shape[1] // KVH
    query_cols = lax.dynamic_slice_in_dim(
        query_sum, head_index * local_heads * HD, local_heads * HD, 2
    )
    query_cols = query_cols.reshape(req_side, steps, local_heads, HD) * inv_rms[:, :, None, None]
    fresh_positions = lengths[:, None] + jnp.arange(steps, dtype=jnp.int32)[None, :]
    queries = rotate(query_cols, fresh_positions[..., None]).astype(jnp.bfloat16)
    queries = queries.reshape(req_side, steps, local_groups, local_heads // local_groups, HD)
    fresh_cols = lax.dynamic_slice_in_dim(
        latent_sum, head_index * local_groups * latent_width, local_groups * latent_width, 2
    )
    fresh_latent = (
        fresh_cols.reshape(req_side, steps, local_groups, latent_width) * inv_rms[:, :, None, None]
    ).astype(jnp.bfloat16)
    fresh_keys, fresh_values = rebuild(fresh_latent, fresh_positions, key_up, value_up)
    token_rows = cached_hidden.reshape(req_side * len_dev, model_width)
    latent = jnp.dot(
        token_rows,
        lax.all_gather(down_proj, ("seq", "head"), axis=0, tiled=True),
        preferred_element_type=jnp.float32,
    )
    latent = latent.astype(jnp.bfloat16)
    pages = len_dev // PAGE
    page_rows = latent.reshape(req_side * pages, PAGE * latent.shape[-1])
    wanted = (jnp.arange(req_side, dtype=jnp.int32)[:, None] * pages + page_order).reshape(-1)
    ordered = jnp.take(page_rows, wanted, axis=0).reshape(req_side, len_dev, KVH, latent_width)
    received = lax.all_to_all(ordered, "head", split_axis=2, concat_axis=1, tiled=True)
    span = received.shape[1]
    positions = seq_index * span + jnp.arange(span, dtype=jnp.int32)
    cache_keys, cache_values = rebuild(received, positions, key_up, value_up)
    scaling = 1.0 / math.sqrt(HD)
    cache_scores = (
        jnp.einsum("rtgjd,rpgd->rtgjp", queries, cache_keys, preferred_element_type=jnp.float32)
        * scaling
    )
    fresh_scores = (
        jnp.einsum("rtgjd,rugd->rtgju", queries, fresh_keys, preferred_element_type=jnp.float32)
        * scaling
    )
    live = (positions[None, :] < lengths[:, None])[:, None, None, None, :]
    causal = (jnp.arange(steps)[:, None] >= jnp.arange(steps)[None, :]) & (seq_index == 0)
    seen = causal[None, :, None, None, :]
    cache_scores = jnp.where(live, cache_scores, masked_score)
    fresh_scores = jnp.where(seen, fresh_scores, masked_score)
    row_peak = jnp.maximum(jnp.max(cache_scores, axis=-1), jnp.max(fresh_scores, axis=-1))
    cache_weights = jnp.where(live, jnp.exp(cache_scores - row_peak[..., None]), 0.0)
    fresh_weights = jnp.where(seen, jnp.exp(fresh_scores - row_peak[..., None]), 0.0)
    totals = jnp.sum(cache_weights, axis=-1) + jnp.sum(fresh_weights, axis=-1)
    summed = jnp.einsum(
        "rtgjp,rpgd->rtgjd",
        cache_weights.astype(jnp.bfloat16),
        cache_values,
        preferred_element_type=jnp.float32,
    )
    summed = summed + jnp.einsum(
        "rtgju,rugd->rtgjd",
        fresh_weights.astype(jnp.bfloat16),
        fresh_values,
        preferred_element_type=jnp.float32,
    )
    row_peak, totals, summed = combined_all((row_peak, totals, summed), "seq", combine)
    context = (summed / totals[..., None]).astype(jnp.bfloat16).reshape(req_side * steps, -1)
    partial_out = jnp.dot(context, out_proj, preferred_element_type=jnp.float32)
    attended = lax.psum(partial_out, "head")
    return attended.astype(jnp.bfloat16).reshape(req_side, steps, -1)


def solution(mesh):
    return jax.shard_map(
        local,
        mesh=mesh,
        in_specs=(
            P("side", ("seq", "head"), None),
            P("side", ("seq", "head")),
            P("side"),
            P(),
            P("side", ("seq", "head")),
            P(("seq", "head"), None),
            P(("seq", "head"), None),
            P("head", None, None),
            P("head", None, None),
            P("head", "seq"),
        ),
        out_specs=P("side", None, "seq"),
        check_vma=False,
    )
```

profile of v0, /device:TPU:0, one launch (start us, length us, event | category | flops | bytes accessed | tf_op | source)
XLA Modules:
  0.0 307.8 jit_solution(5246368960718417951)
XLA Ops:
  7.4 0.7 all-gather.5.cloned.1.call-update
  10.0 1.9 gather_fusion.1
  11.9 1.6 fusion.70
  14.2 5.0 %fusion.71 = f32[32,8192]{1,0:T(8,128)S(1)} fusion(bf16[512,8192]{1,0:T(8,128)(2,1)} %param.17, bf16[32,512]{1,0:T(8,128)(2,1)S(1)} %gather_fusion.1, pred[32]{0:T(512)(128)(4,1)S(1)} %compare_and_fusion, pred[32]{0:T(512)(128)(4,1)S(1)} %and.40), kind=kOutput, calls=%fused_computation.104 | convolution fusion | flops 268468224 | bytes 9470016 | tf_op jit(solution)/shard_map/dot_general | solution.py:89
  19.2 1.3 reshape.325
  21.3 43.5 %psum.29 = f32[8,4]{1,0:T(8,128)S(1)} all-reduce(f32[8,4]{1,0:T(8,128)S(1)} %reshape.327), channel_id=1, replica_groups=mesh['side'=2,'seq'=4,'head'=4] {'side','seq','head'}, use_global_device_ids=true, to_apply=%region_2.3 | all-reduce | flops 32 | bytes 256 | tf_op jit(solution)/shard_map/psum | solution.py:97
  64.9 78.2 %all-gather.5.cloned.1.call-done = bf16[8192,1024]{1,0:T(8,128)(2,1)} async-done(((bf16[512,1024]{1,0:T(8,128)(2,1)}), bf16[8192,1024]{1,0:T(8,128)(2,1)}) %all-gather.5.cloned.1.call-update) | async-done | bytes 16777232 | tf_op jit(solution)/shard_map/all_gather | solution.py:125
  143.1 18.8 %convolution_convert_fusion.1 = bf16[768,1024]{1,0:T(8,128)(2,1)S(1)} fusion(bf16[768,8192]{1,0:T(8,128)(2,1)} %bitcast.108, bf16[8192,1024]{1,0:T(8,128)(2,1)} %all-gather.5.cloned.1.call-done), kind=kOutput, calls=%fused_computation.15 | convolution fusion | flops 12885688320 | bytes 30932992 | tf_op jit(solution)/shard_map/dot_general | solution.py:123
  161.9 0.8 reshape.323
  162.7 1.5 gather_fusion
  164.3 0.8 gather.11
  165.1 1.4 copy_select_fusion
  166.5 3.7 %all-to-all-start = ((bf16[4,192,8,128]{3,1,0,2:T(8,128)(2,1)}), bf16[4,192,8,128]{3,1,0,2:T(8,128)(2,1)S(1)}, u32[]{:S(2)}, u32[]{:S(2)}) async-start(bf16[4,192,8,128]{3,1,0,2:T(8,128)(2,1)} %copy_select_fusion), calls=%async_computation | async-start | bytes 3145728 | tf_op jit(solution)/shard_map/all_to_all | solution.py:133
  170.5 1.4 multiply_cosine_fusion
  171.9 77.0 %all-reduce.4.cloned.1.call-done = (f32[8,4,8192]{2,1,0:T(4,128)}, f32[8,4,1024]{2,1,0:T(4,128)}) async-done(((f32[8,4,8192]{2,1,0:T(4,128)}, f32[8,4,1024]{2,1,0:T(4,128)}), (f32[8,4,8192]{2,1,0:T(4,128)}, f32[8,4,1024]{2,1,0:T(4,128)})) %all-reduce.4.cloned.1.call-update) | async-done | bytes 1179664 | tf_op jit(solution)/shard_map/psum | solution.py:97
  248.9 1.0 constant_dynamic-slice_fusion.2
  250.0 0.8 fusion.59
  254.8 5.2 %all-gather.1 = f32[16,4,2,8]{3,1,2,0:T(4,128)S(1)} all-gather(f32[4,4,2,8]{3,1,2,0:T(4,128)S(1)} %add.168), channel_id=3, replica_groups=mesh['side'=2,'seq'=4,'head'=4] {'seq'}, dimensions={0}, use_global_device_ids=true | all-gather | bytes 5120 | tf_op jit(solution)/shard_map/all_gather | solution.py:20
  260.0 5.2 %all-gather = f32[16,4,2,8]{3,1,2,0:T(4,128)S(1)} all-gather(f32[4,4,2,8]{3,1,2,0:T(4,128)S(1)} %max.24), channel_id=2, replica_groups=mesh['side'=2,'seq'=4,'head'=4] {'seq'}, dimensions={0}, use_global_device_ids=true | all-gather | bytes 5120 | tf_op jit(solution)/shard_map/all_gather | solution.py:20
  265.6 0.9 fusion.28
  266.5 7.4 %all-gather.2 = f32[16,4,2,8,128]{4,3,2,1,0:T(8,128)S(1)} all-gather(f32[4,4,2,8,128]{4,3,2,1,0:T(8,128)S(1)} %copy.49), channel_id=4, replica_groups=mesh['side'=2,'seq'=4,'head'=4] {'seq'}, dimensions={0}, use_global_device_ids=true | all-gather | bytes 655360 | tf_op jit(solution)/shard_map/all_gather | solution.py:20
  274.1 0.8 while.14
  275.0 4.6 %fusion.75 = f32[16,2048]{1,0:T(8,128)S(1)} fusion(bf16[16,2048]{1,0:T(8,128)(2,1)S(1)} %reshape.330, bf16[2048,2048]{1,0:T(8,128)(2,1)} %param.21), kind=kOutput, calls=%fused_computation.107 | convolution fusion | flops 134217728 | bytes 8585216 | tf_op jit(solution)/shard_map/dot_general | solution.py:169
  279.6 20.2 %all-reduce.5 = bf16[16,2048]{1,0:T(8,128)(2,1)S(1)} all-reduce(f32[16,2048]{1,0:T(8,128)S(1)} %fusion.75), channel_id=1, replica_groups=mesh['side'=2,'seq'=4,'head'=4] {'head'}, use_global_device_ids=true, to_apply=%region_10.11 | all-reduce | flops 32768 | bytes 196608 | tf_op jit(solution)/shard_map/psum | solution.py:170
  (90 shorter events, 9.3 us)
Async XLA Ops:
  7.4 243.5 %copy-start = (bf16[2,64,128]{2,1,0:T(8,128)(2,1)S(1)}, bf16[2,64,128]{2,1,0:T(8,128)(2,1)}, u32[]{:S(2)}) copy-start(bf16[2,64,128]{2,1,0:T(8,128)(2,1)} %param.19) | copy-start | bytes 98308
  7.4 135.7 %all-gather.5.cloned.1.call-start = ((), (), s32[]{:S(2)}) async-start(), calls=%async_computation.1 | async-start | bytes 17825792 | tf_op jit(solution)/shard_map/all_gather | solution.py:125
  8.1 240.8 %all-reduce.4.cloned.1.call-start = ((), (), s32[]{:S(2)}) async-start(), calls=%async_computation.2 | async-start | bytes 2359296 | tf_op jit(solution)/shard_map/psum | solution.py:97
  19.2 1.6 copy-start.8
  19.2 1.6 copy-start.7
  166.5 85.3 %all-to-all-start = ((bf16[4,192,8,128]{3,1,0,2:T(8,128)(2,1)}), bf16[4,192,8,128]{3,1,0,2:T(8,128)(2,1)S(1)}, u32[]{:S(2)}, u32[]{:S(2)}) async-start(bf16[4,192,8,128]{3,1,0,2:T(8,128)(2,1)} %copy_select_fusion), calls=%async_computation | async-start | bytes 3145728 | tf_op jit(solution)/shard_map/all_to_all | solution.py:133
  251.3 0.6 copy-start.4
  252.1 0.9 copy-start.1
  253.0 0.8 copy-start.5
  253.8 11.4 %copy-start.6 = (bf16[2,64,128]{2,1,0:T(8,128)(2,1)S(1)}, bf16[2,64,128]{2,1,0:T(8,128)(2,1)}, u32[]{:S(2)}) copy-start(bf16[2,64,128]{2,1,0:T(8,128)(2,1)} %param.20) | copy-start | bytes 98308
  260.0 6.4 %copy-start.2 = (f32[16,4,2,8]{3,1,2,0:T(4,128)}, f32[16,4,2,8]{3,1,2,0:T(4,128)S(1)}, u32[]{:S(2)}) copy-start(f32[16,4,2,8]{3,1,2,0:T(4,128)S(1)} %all-gather.1) | copy-start | bytes 12292
  265.2 1.2 copy-start.3
  266.5 7.5 %slice-start = ((f32[16,4,2,8]{3,1,2,0:T(4,128)}), f32[4,4,2,8]{3,1,2,0:T(4,128)S(1)}, s32[]{:S(2)}) async-start(f32[16,4,2,8]{3,1,2,0:T(4,128)} %copy-done.2), calls=%async_computation.3 | async-start | bytes 32768 | tf_op jit(solution)/shard_map/slice | solution.py:21
  266.5 7.5 %slice-start.2 = ((f32[16,4,2,8]{3,1,2,0:T(4,128)}), f32[4,4,2,8]{3,1,2,0:T(4,128)S(1)}, s32[]{:S(2)}) async-start(f32[16,4,2,8]{3,1,2,0:T(4,128)} %copy-done.3), calls=%async_computation.5 | async-start | bytes 32768 | tf_op jit(solution)/shard_map/slice | solution.py:21
  266.5 7.5 %slice-start.1 = ((f32[16,4,2,8]{3,1,2,0:T(4,128)}), f32[12,4,2,8]{3,1,2,0:T(4,128)S(1)}, s32[]{:S(2)}) async-start(f32[16,4,2,8]{3,1,2,0:T(4,128)} %copy-done.2), calls=%async_computation.4 | async-start | bytes 98304 | tf_op jit(solution)/shard_map/slice | solution.py:22
  266.5 7.5 %slice-start.3 = ((f32[16,4,2,8]{3,1,2,0:T(4,128)}), f32[12,4,2,8]{3,1,2,0:T(4,128)S(1)}, s32[]{:S(2)}) async-start(f32[16,4,2,8]{3,1,2,0:T(4,128)} %copy-done.3), calls=%async_computation.6 | async-start | bytes 98304 | tf_op jit(solution)/shard_map/slice | solution.py:22
Sparse Core Ops, SparseCore 0:
  10.4 132.6 all-gather.4
Sparse Core Ops, SparseCore 1:
  20.6 228.3 all-reduce.3
where the time goes:
time: 309 us; the launch traced here: 308 us
  waiting for transfers between devices  156 us (50%)
  blocking collectives  81.6 us (26%)
  matrix products  32.8 us (11%)
  between operations  15.3 us (5%)
  local copies, waits for them, and re-layouts  10.6 us (3%)
  other arithmetic  7.68 us (2%)
  starting transfers between devices  3.79 us (1%)
    all_gather x1, waiting for transfers between devices, local(): lax.all_gather(down_proj, ('seq', 'head'), axis=0, tiled=True)  78.2 us
    psum x1, waiting for transfers between devices, local(): lax.psum((query_part, latent_part, square_part), ('side', 'seq', 'head'))  77 us
    psum x1, blocking collectives, local(): lax.psum((query_part, latent_part, square_part), ('side', 'seq', 'head'))  43.5 us
    psum x1, blocking collectives, local(): attended = lax.psum(partial_out, 'head')  20.2 us
    dot_general x1, matrix products, local(): jnp.dot(token_rows, lax.all_gather(down_proj, ('seq', 'head'), axis=0, ti...  18.8 us
    all_gather x3, blocking collectives, combined_all(): pieces = jax.tree.map(lambda part: lax.all_gather(part, axis), value)  17.9 us
  transfers between devices with their start and end apart: 3, of which 2 were waited for; matrix products, arithmetic and copies ran while one was open for 13% of the time, Pallas kernels for 0%

commit v1 on v0

v1 whole, which is shorter than its diff:
```python
import functools
import math

import jax
import jax.numpy as jnp
from jax import lax
from jax.experimental import pallas as pl
from jax.experimental.pallas import tpu as pltpu
from jax.sharding import PartitionSpec as P

D = 8192
HQ = 64
KVH = 8
HD = 128
RANK = 64
PAGE = 16
FRESH = 16

AXES = ("side", "seq", "head")
rope_base = 500000.0
masked_score = -1e30
BF = jnp.bfloat16
F32 = jnp.float32


def sincos(positions):
    half = HD // 2
    frequency = 1.0 / rope_base ** (jnp.arange(half, dtype=F32) * 2.0 / HD)
    angles = positions.astype(F32)[..., None] * frequency
    cosine, sines = jnp.cos(angles), jnp.sin(angles)
    return (
        jnp.concatenate([cosine, cosine], axis=-1),
        jnp.concatenate([-sines, sines], axis=-1),
    )


class Grid:
    def __init__(self):
        self.sides, self.seqs, self.heads = (lax.axis_size(a) for a in AXES)
        self.ys = self.seqs // 2
        self.side, seq, self.z = (lax.axis_index(a) for a in AXES)
        self.y, self.c = lax.div(seq, 2), lax.rem(seq, 2)

    def send(self, value, side=0, y=0, core=0, head=0):
        pairs = []
        for a in range(self.sides):
            for b in range(self.ys):
                for c in range(2):
                    for d in range(self.heads):
                        to = (
                            (a + side) % self.sides,
                            (b + y) % self.ys,
                            (c + core) % 2,
                            (d + head) % self.heads,
                        )
                        pairs.append((self.flat(a, b, c, d), self.flat(*to)))
        return lax.ppermute(value, AXES, pairs)

    def place(self, dy, dc, dz):
        seq = lax.rem(self.y + self.ys - dy, self.ys) * 2 + (1 - self.c if dc else self.c)
        return seq * self.heads + lax.rem(self.z + self.heads - dz, self.heads)

    def flat(self, a, b, c, d):
        return (a * self.seqs + b * 2 + c) * self.heads + d


def latent_kernel(counts, segments, depth, has_total, hidden_ref, *refs):
    pieces, refs = refs[: len(counts)], refs[len(counts) :]
    if has_total:
        before_ref, refs = refs[0], refs[1:]
    out_ref, hidden_buf, piece_buf, total, sems = refs
    grid = Grid()
    rows = hidden_ref.shape[0]
    whole = len(segments) + len(pieces)
    if has_total:
        load = pltpu.make_async_copy(before_ref, total, sems.at[whole])
        load.start()
    waits = []
    at = 0
    for i, count in enumerate(counts):
        copies = [
            pltpu.make_async_copy(
                pieces[i], piece_buf.at[pl.ds(at, count), :], sems.at[len(segments) + i]
            )
        ]
        inside = 0
        for k, (owner, extent, dy, dc, dz, base, step) in enumerate(segments):
            if owner == i:
                source = grid.place(dy, dc, dz) * depth + base + step * grid.side
                source = pl.multiple_of(source, 128)
                copies.append(
                    pltpu.make_async_copy(
                        hidden_ref.at[:, pl.ds(source, extent)],
                        hidden_buf.at[:, pl.ds(at + inside, extent)],
                        sems.at[k],
                    )
                )
                inside += extent
        for copy in copies:
            copy.start()
        waits.append((copies, at, count))
        at += count
    if has_total:
        load.wait()
    pairs = [waits[i : i + 2] for i in range(0, len(waits), 2)]
    stores = []
    for k, pair in enumerate(pairs):
        for copies, _, _ in pair:
            for copy in copies:
                copy.wait()
        first = pair[0][1]
        span = sum(count for _, _, count in pair)
        last = k == len(pairs) - 1
        tile = rows // 4 if last else rows
        for m in range(rows // tile):
            part = slice(m * tile, (m + 1) * tile)
            term = jnp.dot(
                hidden_buf[part, first : first + span],
                piece_buf[first : first + span, :],
                preferred_element_type=F32,
            )
            total[part, :] = total[part, :] + term if k or has_total else term
            if last:
                store = pltpu.make_async_copy(
                    total.at[pl.ds(m * tile, tile), :],
                    out_ref.at[pl.ds(m * tile, tile), :],
                    sems.at[whole + 1 + m],
                )
                store.start()
                stores.append(store)
    for store in stores:
        store.wait()


def add_latents(hidden, depth, batch, total=None):
    pieces = [piece for piece, _ in batch]
    counts = [piece.shape[0] for piece in pieces]
    segments = [(i, *part) for i, (_, parts) in enumerate(batch) for part in parts]
    deep, columns = sum(counts), pieces[0].shape[1]
    rows = hidden.shape[0]
    operands = [hidden, *pieces]
    if total is not None:
        operands.append(total)
    return pl.pallas_call(
        functools.partial(latent_kernel, counts, segments, depth, total is not None),
        out_shape=jax.ShapeDtypeStruct((rows, columns), F32),
        in_specs=[pl.BlockSpec(memory_space=pl.ANY)] * len(operands),
        out_specs=pl.BlockSpec(memory_space=pl.ANY),
        scratch_shapes=[
            pltpu.VMEM((rows, deep), BF),
            pltpu.VMEM((deep, columns), BF),
            pltpu.VMEM((rows, columns), F32),
            pltpu.SemaphoreType.DMA((len(segments) + len(pieces) + 5,)),
        ],
        compiler_params=pltpu.CompilerParams(vmem_limit_bytes=53 * 1024 * 1024),
        cost_estimate=pl.CostEstimate(
            flops=2 * rows * deep * columns,
            bytes_accessed=2 * deep * (rows + columns) + 8 * rows * columns,
            transcendentals=0,
        ),
        name="latents",
    )(*operands)


def assemble_kernel(layout, *refs):
    ins, outs = refs[: len(layout)], refs[len(layout) :]
    side = lax.axis_index("side")
    for source, (o, at, count, base, step) in zip(ins, layout):
        start = pl.multiple_of(base + step * side, 32)
        outs[o][at : at + count, :] = source[pl.ds(start, count), :]


def assemble(*arrays):
    layout, sources, shapes = [], [], []
    for o, parts in enumerate(arrays):
        at = 0
        for source, count, base, step in parts:
            layout.append((o, at, count, base, step))
            sources.append(source)
            at += count
        shapes.append(jax.ShapeDtypeStruct((at, source.shape[1]), source.dtype))
    return pl.pallas_call(
        functools.partial(assemble_kernel, layout),
        out_shape=shapes,
        name="assemble",
    )(*sources)


def in_three(value):
    high = value.astype(BF).astype(F32)
    middle = (value - high).astype(BF).astype(F32)
    return high, middle, value - high - middle


def attend_kernel(scale, span, lat_ref, fresh_ref, cos_ref, sin_ref, live_ref, query_ref, up_ref, out_ref):
    requests, groups, lanes, _ = query_ref.shape
    blocks = out_ref.shape[0]
    each = groups // blocks
    peaks, totals, summed = [], [], []
    for r in range(requests):
        latent = jnp.concatenate(
            [lat_ref[r * span : (r + 1) * span, :].astype(BF), fresh_ref[r]], axis=0
        )
        cosine, sines = cos_ref[r], sin_ref[r]
        columns, values = [], []
        for g in range(groups):
            at = g * 2 * RANK
            key = jnp.dot(latent[:, at : at + RANK], up_ref[g], preferred_element_type=F32)
            key = (key * cosine + pltpu.roll(key, HD // 2, 1) * sines).astype(BF)
            columns.append(
                lax.dot_general(
                    key, query_ref[r, g], (((1,), (1,)), ((), ())), preferred_element_type=F32
                )
            )
            values.append(latent[:, at + RANK : at + 2 * RANK])
        scores = jnp.concatenate(columns, axis=1) * scale
        live = live_ref[r] > 0
        live = jnp.concatenate([live] * (scores.shape[1] // live.shape[1]), axis=1)
        scores = jnp.where(live, scores, masked_score)
        peak = jnp.max(scores, axis=0, keepdims=True)
        weights = jnp.where(live, jnp.exp(scores - peak), 0.0)
        peaks.append(peak)
        totals.append(jnp.sum(weights, axis=0, keepdims=True))
        summed.append(
            lax.dot_general(
                jnp.concatenate(values, axis=1),
                weights.astype(BF),
                (((0,), (0,)), ((), ())),
                preferred_element_type=F32,
            )
        )
    for b in range(blocks):
        stats = []
        for i in range(each):
            g = b * each + i
            cut = slice(g * lanes, (g + 1) * lanes)
            out_ref[b, i * RANK : (i + 1) * RANK, :] = jnp.concatenate(
                [s[g * RANK : (g + 1) * RANK, cut] for s in summed], axis=1
            ).astype(BF)
            stats += in_three(jnp.concatenate([p[:, cut] for p in peaks], axis=1))
            stats += in_three(jnp.concatenate([t[:, cut] for t in totals], axis=1))
        stats += [jnp.zeros_like(stats[0])] * (16 - len(stats))
        out_ref[b, each * RANK :, :] = jnp.concatenate(stats, axis=0).astype(BF)


def attend(span, latent, fresh, cosine, sines, live, queries, key_up, blocks):
    requests, groups, lanes, _ = queries.shape
    rows = groups // blocks * RANK + 16
    return pl.pallas_call(
        functools.partial(attend_kernel, 1.0 / math.sqrt(HD), span),
        out_shape=jax.ShapeDtypeStruct((blocks, rows, requests * lanes), BF),
        compiler_params=pltpu.CompilerParams(vmem_limit_bytes=28 * 1024 * 1024),
        name="attend",
    )(latent, fresh, cosine, sines, live, queries, key_up)


def join(states):
    peak = functools.reduce(jnp.maximum, [p for p, _, _ in states])
    total, summed = 0.0, 0.0
    for p, t, s in states:
        weight = jnp.exp(p - peak)
        total = total + t * weight
        summed = summed + s * weight
    return peak, total, summed


def pack(states, out_ref):
    each = len(states)
    stats = []
    for i, (peak, total, summed) in enumerate(states):
        out_ref[i * RANK : (i + 1) * RANK, :] = summed
        stats += [peak, total]
    stats += [jnp.zeros_like(stats[0])] * (8 - len(stats))
    out_ref[each * RANK :, :] = jnp.concatenate(stats, axis=0)


def unpack(ref, each):
    at = each * RANK
    return [
        (ref[at + 2 * i : at + 2 * i + 1, :], ref[at + 2 * i + 1 : at + 2 * i + 2, :], ref[i * RANK : (i + 1) * RANK, :])
        for i in range(each)
    ]


def join_narrow_kernel(each, *refs):
    refs, out_ref = refs[:-1], refs[-1]
    states = []
    for i in range(each):
        parts = []
        for ref in refs:
            stats = ref[each * RANK :, :].astype(F32)
            at = 6 * i
            peak = stats[at : at + 1] + stats[at + 1 : at + 2] + stats[at + 2 : at + 3]
            total = stats[at + 3 : at + 4] + stats[at + 4 : at + 5] + stats[at + 5 : at + 6]
            parts.append((peak, total, ref[i * RANK : (i + 1) * RANK, :].astype(F32)))
        states.append(join(parts))
    pack(states, out_ref)


def join_narrow(parts):
    rows, lanes = parts[0].shape
    return pl.pallas_call(
        functools.partial(join_narrow_kernel, (rows - 16) // RANK),
        out_shape=jax.ShapeDtypeStruct((rows - 8, lanes), F32),
        name="join_narrow",
    )(*parts)


def join_wide_kernel(each, *refs):
    refs, out_ref = refs[:-1], refs[-1]
    parts = [unpack(ref, each) for ref in refs]
    pack([join([part[i] for part in parts]) for i in range(each)], out_ref)


def join_wide(parts):
    return pl.pallas_call(
        functools.partial(join_wide_kernel, (parts[0].shape[0] - 8) // RANK),
        out_shape=jax.ShapeDtypeStruct(parts[0].shape, F32),
        name="join_wide",
    )(*parts)


def context_kernel(requests, steps, *refs):
    up_ref, out_ref = refs[-2:]
    each = up_ref.shape[0]
    parts = [unpack(ref, each) for ref in refs[:-2]]
    lanes = refs[0].shape[1]
    rows = requests * steps
    heads = lanes // rows
    old = lax.broadcasted_iota(jnp.int32, (lanes, lanes), 0)
    new = lax.broadcasted_iota(jnp.int32, (lanes, lanes), 1)
    request, rest = old // (heads * steps), old % (heads * steps)
    moved = (rest // steps) * rows + request * steps + rest % steps
    order = jnp.where(moved == new, 1.0, 0.0).astype(BF)
    for i in range(each):
        _, total, summed = join([part[i] for part in parts])
        scaled = (summed / total).astype(BF)
        context = lax.dot_general(
            up_ref[i], scaled, (((0,), (0,)), ((), ())), preferred_element_type=F32
        ).astype(BF)
        context = lax.dot_general(
            order, context, (((0,), (1,)), ((), ())), preferred_element_type=F32
        ).astype(BF)
        for j in range(heads):
            at = (i * heads + j) * HD
            out_ref[:, at : at + HD] = context[j * rows : (j + 1) * rows, :]


def context_of(parts, value_up, requests, steps):
    rows = requests * steps
    columns = value_up.shape[0] * parts[0].shape[1] // rows * HD
    return pl.pallas_call(
        functools.partial(context_kernel, requests, steps),
        out_shape=jax.ShapeDtypeStruct((rows, columns), BF),
        name="context",
    )(*parts, value_up)


def take(stack, index):
    return lax.dynamic_index_in_dim(stack, index, 0, keepdims=False)


def tie(*values):
    leaves, tree = jax.tree.flatten(values)
    arrays = [i for i, leaf in enumerate(leaves) if getattr(leaf, "ndim", 0)]
    for i, leaf in zip(arrays, lax.optimization_barrier([leaves[i] for i in arrays])):
        leaves[i] = leaf
    return jax.tree.unflatten(tree, leaves)


def in_order(parts, mine):
    count = len(parts)
    if count == 2:
        swap = mine == 0
        return jnp.stack([jnp.where(swap, parts[0], parts[1]), jnp.where(swap, parts[1], parts[0])])
    twice = jnp.stack(parts[::-1] * 2)
    return lax.dynamic_slice_in_dim(twice, count - 1 - mine, count, 0)


def local(
    cached_hidden,
    page_order,
    lengths,
    new_ids,
    embedding,
    query_proj,
    down_proj,
    key_up,
    value_up,
    out_proj,
):
    grid = Grid()
    side, y, c, z = grid.side, grid.y, grid.c, grid.z
    ys, heads = grid.ys, grid.heads
    requests, span, width = cached_hidden.shape
    tokens, steps = new_ids.shape
    rows = requests * steps
    depth = down_proj.shape[0]
    hidden = cached_hidden.reshape(requests * span, width)

    def both(piece, *segments):
        placed = [
            [(rows, dy, dc, dz, base, step) for rows, dy, dz, base, step in segments]
            for dc in range(2)
        ]
        return [(piece, placed[0]), (grid.send(piece, core=1), placed[1])]

    def project_shared(own, between):
        b = depth // 4

        def edge(piece):
            return piece, b, 0, piece.shape[0] - b

        (r0,) = assemble([(own, 3 * b, 0, b)])
        r1 = grid.send(r0, head=1)
        y0 = grid.send(own, y=1)
        own_both = both(own, (4 * b, 0, 0, 0, 0))
        extra = between[0](r0)
        r1, y0, own_both, extra = tie(r1, y0, own_both, extra)
        r2 = grid.send(r1, head=1)
        y1 = grid.send(r1, y=1)
        extra = between[1](extra)
        r1, r2, y0, y1, extra = tie(r1, r2, y0, y1, extra)
        r3 = grid.send(r2, head=1)
        y2 = grid.send(r2, y=1)
        (edges,) = assemble([edge(r1), edge(r2), edge(y1)])
        x2 = grid.send(edges, side=1)
        r1_both = both(r1, (3 * b, 0, 1, 0, b))
        y0_both = both(y0, (4 * b, 1, 0, 0, 0))
        latent = add_latents(hidden, depth, own_both + r1_both + y0_both)
        extra = between[2](extra)
        r2, r3, y1, y2, x2, latent, extra = tie(r2, r3, y1, y2, x2, latent, extra)
        last, edges = assemble([(r3, 2 * b, 0, b)], [edge(r3), edge(y2)])
        last, edges, r2, y1 = tie(last, edges, r2, y1)
        y3 = grid.send(last, y=1)
        x3 = grid.send(edges, side=1)
        r2_both = both(r2, (3 * b, 0, 2, 0, b))
        y1_both = both(y1, (3 * b, 1, 1, 0, b))
        latent = add_latents(hidden, depth, r2_both + y1_both, latent)
        extra = between[3](extra)
        r3, y2, x2, x3, y3, latent, extra = tie(r3, y2, x2, x3, y3, latent, extra)
        x4 = grid.send(y3, side=1)
        x2_both = both(
            x2, (b, 0, 1, 3 * b, -3 * b), (b, 0, 2, 3 * b, -3 * b), (b, 1, 1, 3 * b, -3 * b)
        )
        r3_both = both(r3, (3 * b, 0, 3, 0, b))
        y2_both = both(y2, (3 * b, 1, 2, 0, b))
        latent = add_latents(hidden, depth, x2_both + r3_both + y2_both, latent)
        y3_both = both(y3, (2 * b, 1, 3, 0, 2 * b))
        x3_both = both(x3, (b, 0, 3, 3 * b, -3 * b), (b, 1, 2, 3 * b, -3 * b))
        extra = between[4](extra)
        x3_both, y3_both, latent, extra = tie(x3_both, y3_both, latent, extra)
        x4_both = both(x4, (2 * b, 1, 3, 2 * b, -2 * b))
        return add_latents(hidden, depth, x3_both + y3_both + x4_both, latent), extra

    def project_plain(own, between):
        latent, extra = None, own
        ring = own
        for k in range(heads):
            if k:
                ring = grid.send(ring, head=1)
            latent = add_latents(hidden, depth, both(ring, (depth, 0, k, 0, 0)), latent)
            for dy in range(1, ys):
                piece = grid.send(ring, y=dy)
                latent = add_latents(hidden, depth, both(piece, (depth, dy, k, 0, 0)), latent)
        for step in between:
            extra = step(extra)
        return latent, extra

    blocks = 2 * ys * heads
    query_width = query_proj.shape[1] // blocks
    latent_width = down_proj.shape[1] // blocks
    cut = query_width + latent_width

    def embed(after):
        ids, _ = tie(new_ids, after)
        vocab_half = embedding.shape[0]
        local_ids = ids.reshape(-1) - side * vocab_half
        inside = (local_ids >= 0) & (local_ids < vocab_half)
        picked = jnp.take(embedding, jnp.clip(local_ids, 0, vocab_half - 1), axis=0)
        picked = jnp.where(inside[:, None], picked, jnp.zeros_like(picked)).reshape(2, rows, -1)
        embedded = take(picked, side) + grid.send(take(picked, 1 - side), side=1)
        query_part = jnp.dot(embedded, query_proj, preferred_element_type=F32)
        latent_part = jnp.dot(embedded, down_proj, preferred_element_type=F32)
        widened = embedded.astype(F32)
        square_part = jnp.sum(widened * widened, axis=-1)
        packed = jnp.concatenate(
            [
                query_part.reshape(rows, blocks, query_width),
                latent_part.reshape(rows, blocks, latent_width),
                jnp.broadcast_to(square_part[:, None, None], (rows, blocks, 128 - latent_width)),
            ],
            axis=-1,
        ).transpose(1, 0, 2)
        packed = packed.reshape(2, ys, heads, rows, -1)
        packed = take(packed, c) + grid.send(take(packed, 1 - c), core=1)
        kept = take(packed, y)
        for dy in range(1, ys):
            kept = kept + grid.send(take(packed, (y + dy) % ys), y=dy)
        return kept

    def reduce_query(kept):
        mine = take(kept, z)
        for dz in range(1, heads):
            mine = mine + grid.send(take(kept, (z + dz) % heads), head=dz)
        return mine

    def spread_query(mine):
        inv_rms = lax.rsqrt(mine[:, -1:] / D + 1e-05)
        fresh_positions = lengths[:, None] + jnp.arange(steps, dtype=jnp.int32)[None, :]
        cos_new, sin_new = sincos(fresh_positions.reshape(-1))
        raw = (mine[:, :query_width] * inv_rms).reshape(rows, -1, HD)
        turned = jnp.concatenate([raw[..., HD // 2 :], raw[..., : HD // 2]], axis=-1)
        raw = raw * cos_new[:, None, :] + turned * sin_new[:, None, :]
        latent_new = mine[:, query_width : query_width + latent_width] * inv_rms
        block = jnp.concatenate(
            [raw.reshape(rows, -1).astype(BF), latent_new.astype(BF), key_up.reshape(rows, -1)], axis=-1
        )
        return block

    def spread_head(block):
        by_head = in_order([block] + [grid.send(block, head=k) for k in range(1, heads)], z)
        all_key_up = by_head[..., cut:].reshape(KVH, RANK, HD)
        return by_head[..., :cut], all_key_up

    def share_query(state):
        by_head, all_key_up = state
        by_y = in_order([by_head] + [grid.send(by_head, y=k) for k in range(1, ys)], y)
        by_core = in_order([by_y, grid.send(by_y, core=1)], c)
        by_block = by_core.reshape(blocks, rows, cut)
        queries = by_block[..., :query_width].reshape(blocks, requests, steps, -1, HD)
        queries = queries.transpose(1, 0, 3, 2, 4).reshape(requests, KVH, -1, HD)
        fresh = by_block[..., query_width:].transpose(1, 0, 2).reshape(requests, steps, -1)
        fresh = jnp.pad(fresh, ((0, 0), (0, FRESH - steps), (0, 0)))
        return queries, fresh, all_key_up

    pages = page_order.shape[1]
    logical = jnp.arange(pages, dtype=jnp.int32)
    page_of = jnp.sum(
        jnp.where(page_order[:, :, None] == logical[None, None, :], logical[None, :, None], 0), axis=1
    )
    start = ((y * 2 + c) * heads + z) * span
    positions = (
        start + page_of[:, :, None] * PAGE + jnp.arange(PAGE, dtype=jnp.int32)[None, None, :]
    ).reshape(requests, span)
    new_rows = jnp.arange(FRESH, dtype=jnp.int32)
    row_positions = jnp.concatenate(
        [positions, lengths[:, None] + jnp.minimum(new_rows, steps - 1)[None, :]], axis=1
    )
    cosine, sines = sincos(row_positions)
    lanes = max(128, HQ // KVH * steps)
    step_of = jnp.arange(lanes, dtype=jnp.int32) % steps
    holds_new = (y == 0) & (c == 0) & (z == 0)
    new_seen = (new_rows[:, None] <= step_of[None, :]) & holds_new
    live = jnp.concatenate(
        [
            jnp.broadcast_to((positions < lengths[:, None])[:, :, None], (requests, span, lanes)),
            jnp.broadcast_to(new_seen[None], (requests, FRESH, lanes)),
        ],
        axis=1,
    ).astype(F32)

    between = [embed, reduce_query, spread_query, spread_head, share_query]
    shared = ys == 2 and heads == 4 and grid.sides == 2 and depth % 512 == 0
    latent, extra = (project_shared if shared else project_plain)(down_proj, between)
    queries, fresh, all_key_up = extra
    states = attend(span, latent, fresh, cosine, sines, live, queries, all_key_up, heads)
    parts = [take(states, z)]
    for dz in range(1, heads):
        parts.append(grid.send(take(states, (z + dz) % heads), head=dz))
    state = join_narrow(parts)
    state = join_wide([state] + [grid.send(state, y=k) for k in range(1, ys)])
    context = context_of([state, grid.send(state, core=1)], value_up, requests, steps)
    partial_out = jnp.dot(context, out_proj, preferred_element_type=F32)
    sent = partial_out.astype(BF)
    attended = partial_out
    for dz in range(1, heads):
        attended = attended + grid.send(sent, head=dz).astype(F32)
    return attended.astype(BF).reshape(requests, steps, -1)


def solution(mesh):
    return jax.shard_map(
        local,
        mesh=mesh,
        in_specs=(
            P("side", ("seq", "head"), None),
            P("side", ("seq", "head")),
            P("side"),
            P(),
            P("side", ("seq", "head")),
            P(("seq", "head"), None),
            P(("seq", "head"), None),
            P("head", None, None),
            P("head", None, None),
            P("head", "seq"),
        ),
        out_specs=P("side", None, "seq"),
        check_vma=False,
    )
```

time: 309 us -> 177 us (0.57)
  waiting for transfers between devices: 156 us -> 58.7 us
  blocking collectives: 81.6 us -> 0 us
  Pallas kernels: 0 us -> 45.2 us
  starting transfers between devices: 3.79 us -> 38.8 us
  matrix products: 32.8 us -> 10.7 us
  between operations: 15.3 us -> 0.58 us
  local copies, waits for them, and re-layouts: 10.6 us -> 15.5 us
    all_gather x1 -> x0, waiting for transfers between devices: 78.2 us -> none  [local(): lax.all_gather(down_proj, ('seq', 'head'), axis=0, tiled=True)]
    psum x1 -> x0, waiting for transfers between devices: 77 us -> none  [local(): lax.psum((query_part, latent_part, square_part), ('side', 'seq', 'head'))]
    psum x2 -> x0, blocking collectives: 63.7 us -> none  [the longest x1 43.5 us: local(): lax.psum((query_part, latent_part, square_part), ('side', 'seq', 'head'))]
    ppermute x0 -> x40, waiting for transfers between devices: none -> 58.7 us  [send(): return lax.ppermute(value, AXES, pairs)]
    pallas_call x0 -> x11, Pallas kernels: none -> 45.2 us  [the longest x4 28.8 us: add_latents(): pl.pallas_call(functools.partial(latent_kernel, counts, segments, depth,...]
    ppermute x0 -> x40, starting transfers between devices: none -> 38.8 us  [send(): return lax.ppermute(value, AXES, pairs)]
    dot_general x10 -> x3, matrix products: 32.8 us -> 10.7 us  [the longest x1 4.61 us: local(): partial_out = jnp.dot(context, out_proj, preferred_element_type=F32)]
    all_gather x3 -> x0, blocking collectives: 17.9 us -> none  [combined_all(): pieces = jax.tree.map(lambda part: lax.all_gather(part, axis), value)]
  transfers between devices with their start and end apart: 3 -> 40, of which waited for: 2 -> 19; matrix products, arithmetic and copies ran while one was open for 13% -> 11% of each run, Pallas kernels for 0% -> 17%
where the time goes in v1:
time: 177 us; the launch traced here: 176 us
  waiting for transfers between devices  58.7 us (33%)
  Pallas kernels  45.2 us (26%)
  starting transfers between devices  38.8 us (22%)
  local copies, waits for them, and re-layouts  15.5 us (9%)
  matrix products  10.7 us (6%)
  other arithmetic  6.37 us (4%)
    ppermute x40, waiting for transfers between devices, send(): return lax.ppermute(value, AXES, pairs)  58.7 us
    ppermute x40, starting transfers between devices, send(): return lax.ppermute(value, AXES, pairs)  38.8 us
    pallas_call x4, Pallas kernels, add_latents(): pl.pallas_call(functools.partial(latent_kernel, counts, segments, depth,...  28.8 us
    unnamed x41, local copies, waits for them, and re-layouts  7.7 us
    pallas_call x3, Pallas kernels, assemble(): pl.pallas_call(functools.partial(assemble_kernel, layout), out_shape=shap...  7.49 us
    dot_general x1, matrix products, local(): partial_out = jnp.dot(context, out_proj, preferred_element_type=F32)  4.61 us
    dot_general x1, matrix products, embed(): query_part = jnp.dot(embedded, query_proj, preferred_element_type=F32)  4.6 us
    pallas_call x1, Pallas kernels, attend(): pl.pallas_call(functools.partial(attend_kernel, 1.0 / math.sqrt(HD), span...  3.92 us
  transfers between devices with their start and end apart: 40, of which 19 were waited for; matrix products, arithmetic and copies ran while one was open for 11% of the time, Pallas kernels for 17%

profile of v1, /device:TPU:0, one launch (start us, length us, event | category | flops | bytes accessed | tf_op | source)
XLA Modules:
  0.0 175.9 jit_solution(10976813751723799627)
XLA Ops:
  0.0 3.0 %collective-permute-start.1 = (bf16[512,1024]{1,0:T(8,128)(2,1)}, bf16[512,1024]{1,0:T(8,128)(2,1)}, u32[]{:S(2)}, u32[]{:S(2)}) collective-permute-start(bf16[512,1024]{1,0:T(8,128)(2,1)} %refs_0_.2), channel_id=1, source_target_pairs={{0,8},{1,9},{2,10},{3,11},{4,12},{5,13},{6,14},{7,15},{8,0},{9,1},... | collective-permute-start | bytes 3145736 | tf_op jit(solution)/shard_map/ppermute | solution.py:57
  16.0 4.6 %fusion.11 = f32[16,8192]{1,0:T(8,128)S(1)} fusion(bf16[16,512]{1,0:T(8,128)(2,1)S(1)} %get-tuple-element.88, bf16[512,8192]{1,0:T(8,128)(2,1)} %param.15), kind=kOutput, calls=%fused_computation.79 | convolution fusion | flops 134217728 | bytes 8929280 | tf_op jit(solution)/shard_map/dot_general | solution.py:483
  23.9 5.9 %collective-permute-done.5 = f32[4,16,640]{2,1,0:T(8,128)S(1)} collective-permute-done((f32[4,16,640]{2,1,0:T(8,128)S(1)}, f32[4,16,640]{2,1,0:T(8,128)S(1)}, u32[]{:S(2)}, u32[]{:S(2)}) %collective-permute-start.5) | collective-permute-done | bytes 163872 | tf_op jit(solution)/shard_map/ppermute | solution.py:57
  34.3 2.4 %fusion = (f32[4,208,64]{2,1,0:T(8,128)S(1)}, f32[4,208,64]{2,1,0:T(8,128)}, f32[4,208,64]{2,1,0:T(8,128)}) fusion(f32[64]{0:T(128)S(1)} %negate_power_fusion, f32[4,208]{1,0:T(4,128)S(1)} %add_convert_fusion.2), kind=kLoop, calls=%fused_computation.15 | loop fusion | flops 106496 | bytes 642560 | tf_op jit(solution)/shard_map/neg | solution.py:33
  36.7 2.3 %collective-permute-start.10 = (f32[16,640]{1,0:T(8,128)S(1)}, f32[16,640]{1,0:T(8,128)S(1)}, u32[]{:S(2)}, u32[]{:S(2)}) collective-permute-start(f32[16,640]{1,0:T(8,128)S(1)} %get-tuple-element.94), channel_id=1, source_target_pairs={{0,3},{1,0},{2,1},{3,2},{4,7},{5,4},{6,5},{7,6},{8,11},{9,8},{10,9... | collective-permute-start | bytes 122888 | tf_op jit(solution)/shard_map/ppermute | solution.py:57
  39.0 2.4 %collective-permute-start.9 = (f32[16,640]{1,0:T(8,128)S(1)}, f32[16,640]{1,0:T(8,128)S(1)}, u32[]{:S(2)}, u32[]{:S(2)}) collective-permute-start(f32[16,640]{1,0:T(8,128)S(1)} %get-tuple-element.95), channel_id=1, source_target_pairs={{0,2},{1,3},{2,0},{3,1},{4,6},{5,7},{6,4},{7,5},{8,10},{9,11},{10,... | collective-permute-start | bytes 122888 | tf_op jit(solution)/shard_map/ppermute | solution.py:57
  41.5 11.5 %collective-permute-done.10 = f32[16,640]{1,0:T(8,128)S(1)} collective-permute-done((f32[16,640]{1,0:T(8,128)S(1)}, f32[16,640]{1,0:T(8,128)S(1)}, u32[]{:S(2)}, u32[]{:S(2)}) %collective-permute-start.10) | collective-permute-done | bytes 40992 | tf_op jit(solution)/shard_map/ppermute | solution.py:57
  57.4 2.6 %assemble.4 = bf16[384,1024]{1,0:T(8,128)(2,1)} custom-call(bf16[384,1024]{1,0:T(8,128)(2,1)} %copy-done.1, bf16[384,1024]{1,0:T(8,128)(2,1)} %collective-permute-done.6.refs_1_.refs_0_, bf16[384,1024]{1,0:T(8,128)(2,1)} %copy-done.3), custom_call_target="tpu_custom_call" | custom-call | tf_op jit(solution)/shard_map/assemble/pallas_call | solution.py:182
  62.9 8.1 %latents.4.refs_4_ = f32[768,1024]{1,0:T(8,128)} custom-call(bf16[768,8192]{1,0:T(8,128)(2,1)} %bitcast.86, bf16[512,1024]{1,0:T(8,128)(2,1)} %refs_0_.2, bf16[512,1024]{1,0:T(8,128)(2,1)} %copy-done.7, bf16[384,1024]{1,0:T(8,128)(2,1)S(1)} %copy-done.2, bf16[384,1024]{1,0:T(8,128)(2,1)} %collective-permute-done.14.refs_3_, ...), custom_call_target="tpu_custom_call" | custom-call | flops 4429185024 | bytes 16384000 | tf_op jit(solution)/shard_map/latents/pallas_call | solution.py:144
  71.1 8.9 %collective-permute-done.13.refs_0_ = bf16[384,1024]{1,0:T(8,128)(2,1)S(1)} collective-permute-done((bf16[384,1024]{1,0:T(8,128)(2,1)}, bf16[384,1024]{1,0:T(8,128)(2,1)S(1)}, u32[]{:S(2)}, u32[]{:S(2)}) %collective-permute-start.13) | collective-permute-done | bytes 786464 | tf_op jit(solution)/shard_map/ppermute | solution.py:57
  80.0 3.7 %collective-permute-start.20 = (bf16[16,1600]{1,0:T(8,128)(2,1)S(1)}, bf16[16,1600]{1,0:T(8,128)(2,1)S(1)}, u32[]{:S(2)}, u32[]{:S(2)}) collective-permute-start(bf16[16,1600]{1,0:T(8,128)(2,1)S(1)} %concatenate.35), channel_id=1, source_target_pairs={{0,3},{1,0},{2,1},{3,2},{4,7},{5,4},{6,5},{7,6},{8,11},{9,8},{10,9... | collective-permute-start | bytes 153608 | tf_op jit(solution)/shard_map/ppermute | solution.py:57
  84.4 2.7 %assemble.5 = (bf16[256,1024]{1,0:T(8,128)(2,1)}, bf16[256,1024]{1,0:T(8,128)(2,1)}) custom-call(bf16[384,1024]{1,0:T(8,128)(2,1)} %collective-permute-done.11.refs_0_.refs_1_.refs_2_, bf16[384,1024]{1,0:T(8,128)(2,1)} %collective-permute-done.11.refs_0_.refs_1_.refs_2_, bf16[384,1024]{1,0:T(8,128)(2,1)} %collective-permute-done.12.refs_2_.refs_4_), custom_call_target="tpu_custom_call" | custom-call | tf_op jit(solution)/shard_map/assemble/pallas_call | solution.py:182
  92.2 6.5 %latents.5.refs_6_ = f32[768,1024]{1,0:T(8,128)} custom-call(bf16[768,8192]{1,0:T(8,128)(2,1)} %bitcast.87, bf16[384,1024]{1,0:T(8,128)(2,1)} %collective-permute-done.6.refs_1_.refs_0_, bf16[384,1024]{1,0:T(8,128)(2,1)} %collective-permute-done.18.refs_1_, bf16[384,1024]{1,0:T(8,128)(2,1)} %copy-done.3, bf16[384,1024]{1,0:T(8,128)(2,1)} %collective-permute-done.19.refs_3_, ...), custom_call_target="tpu_custom_call" | custom-call | flops 2415919104 | bytes 11796480 | tf_op jit(solution)/shard_map/latents/pallas_call | solution.py:144
  98.8 2.9 %collective-permute-done.16.refs_0_ = bf16[256,1024]{1,0:T(8,128)(2,1)S(1)} collective-permute-done((bf16[256,1024]{1,0:T(8,128)(2,1)}, bf16[256,1024]{1,0:T(8,128)(2,1)S(1)}, u32[]{:S(2)}, u32[]{:S(2)}) %collective-permute-start.16) | collective-permute-done | bytes 524320 | tf_op jit(solution)/shard_map/ppermute | solution.py:57
  105.2 2.4 %collective-permute-done.28 = bf16[4,16,576]{2,1,0:T(8,128)(2,1)S(1)} collective-permute-done((bf16[4,16,576]{2,1,0:T(8,128)(2,1)S(1)}, bf16[4,16,576]{2,1,0:T(8,128)(2,1)S(1)}, u32[]{:S(2)}, u32[]{:S(2)}) %collective-permute-start.28) | collective-permute-done | bytes 73760 | tf_op jit(solution)/shard_map/ppermute | solution.py:57
  111.2 8.3 %collective-permute-done.30.refs_4_ = bf16[256,1024]{1,0:T(8,128)(2,1)} collective-permute-done((bf16[256,1024]{1,0:T(8,128)(2,1)}, bf16[256,1024]{1,0:T(8,128)(2,1)}, u32[]{:S(2)}, u32[]{:S(2)}) %collective-permute-start.30) | collective-permute-done | bytes 524320 | tf_op jit(solution)/shard_map/ppermute | solution.py:57
  120.2 7.7 %latents.6.refs_6_ = f32[768,1024]{1,0:T(8,128)} custom-call(bf16[768,8192]{1,0:T(8,128)(2,1)} %bitcast.88, bf16[384,1024]{1,0:T(8,128)(2,1)S(1)} %collective-permute-done.13.refs_0_, bf16[384,1024]{1,0:T(8,128)(2,1)} %collective-permute-done.25.refs_1_, bf16[384,1024]{1,0:T(8,128)(2,1)} %collective-permute-done.11.refs_0_.refs_1_.refs_2_, ...), custom_call_target="tpu_custom_call" | custom-call | flops 3623878656 | bytes 14548992 | tf_op jit(solution)/shard_map/latents/pallas_call | solution.py:144
  127.9 6.4 %latents.7.lat_ref = f32[768,1024]{1,0:T(8,128)} custom-call(bf16[768,8192]{1,0:T(8,128)(2,1)} %bitcast.89, bf16[256,1024]{1,0:T(8,128)(2,1)S(1)} %collective-permute-done.16.refs_0_, bf16[256,1024]{1,0:T(8,128)(2,1)} %collective-permute-done.23.refs_1_, bf16[256,1024]{1,0:T(8,128)(2,1)} %collective-permute-done.17.refs_2_, ...), custom_call_target="tpu_custom_call" | custom-call | flops 2415919104 | bytes 11796480 | tf_op jit(solution)/shard_map/latents/pallas_call | solution.py:144
  136.2 3.9 %attend.1 = bf16[4,144,128]{2,1,0:T(8,128)(2,1)S(1)} custom-call(f32[768,1024]{1,0:T(8,128)S(1)} %copy-done, bf16[4,16,1024]{2,1,0:T(8,128)(2,1)S(1)} %pad.4.fresh_ref, f32[4,208,128]{2,1,0:T(8,128)S(1)} %get-tuple-element.112.cos_ref, f32[4,208,128]{2,1,0:T(8,128)S(1)} %get-tuple-element.113.sin_ref, f32[4,208,128]{2,1,0:T(8,128)S(1)} %add_convert_fusion.live_ref, ...), custom_call_target="tpu_custom_call" | custom-call | tf_op jit(solution)/shard_map/attend/pallas_call | solution.py:249
  140.8 2.8 %collective-permute-start.32 = (bf16[144,128]{1,0:T(8,128)(2,1)S(1)}, bf16[144,128]{1,0:T(8,128)(2,1)S(1)}, u32[]{:S(2)}, u32[]{:S(2)}) collective-permute-start(bf16[144,128]{1,0:T(8,128)(2,1)S(1)} %get-tuple-element.98), channel_id=1, source_target_pairs={{0,1},{1,2},{2,3},{3,0},{4,5},{5,6},{6,7},{7,4},{8,9},{9,10},{10,1... | collective-permute-start | bytes 110600 | tf_op jit(solution)/shard_map/ppermute | solution.py:57
  151.8 3.7 %collective-permute-done.35.refs_1_ = f32[136,128]{1,0:T(8,128)S(1)} collective-permute-done((f32[136,128]{1,0:T(8,128)}, f32[136,128]{1,0:T(8,128)S(1)}, u32[]{:S(2)}, u32[]{:S(2)}) %collective-permute-start.35) | collective-permute-done | bytes 69664 | tf_op jit(solution)/shard_map/ppermute | solution.py:57
  161.7 4.6 %fusion.10 = (bf16[16,2048]{1,0:T(8,128)(2,1)S(1)}, f32[16,2048]{1,0:T(8,128)S(1)}) fusion(bf16[16,2048]{1,0:T(8,128)(2,1)} %context.1, bf16[2048,2048]{1,0:T(8,128)(2,1)} %param.19), kind=kOutput, calls=%fused_computation.78 | convolution fusion | flops 134250496 | bytes 8650752 | tf_op jit(solution)/shard_map/dot_general | solution.py:574
  166.9 2.8 %collective-permute-start.38 = (bf16[16,2048]{1,0:T(8,128)(2,1)S(1)}, bf16[16,2048]{1,0:T(8,128)(2,1)S(1)}, u32[]{:S(2)}, u32[]{:S(2)}) collective-permute-start(bf16[16,2048]{1,0:T(8,128)(2,1)S(1)} %get-tuple-element.108), channel_id=1, source_target_pairs={{0,2},{1,3},{2,0},{3,1},{4,6},{5,7},{6,4},{7,5},{8,10},{9,11},{10,... | collective-permute-start | bytes 196616 | tf_op jit(solution)/shard_map/ppermute | solution.py:57
  170.8 2.4 %collective-permute-done.37 = bf16[16,2048]{1,0:T(8,128)(2,1)S(1)} collective-permute-done((bf16[16,2048]{1,0:T(8,128)(2,1)S(1)}, bf16[16,2048]{1,0:T(8,128)(2,1)S(1)}, u32[]{:S(2)}, u32[]{:S(2)}) %collective-permute-start.37) | collective-permute-done | bytes 65568 | tf_op jit(solution)/shard_map/ppermute | solution.py:57
  (186 shorter events, 62.7 us)
Async XLA Ops:
  0.0 29.9 %collective-permute-start.1 = (bf16[512,1024]{1,0:T(8,128)(2,1)}, bf16[512,1024]{1,0:T(8,128)(2,1)}, u32[]{:S(2)}, u32[]{:S(2)}) collective-permute-start(bf16[512,1024]{1,0:T(8,128)(2,1)} %refs_0_.2), channel_id=1, source_target_pairs={{0,8},{1,9},{2,10},{3,11},{4,12},{5,13},{6,14},{7,15},{8,0},{9,1},... | collective-permute-start | bytes 3145736 | tf_op jit(solution)/shard_map/ppermute | solution.py:57
  3.0 26.9 %collective-permute-start.2 = (bf16[512,1024]{1,0:T(8,128)(2,1)}, bf16[512,1024]{1,0:T(8,128)(2,1)S(1)}, u32[]{:S(2)}, u32[]{:S(2)}) collective-permute-start(bf16[512,1024]{1,0:T(8,128)(2,1)} %refs_0_.2), channel_id=1, source_target_pairs={{0,4},{1,5},{2,6},{3,7},{4,0},{5,1},{6,2},{7,3},{8,12},{9,13},{10,... | collective-permute-start | bytes 3145736 | tf_op jit(solution)/shard_map/ppermute | solution.py:57
  5.2 24.7 %collective-permute-start = (bf16[384,1024]{1,0:T(8,128)(2,1)}, bf16[384,1024]{1,0:T(8,128)(2,1)S(1)}, u32[]{:S(2)}, u32[]{:S(2)}) collective-permute-start(bf16[384,1024]{1,0:T(8,128)(2,1)} %assemble.3), channel_id=1, source_target_pairs={{0,1},{1,2},{2,3},{3,0},{4,5},{5,6},{6,7},{7,4},{8,9},{9,10},{10,1... | collective-permute-start | bytes 2359304 | tf_op jit(solution)/shard_map/ppermute | solution.py:57
  30.9 24.4 %collective-permute-start.6 = (bf16[384,1024]{1,0:T(8,128)(2,1)S(1)}, bf16[384,1024]{1,0:T(8,128)(2,1)}, u32[]{:S(2)}, u32[]{:S(2)}) collective-permute-start(bf16[384,1024]{1,0:T(8,128)(2,1)S(1)} %collective-permute-done.refs_0_.refs_2_), channel_id=1, source_target_pairs={{0,1},{1,2},{2,3},{3,0},{4,5},{5,6},{6,7},{7,4},{8,9},{9,10},{10,1... | collective-permute-start | bytes 2359304 | tf_op jit(solution)/shard_map/ppermute | solution.py:57
  32.7 22.6 %collective-permute-start.7 = (bf16[384,1024]{1,0:T(8,128)(2,1)S(1)}, bf16[384,1024]{1,0:T(8,128)(2,1)S(1)}, u32[]{:S(2)}, u32[]{:S(2)}) collective-permute-start(bf16[384,1024]{1,0:T(8,128)(2,1)S(1)} %collective-permute-done.refs_0_.refs_2_), channel_id=1, source_target_pairs={{0,8},{1,9},{2,10},{3,11},{4,12},{5,13},{6,14},{7,15},{8,0},{9,1},... | collective-permute-start | bytes 2359304 | tf_op jit(solution)/shard_map/ppermute | solution.py:57
  36.7 16.3 %collective-permute-start.10 = (f32[16,640]{1,0:T(8,128)S(1)}, f32[16,640]{1,0:T(8,128)S(1)}, u32[]{:S(2)}, u32[]{:S(2)}) collective-permute-start(f32[16,640]{1,0:T(8,128)S(1)} %get-tuple-element.94), channel_id=1, source_target_pairs={{0,3},{1,0},{2,1},{3,2},{4,7},{5,4},{6,5},{7,6},{8,11},{9,8},{10,9... | collective-permute-start | bytes 122888 | tf_op jit(solution)/shard_map/ppermute | solution.py:57
  39.0 15.1 %collective-permute-start.8 = (f32[16,640]{1,0:T(8,128)S(1)}, f32[16,640]{1,0:T(8,128)S(1)}, u32[]{:S(2)}, u32[]{:S(2)}) collective-permute-start(f32[16,640]{1,0:T(8,128)S(1)} %get-tuple-element.93), channel_id=1, source_target_pairs={{0,1},{1,2},{2,3},{3,0},{4,5},{5,6},{6,7},{7,4},{8,9},{9,10},{10,1... | collective-permute-start | bytes 122888 | tf_op jit(solution)/shard_map/ppermute | solution.py:57
  39.0 16.3 %collective-permute-start.9 = (f32[16,640]{1,0:T(8,128)S(1)}, f32[16,640]{1,0:T(8,128)S(1)}, u32[]{:S(2)}, u32[]{:S(2)}) collective-permute-start(f32[16,640]{1,0:T(8,128)S(1)} %get-tuple-element.95), channel_id=1, source_target_pairs={{0,2},{1,3},{2,0},{3,1},{4,6},{5,7},{6,4},{7,5},{8,10},{9,11},{10,... | collective-permute-start | bytes 122888 | tf_op jit(solution)/shard_map/ppermute | solution.py:57
  55.6 24.4 %collective-permute-start.11 = (bf16[384,1024]{1,0:T(8,128)(2,1)}, bf16[384,1024]{1,0:T(8,128)(2,1)}, u32[]{:S(2)}, u32[]{:S(2)}) collective-permute-start(bf16[384,1024]{1,0:T(8,128)(2,1)} %collective-permute-done.6.refs_1_.refs_0_), channel_id=1, source_target_pairs={{0,1},{1,2},{2,3},{3,0},{4,5},{5,6},{6,7},{7,4},{8,9},{9,10},{10,1... | collective-permute-start | bytes 2359304 | tf_op jit(solution)/shard_map/ppermute | solution.py:57
  55.6 24.3 %collective-permute-start.12 = (bf16[384,1024]{1,0:T(8,128)(2,1)}, bf16[384,1024]{1,0:T(8,128)(2,1)}, u32[]{:S(2)}, u32[]{:S(2)}) collective-permute-start(bf16[384,1024]{1,0:T(8,128)(2,1)} %collective-permute-done.6.refs_1_.refs_0_), channel_id=1, source_target_pairs={{0,8},{1,9},{2,10},{3,11},{4,12},{5,13},{6,14},{7,15},{8,0},{9,1},... | collective-permute-start | bytes 2359304 | tf_op jit(solution)/shard_map/ppermute | solution.py:57
  60.0 20.0 %collective-permute-start.13 = (bf16[384,1024]{1,0:T(8,128)(2,1)}, bf16[384,1024]{1,0:T(8,128)(2,1)S(1)}, u32[]{:S(2)}, u32[]{:S(2)}) collective-permute-start(bf16[384,1024]{1,0:T(8,128)(2,1)} %assemble.4), channel_id=1, source_target_pairs={{0,16},{1,17},{2,18},{3,19},{4,20},{5,21},{6,22},{7,23},{8,24},{9,... | collective-permute-start | bytes 2359304 | tf_op jit(solution)/shard_map/ppermute | solution.py:57
  80.0 7.6 %collective-permute-start.20 = (bf16[16,1600]{1,0:T(8,128)(2,1)S(1)}, bf16[16,1600]{1,0:T(8,128)(2,1)S(1)}, u32[]{:S(2)}, u32[]{:S(2)}) collective-permute-start(bf16[16,1600]{1,0:T(8,128)(2,1)S(1)} %concatenate.35), channel_id=1, source_target_pairs={{0,3},{1,0},{2,1},{3,2},{4,7},{5,4},{6,5},{7,6},{8,11},{9,8},{10,9... | collective-permute-start | bytes 153608 | tf_op jit(solution)/shard_map/ppermute | solution.py:57
  83.7 6.6 %collective-permute-start.22 = (bf16[16,1600]{1,0:T(8,128)(2,1)S(1)}, bf16[16,1600]{1,0:T(8,128)(2,1)S(1)}, u32[]{:S(2)}, u32[]{:S(2)}) collective-permute-start(bf16[16,1600]{1,0:T(8,128)(2,1)S(1)} %concatenate.35), channel_id=1, source_target_pairs={{0,1},{1,2},{2,3},{3,0},{4,5},{5,6},{6,7},{7,4},{8,9},{9,10},{10,1... | collective-permute-start | bytes 153608 | tf_op jit(solution)/shard_map/ppermute | solution.py:57
  87.6 14.1 %collective-permute-start.16 = (bf16[256,1024]{1,0:T(8,128)(2,1)}, bf16[256,1024]{1,0:T(8,128)(2,1)S(1)}, u32[]{:S(2)}, u32[]{:S(2)}) collective-permute-start(bf16[256,1024]{1,0:T(8,128)(2,1)} %get-tuple-element.63), channel_id=1, source_target_pairs={{0,16},{1,17},{2,18},{3,19},{4,20},{5,21},{6,22},{7,23},{8,24},{9,... | collective-permute-start | bytes 1572872 | tf_op jit(solution)/shard_map/ppermute | solution.py:57
  89.1 14.0 %collective-permute-start.17 = (bf16[256,1024]{1,0:T(8,128)(2,1)}, bf16[256,1024]{1,0:T(8,128)(2,1)}, u32[]{:S(2)}, u32[]{:S(2)}) collective-permute-start(bf16[256,1024]{1,0:T(8,128)(2,1)} %get-tuple-element.64), channel_id=1, source_target_pairs={{0,8},{1,9},{2,10},{3,11},{4,12},{5,13},{6,14},{7,15},{8,0},{9,1},... | collective-permute-start | bytes 1572872 | tf_op jit(solution)/shard_map/ppermute | solution.py:57
  104.3 15.2 %collective-permute-start.25 = (bf16[384,1024]{1,0:T(8,128)(2,1)S(1)}, bf16[384,1024]{1,0:T(8,128)(2,1)}, u32[]{:S(2)}, u32[]{:S(2)}) collective-permute-start(bf16[384,1024]{1,0:T(8,128)(2,1)S(1)} %collective-permute-done.13.refs_0_), channel_id=1, source_target_pairs={{0,4},{1,5},{2,6},{3,7},{4,0},{5,1},{6,2},{7,3},{8,12},{9,13},{10,... | collective-permute-start | bytes 2359304 | tf_op jit(solution)/shard_map/ppermute | solution.py:57
  104.3 15.8 %collective-permute-start.26 = (bf16[384,1024]{1,0:T(8,128)(2,1)}, bf16[384,1024]{1,0:T(8,128)(2,1)}, u32[]{:S(2)}, u32[]{:S(2)}) collective-permute-start(bf16[384,1024]{1,0:T(8,128)(2,1)} %collective-permute-done.11.refs_0_.refs_1_.refs_2_), channel_id=1, source_target_pairs={{0,4},{1,5},{2,6},{3,7},{4,0},{5,1},{6,2},{7,3},{8,12},{9,13},{10,... | collective-permute-start | bytes 2359304 | tf_op jit(solution)/shard_map/ppermute | solution.py:57
  104.8 15.4 %collective-permute-start.27 = (bf16[384,1024]{1,0:T(8,128)(2,1)}, bf16[384,1024]{1,0:T(8,128)(2,1)}, u32[]{:S(2)}, u32[]{:S(2)}) collective-permute-start(bf16[384,1024]{1,0:T(8,128)(2,1)} %collective-permute-done.12.refs_2_.refs_4_), channel_id=1, source_target_pairs={{0,4},{1,5},{2,6},{3,7},{4,0},{5,1},{6,2},{7,3},{8,12},{9,13},{10,... | collective-permute-start | bytes 2359304 | tf_op jit(solution)/shard_map/ppermute | solution.py:57
  104.9 14.6 %collective-permute-start.30 = (bf16[256,1024]{1,0:T(8,128)(2,1)}, bf16[256,1024]{1,0:T(8,128)(2,1)}, u32[]{:S(2)}, u32[]{:S(2)}) collective-permute-start(bf16[256,1024]{1,0:T(8,128)(2,1)} %collective-permute-done.17.refs_2_), channel_id=1, source_target_pairs={{0,16},{1,17},{2,18},{3,19},{4,20},{5,21},{6,22},{7,23},{8,24},{9,... | collective-permute-start | bytes 1572872 | tf_op jit(solution)/shard_map/ppermute | solution.py:57
  109.1 18.8 %collective-permute-start.24 = (bf16[256,1024]{1,0:T(8,128)(2,1)}, bf16[256,1024]{1,0:T(8,128)(2,1)}, u32[]{:S(2)}, u32[]{:S(2)}) collective-permute-start(bf16[256,1024]{1,0:T(8,128)(2,1)} %collective-permute-done.17.refs_2_), channel_id=1, source_target_pairs={{0,4},{1,5},{2,6},{3,7},{4,0},{5,1},{6,2},{7,3},{8,12},{9,13},{10,... | collective-permute-start | bytes 1572872 | tf_op jit(solution)/shard_map/ppermute | solution.py:57
  119.5 8.5 %collective-permute-start.23 = (bf16[256,1024]{1,0:T(8,128)(2,1)S(1)}, bf16[256,1024]{1,0:T(8,128)(2,1)}, u32[]{:S(2)}, u32[]{:S(2)}) collective-permute-start(bf16[256,1024]{1,0:T(8,128)(2,1)S(1)} %collective-permute-done.16.refs_0_), channel_id=1, source_target_pairs={{0,4},{1,5},{2,6},{3,7},{4,0},{5,1},{6,2},{7,3},{8,12},{9,13},{10,... | collective-permute-start | bytes 1572872 | tf_op jit(solution)/shard_map/ppermute | solution.py:57
  119.5 8.5 %collective-permute-start.31 = (bf16[256,1024]{1,0:T(8,128)(2,1)}, bf16[256,1024]{1,0:T(8,128)(2,1)}, u32[]{:S(2)}, u32[]{:S(2)}) collective-permute-start(bf16[256,1024]{1,0:T(8,128)(2,1)} %collective-permute-done.30.refs_4_), channel_id=1, source_target_pairs={{0,4},{1,5},{2,6},{3,7},{4,0},{5,1},{6,2},{7,3},{8,12},{9,13},{10,... | collective-permute-start | bytes 1572872 | tf_op jit(solution)/shard_map/ppermute | solution.py:57
  166.3 6.9 %collective-permute-start.37 = (bf16[16,2048]{1,0:T(8,128)(2,1)S(1)}, bf16[16,2048]{1,0:T(8,128)(2,1)S(1)}, u32[]{:S(2)}, u32[]{:S(2)}) collective-permute-start(bf16[16,2048]{1,0:T(8,128)(2,1)S(1)} %get-tuple-element.108), channel_id=1, source_target_pairs={{0,1},{1,2},{2,3},{3,0},{4,5},{5,6},{6,7},{7,4},{8,9},{9,10},{10,1... | collective-permute-start | bytes 196616 | tf_op jit(solution)/shard_map/ppermute | solution.py:57
  166.9 8.2 %collective-permute-start.38 = (bf16[16,2048]{1,0:T(8,128)(2,1)S(1)}, bf16[16,2048]{1,0:T(8,128)(2,1)S(1)}, u32[]{:S(2)}, u32[]{:S(2)}) collective-permute-start(bf16[16,2048]{1,0:T(8,128)(2,1)S(1)} %get-tuple-element.108), channel_id=1, source_target_pairs={{0,2},{1,3},{2,0},{3,1},{4,6},{5,7},{6,4},{7,5},{8,10},{9,11},{10,... | collective-permute-start | bytes 196616 | tf_op jit(solution)/shard_map/ppermute | solution.py:57
  (32 other events, 211.6 us)

commit v2 on v1

v2 whole, which is shorter than its diff:
```python
import functools
import math

import jax
import jax.numpy as jnp
from jax import lax
from jax.experimental import pallas as pl
from jax.experimental.pallas import tpu as pltpu
from jax.sharding import PartitionSpec as P

D = 8192
HQ = 64
KVH = 8
HD = 128
RANK = 64
PAGE = 16
FRESH = 16

AXES = ("side", "seq", "head")
rope_base = 500000.0
masked_score = -1e30
BF = jnp.bfloat16
F32 = jnp.float32


def sincos(positions):
    half = HD // 2
    frequency = 1.0 / rope_base ** (jnp.arange(half, dtype=F32) * 2.0 / HD)
    angles = positions.astype(F32)[..., None] * frequency
    cosine, sines = jnp.cos(angles), jnp.sin(angles)
    return (
        jnp.concatenate([cosine, cosine], axis=-1),
        jnp.concatenate([-sines, sines], axis=-1),
    )


class Grid:
    def __init__(self):
        self.sides, self.seqs, self.heads = (lax.axis_size(a) for a in AXES)
        self.ys = self.seqs // 2
        self.side, seq, self.z = (lax.axis_index(a) for a in AXES)
        self.y, self.c = lax.div(seq, 2), lax.rem(seq, 2)

    def send(self, value, side=0, y=0, core=0, head=0):
        pairs = []
        for a in range(self.sides):
            for b in range(self.ys):
                for c in range(2):
                    for d in range(self.heads):
                        to = (
                            (a + side) % self.sides,
                            (b + y) % self.ys,
                            (c + core) % 2,
                            (d + head) % self.heads,
                        )
                        pairs.append((self.flat(a, b, c, d), self.flat(*to)))
        return lax.ppermute(value, AXES, pairs)

    def place(self, dy, dc, dz):
        seq = lax.rem(self.y + self.ys - dy, self.ys) * 2 + (1 - self.c if dc else self.c)
        return seq * self.heads + lax.rem(self.z + self.heads - dz, self.heads)

    def flat(self, a, b, c, d):
        return (a * self.seqs + b * 2 + c) * self.heads + d


def accumulate(
    counts, segments, depth, hidden_ref, pieces, before_ref, hidden_buf, piece_buf, total, sems, store=None
):
    grid = Grid()
    rows = hidden_ref.shape[0]
    if before_ref is not None:
        load = pltpu.make_async_copy(before_ref, total, sems.at[len(segments) + len(pieces)])
    waits = []
    at = 0
    for i, count in enumerate(counts):
        copies = [
            pltpu.make_async_copy(
                pieces[i].at[pl.ds(0, count), :],
                piece_buf.at[pl.ds(at, count), :],
                sems.at[len(segments) + i],
            )
        ]
        inside = 0
        for k, (owner, extent, dy, dc, dz, base, step) in enumerate(segments):
            if owner == i:
                source = grid.place(dy, dc, dz) * depth + base + step * grid.side
                source = pl.multiple_of(source, 128)
                copies.append(
                    pltpu.make_async_copy(
                        hidden_ref.at[:, pl.ds(source, extent)],
                        hidden_buf.at[:, pl.ds(at + inside, extent)],
                        sems.at[k],
                    )
                )
                inside += extent
        for copy in copies:
            copy.start()
        if before_ref is not None and i == 1:
            load.start()
        waits.append((copies, at, count))
        at += count
    pairs = [waits[i : i + 2] for i in range(0, len(waits), 2)]
    for k, pair in enumerate(pairs):
        for copies, _, _ in pair:
            for copy in copies:
                copy.wait()
        first = pair[0][1]
        span = sum(count for _, _, count in pair)
        last = k == len(pairs) - 1
        tile = rows // 4 if last and store else rows
        for m in range(rows // tile):
            part = slice(m * tile, (m + 1) * tile)
            term = jnp.dot(
                hidden_buf[part, first : first + span],
                piece_buf[first : first + span, :],
                preferred_element_type=F32,
            )
            if k == 0 and m == 0 and before_ref is not None:
                load.wait()
            total[part, :] = total[part, :] + term if k or before_ref is not None else term
            if last and store:
                store(m, tile)


def latent_kernel(counts, segments, depth, has_total, hidden_ref, *refs):
    pieces, refs = refs[: len(counts)], refs[len(counts) :]
    before_ref = None
    if has_total:
        before_ref, refs = refs[0], refs[1:]
    out_ref, hidden_buf, piece_buf, total, sems, out_sems = refs
    stores = []

    def store(m, tile):
        rows = pl.ds(m * tile, tile)
        copy = pltpu.make_async_copy(total.at[rows, :], out_ref.at[rows, :], out_sems.at[m])
        copy.start()
        stores.append(copy)

    accumulate(
        counts, segments, depth, hidden_ref, pieces, before_ref, hidden_buf, piece_buf, total, sems, store
    )
    for copy in stores:
        copy.wait()


def add_latents(hidden, depth, batch, total=None):
    pieces = [piece for piece, _ in batch]
    counts = [sum(part[0] for part in parts) for _, parts in batch]
    segments = [(i, *part) for i, (_, parts) in enumerate(batch) for part in parts]
    deep, columns = sum(counts), pieces[0].shape[1]
    rows = hidden.shape[0]
    operands = [hidden, *pieces]
    if total is not None:
        operands.append(total)
    return pl.pallas_call(
        functools.partial(latent_kernel, counts, segments, depth, total is not None),
        out_shape=jax.ShapeDtypeStruct((rows, columns), F32),
        in_specs=[pl.BlockSpec(memory_space=pl.ANY)] * len(operands),
        out_specs=pl.BlockSpec(memory_space=pl.ANY),
        scratch_shapes=[
            pltpu.VMEM((rows, deep), BF),
            pltpu.VMEM((deep, columns), BF),
            pltpu.VMEM((rows, columns), F32),
            pltpu.SemaphoreType.DMA((len(segments) + len(pieces) + 1,)),
            pltpu.SemaphoreType.DMA((4,)),
        ],
        compiler_params=pltpu.CompilerParams(vmem_limit_bytes=28 * 1024 * 1024),
        cost_estimate=pl.CostEstimate(flops=1, bytes_accessed=1, transcendentals=0),
        name="latents",
    )(*operands)


def first_piece_kernel(rows, own_ref, up_ref, out_ref, sems):
    side = lax.axis_index("side")
    groups = up_ref.shape[0]
    each = RANK // FRESH
    start = pl.multiple_of(rows * side, 16)
    copies = [
        pltpu.make_async_copy(
            own_ref.at[pl.ds(start, 3 * rows), :], out_ref.at[pl.ds(0, 3 * rows), :], sems.at[0]
        )
    ]
    for k in range(groups * each):
        copies.append(
            pltpu.make_async_copy(
                up_ref.at[k // each, pl.ds(k % each * FRESH, FRESH), :],
                out_ref.at[pl.ds(3 * rows, FRESH), pl.ds(k * HD, HD)],
                sems.at[1 + k],
            )
        )
    for copy in copies:
        copy.start()
    for copy in copies:
        copy.wait()


def first_piece(own, key_up, rows):
    count = key_up.shape[0] * RANK // FRESH
    return pl.pallas_call(
        functools.partial(first_piece_kernel, rows),
        out_shape=jax.ShapeDtypeStruct((3 * rows + FRESH, own.shape[1]), own.dtype),
        in_specs=[pl.BlockSpec(memory_space=pl.ANY)] * 2,
        out_specs=pl.BlockSpec(memory_space=pltpu.VMEM),
        scratch_shapes=[pltpu.SemaphoreType.DMA((1 + count,))],
        compiler_params=pltpu.CompilerParams(vmem_limit_bytes=8 * 1024 * 1024),
        cost_estimate=pl.CostEstimate(flops=1, bytes_accessed=1, transcendentals=0),
        name="first_piece",
    )(own, key_up)


def assemble_kernel(layout, *refs):
    ins, outs, sems = refs[: len(layout)], refs[len(layout) : -1], refs[-1]
    side = lax.axis_index("side")
    copies = []
    for k, (o, at, count, base, step) in enumerate(layout):
        start = pl.multiple_of(base + step * side, 16)
        copies.append(
            pltpu.make_async_copy(
                ins[k].at[pl.ds(start, count), :], outs[o].at[pl.ds(at, count), :], sems.at[k]
            )
        )
        copies[-1].start()
    for copy in copies:
        copy.wait()


def assemble(*arrays):
    layout, sources, shapes = [], [], []
    for o, parts in enumerate(arrays):
        at = 0
        for source, count, base, step in parts:
            layout.append((o, at, count, base, step))
            sources.append(source)
            at += count
        shapes.append(jax.ShapeDtypeStruct((at, source.shape[1]), source.dtype))
    return pl.pallas_call(
        functools.partial(assemble_kernel, layout),
        out_shape=shapes,
        in_specs=[pl.BlockSpec(memory_space=pl.ANY)] * len(sources),
        out_specs=[pl.BlockSpec(memory_space=pltpu.VMEM)] * len(shapes),
        scratch_shapes=[pltpu.SemaphoreType.DMA((len(layout),))],
        compiler_params=pltpu.CompilerParams(vmem_limit_bytes=8 * 1024 * 1024),
        cost_estimate=pl.CostEstimate(flops=1, bytes_accessed=1, transcendentals=0),
        name="assemble",
    )(*sources)


def in_three(value):
    high = value.astype(BF).astype(F32)
    middle = (value - high).astype(BF).astype(F32)
    return high, middle, value - high - middle


def pack_up(key_up):
    groups = key_up.shape[0]
    parts = key_up.reshape(groups, RANK // FRESH, FRESH, HD).transpose(2, 0, 1, 3)
    return parts.reshape(FRESH, -1)


def unpack_up(up_ref, g):
    each = up_ref.shape[2] // (RANK // FRESH * HD)
    at = g % each * (RANK // FRESH)
    parts = [up_ref[g // each, :, (at + i) * HD : (at + i + 1) * HD] for i in range(RANK // FRESH)]
    return jnp.concatenate(parts, axis=0)


def attend_part(scale, span, lat_ref, fresh_ref, cos_ref, sin_ref, live_ref, query_ref, up_ref, out_ref):
    requests, groups, lanes, _ = query_ref.shape
    blocks = out_ref.shape[0]
    each = groups // blocks
    peaks, totals, summed = [], [], []
    ups = [unpack_up(up_ref, g) for g in range(groups)]
    for r in range(requests):
        latent = jnp.concatenate(
            [
                lat_ref[r * span : (r + 1) * span, :].astype(BF),
                jnp.concatenate([fresh_ref[r, p] for p in range(fresh_ref.shape[1])], axis=1),
            ],
            axis=0,
        )
        cosine, sines = cos_ref[r], sin_ref[r]
        columns, values = [], []
        for g in range(groups):
            at = g * 2 * RANK
            key = jnp.dot(latent[:, at : at + RANK], ups[g], preferred_element_type=F32)
            key = (key * cosine + pltpu.roll(key, HD // 2, 1) * sines).astype(BF)
            columns.append(
                lax.dot_general(
                    key, query_ref[r, g], (((1,), (1,)), ((), ())), preferred_element_type=F32
                )
            )
            values.append(latent[:, at + RANK : at + 2 * RANK])
        scores = jnp.concatenate(columns, axis=1) * scale
        live = live_ref[r] > 0
        live = jnp.concatenate([live] * (scores.shape[1] // live.shape[1]), axis=1)
        scores = jnp.where(live, scores, masked_score)
        peak = jnp.max(scores, axis=0, keepdims=True)
        weights = jnp.where(live, jnp.exp(scores - peak), 0.0)
        peaks.append(peak)
        totals.append(jnp.sum(weights, axis=0, keepdims=True))
        summed.append(
            lax.dot_general(
                jnp.concatenate(values, axis=1),
                weights.astype(BF),
                (((0,), (0,)), ((), ())),
                preferred_element_type=F32,
            )
        )
    for b in range(blocks):
        stats = []
        for i in range(each):
            g = b * each + i
            cut = slice(g * lanes, (g + 1) * lanes)
            out_ref[b, i * RANK : (i + 1) * RANK, :] = jnp.concatenate(
                [s[g * RANK : (g + 1) * RANK, cut] for s in summed], axis=1
            ).astype(BF)
            stats += in_three(jnp.concatenate([p[:, cut] for p in peaks], axis=1))
            stats += in_three(jnp.concatenate([t[:, cut] for t in totals], axis=1))
        stats += [jnp.zeros_like(stats[0])] * (16 - len(stats))
        out_ref[b, each * RANK :, :] = jnp.concatenate(stats, axis=0).astype(BF)


def finish_kernel(counts, segments, depth, scale, span, up_row, hidden_ref, *refs):
    pieces, refs = refs[: len(counts)], refs[len(counts) :]
    before_ref, refs = refs[0], refs[1:]
    heads = lax.axis_size("head")
    tables, ups, weight_ref, refs = refs[:5], refs[5 : 5 + heads], refs[5 + heads], refs[6 + heads :]
    out_ref, weight_out, hidden_buf, piece_buf, total = refs[:5]
    held, up_buf, table_sems, weight_sem = refs[5:10], refs[11], refs[12], refs[13]
    sems = refs[10]
    loads = [
        pltpu.make_async_copy(table, buf, table_sems.at[i])
        for i, (table, buf) in enumerate(zip(tables, held))
    ]
    z = lax.axis_index("head")
    for k, up in enumerate(ups):
        place = lax.rem(z + heads - k, heads)
        loads.append(
            pltpu.make_async_copy(
                up.at[pl.ds(up_row, FRESH), :], up_buf.at[place], table_sems.at[len(tables) + k]
            )
        )
    for load in loads:
        load.start()
    accumulate(counts, segments, depth, hidden_ref, pieces, before_ref, hidden_buf, piece_buf, total, sems)
    for load in loads:
        load.wait()
    bring = pltpu.make_async_copy(weight_ref, weight_out, weight_sem)
    bring.start()
    attend_part(scale, span, total, *held, up_buf, out_ref)
    bring.wait()


def finish(span, hidden, depth, batch, total, fresh, cosine, sines, live, queries, ups, up_row, weight, blocks):
    pieces = [piece for piece, _ in batch]
    counts = [sum(part[0] for part in parts) for _, parts in batch]
    segments = [(i, *part) for i, (_, parts) in enumerate(batch) for part in parts]
    deep, columns = sum(counts), pieces[0].shape[1]
    rows = hidden.shape[0]
    requests, groups, lanes, _ = queries.shape
    tables = (fresh, cosine, sines, live, queries)
    far = [pltpu.with_memory_space_constraint(t, pltpu.HBM) for t in (cosine, sines, live)]
    tables = (fresh, *far, queries)
    operands = [hidden, *pieces, total, *tables, *ups, weight]
    state_rows = groups // blocks * RANK + 16
    return pl.pallas_call(
        functools.partial(finish_kernel, counts, segments, depth, 1.0 / math.sqrt(HD), span, up_row),
        out_shape=(
            jax.ShapeDtypeStruct((blocks, state_rows, requests * lanes), BF),
            pltpu.VMEM(weight.shape, weight.dtype),
        ),
        in_specs=[pl.BlockSpec(memory_space=pl.ANY)] * len(operands),
        out_specs=(pl.BlockSpec(memory_space=pltpu.VMEM), pl.BlockSpec(memory_space=pl.ANY)),
        scratch_shapes=[
            pltpu.VMEM((rows, deep), BF),
            pltpu.VMEM((deep, columns), BF),
            pltpu.VMEM((rows, columns), F32),
        ]
        + [pltpu.VMEM(table.shape, table.dtype) for table in tables]
        + [
            pltpu.SemaphoreType.DMA((len(segments) + len(pieces) + 1,)),
            pltpu.VMEM((len(ups), FRESH, ups[0].shape[1]), BF),
            pltpu.SemaphoreType.DMA((len(tables) + len(ups),)),
            pltpu.SemaphoreType.DMA,
        ],
        compiler_params=pltpu.CompilerParams(vmem_limit_bytes=28 * 1024 * 1024),
        cost_estimate=pl.CostEstimate(flops=1, bytes_accessed=1, transcendentals=0),
        name="finish",
    )(*operands)


def join(states):
    peak = functools.reduce(jnp.maximum, [p for p, _, _ in states])
    total, summed = 0.0, 0.0
    for p, t, s in states:
        weight = jnp.exp(p - peak)
        total = total + t * weight
        summed = summed + s * weight
    return peak, total, summed


def pack(states, out_ref):
    each = len(states)
    stats = []
    for i, (peak, total, summed) in enumerate(states):
        out_ref[i * RANK : (i + 1) * RANK, :] = summed.astype(BF)
        stats += [*in_three(peak), *in_three(total)]
    stats += [jnp.zeros_like(stats[0])] * (16 - len(stats))
    out_ref[each * RANK :, :] = jnp.concatenate(stats, axis=0).astype(BF)


def unpack(ref, each):
    stats = ref[each * RANK :, :].astype(F32)
    states = []
    for i in range(each):
        three = [stats[at : at + 1] for at in range(6 * i, 6 * i + 6)]
        peak, total = three[0] + three[1] + three[2], three[3] + three[4] + three[5]
        states.append((peak, total, ref[i * RANK : (i + 1) * RANK, :].astype(F32)))
    return states


def join_parts_kernel(each, *refs):
    refs, out_ref = refs[:-1], refs[-1]
    parts = [unpack(ref, each) for ref in refs]
    pack([join([part[i] for part in parts]) for i in range(each)], out_ref)


def join_parts(parts):
    return pl.pallas_call(
        functools.partial(join_parts_kernel, (parts[0].shape[0] - 16) // RANK),
        out_shape=jax.ShapeDtypeStruct(parts[0].shape, BF),
        compiler_params=pltpu.CompilerParams(vmem_limit_bytes=4 * 1024 * 1024),
        cost_estimate=pl.CostEstimate(flops=1, bytes_accessed=1, transcendentals=0),
        name="join_parts",
    )(*parts)


def project_out_kernel(requests, steps, *refs):
    up_ref, weight_ref, out_ref = refs[-3:]
    each = up_ref.shape[0]
    parts = [unpack(ref, each) for ref in refs[:-3]]
    lanes = refs[0].shape[1]
    rows = requests * steps
    heads = lanes // rows
    old = lax.broadcasted_iota(jnp.int32, (lanes, lanes), 0)
    new = lax.broadcasted_iota(jnp.int32, (lanes, lanes), 1)
    request, rest = old // (heads * steps), old % (heads * steps)
    moved = (rest // steps) * rows + request * steps + rest % steps
    order = jnp.where(moved == new, 1.0, 0.0).astype(BF)
    context = []
    for i in range(each):
        _, total, summed = join([part[i] for part in parts])
        scaled = (summed / total).astype(BF)
        one = lax.dot_general(
            up_ref[i], scaled, (((0,), (0,)), ((), ())), preferred_element_type=F32
        ).astype(BF)
        one = lax.dot_general(
            order, one, (((0,), (1,)), ((), ())), preferred_element_type=F32
        ).astype(BF)
        context += [one[j * rows : (j + 1) * rows, :] for j in range(heads)]
    out_ref[...] = jnp.dot(
        jnp.concatenate(context, axis=1), weight_ref[...], preferred_element_type=F32
    )


def project_out(parts, value_up, out_proj, requests, steps):
    return pl.pallas_call(
        functools.partial(project_out_kernel, requests, steps),
        out_shape=jax.ShapeDtypeStruct((requests * steps, out_proj.shape[1]), F32),
        compiler_params=pltpu.CompilerParams(vmem_limit_bytes=24 * 1024 * 1024),
        cost_estimate=pl.CostEstimate(flops=1, bytes_accessed=1, transcendentals=0),
        name="project_out",
    )(*parts, value_up, out_proj)


def take(stack, index, axis=0):
    return lax.dynamic_index_in_dim(stack, index, axis, keepdims=False)


def tie(*values):
    leaves, tree = jax.tree.flatten(values)
    arrays = [i for i, leaf in enumerate(leaves) if getattr(leaf, "ndim", 0)]
    for i, leaf in zip(arrays, lax.optimization_barrier([leaves[i] for i in arrays])):
        leaves[i] = leaf
    return jax.tree.unflatten(tree, leaves)


def turn_query_kernel(query_width, latent_width, sums_ref, cos_ref, sin_ref, out_ref):
    sums = sums_ref[0]
    for k in range(1, sums_ref.shape[0]):
        sums = sums + sums_ref[k]
    at = query_width + latent_width
    sums = sums * lax.rsqrt(sums[:, at : at + 1] / D + 1e-05)
    cosine, sines = cos_ref[...], sin_ref[...]
    for h in range(query_width // HD):
        one = sums[:, h * HD : (h + 1) * HD]
        one = one * cosine + pltpu.roll(one, HD // 2, 1) * sines
        out_ref[:, h * HD : (h + 1) * HD] = one.astype(BF)
    out_ref[:, query_width:at] = sums[:, query_width:at].astype(BF)


def turn_query(sums, cosine, sines, query_width, latent_width):
    return pl.pallas_call(
        functools.partial(turn_query_kernel, query_width, latent_width),
        out_shape=jax.ShapeDtypeStruct((sums.shape[1], query_width + latent_width), BF),
        compiler_params=pltpu.CompilerParams(vmem_limit_bytes=4 * 1024 * 1024),
        name="turn_query",
    )(sums, cosine, sines)


def pick_kernel(ids_ref, table_ref, weight_ref, keep_ref, send_ref, weight_out, buf, sems, weight_sem):
    bring = pltpu.make_async_copy(weight_ref, weight_out, weight_sem)
    bring.start()
    side = lax.axis_index("side")
    rows = table_ref.shape[0]
    requests, steps = ids_ref.shape
    count = requests * steps
    places = []
    for i in range(count):
        place = ids_ref[i // steps, i % steps] - side * rows
        inside = jnp.logical_and(place >= 0, place < rows)
        place = jnp.where(inside, place, 0)
        start = pl.multiple_of(lax.div(place, FRESH) * FRESH, FRESH)
        pltpu.make_async_copy(table_ref.at[pl.ds(start, FRESH), :], buf.at[i], sems.at[i]).start()
        places.append(jnp.where(inside, place - start, FRESH))
    row = lax.broadcasted_iota(jnp.int32, buf.shape[1:], 0)
    for half in range(2):
        picked = []
        for i in range(half * count // 2, (half + 1) * count // 2):
            pltpu.make_async_copy(table_ref.at[pl.ds(0, FRESH), :], buf.at[i], sems.at[i]).wait()
            one = jnp.where(row == places[i], buf[i].astype(F32), 0.0)
            picked.append(jnp.sum(one, axis=0, keepdims=True))
        picked = jnp.concatenate(picked, axis=0).astype(BF)

        @pl.when(side == half)
        def _():
            keep_ref[...] = picked

        @pl.when(side != half)
        def _():
            send_ref[...] = picked

    bring.wait()


def pick(ids, table, weight):
    width = table.shape[1]
    half = jax.ShapeDtypeStruct((ids.size // 2, width), BF)
    return pl.pallas_call(
        pick_kernel,
        out_shape=(half, half, pltpu.VMEM(weight.shape, weight.dtype)),
        in_specs=[
            pl.BlockSpec(memory_space=pltpu.SMEM),
            pl.BlockSpec(memory_space=pl.ANY),
            pl.BlockSpec(memory_space=pl.ANY),
        ],
        out_specs=[
            pl.BlockSpec(memory_space=pltpu.VMEM),
            pl.BlockSpec(memory_space=pltpu.VMEM),
            pl.BlockSpec(memory_space=pl.ANY),
        ],
        scratch_shapes=[
            pltpu.VMEM((ids.size, FRESH, width), BF),
            pltpu.SemaphoreType.DMA((ids.size,)),
            pltpu.SemaphoreType.DMA,
        ],
        compiler_params=pltpu.CompilerParams(vmem_limit_bytes=12 * 1024 * 1024),
        name="pick",
    )(ids, table, weight)


def new_sums_kernel(blocks, one_ref, other_ref, query_ref, down_ref, keep_ref, send_ref):
    core = lax.rem(lax.axis_index("seq"), 2)
    rows = one_ref[...] + other_ref[...]
    widened = rows.astype(F32)
    squares = jnp.sum(widened * widened, axis=1, keepdims=True)
    latents = jnp.dot(rows, down_ref[...], preferred_element_type=F32)
    query_width = query_ref.shape[1] // blocks
    latent_width = down_ref.shape[1] // blocks
    rest = 128 - latent_width
    for k in range(blocks):
        part = slice(k * query_width, (k + 1) * query_width)
        query = jnp.dot(rows, query_ref[:, part], preferred_element_type=F32)
        tail = jnp.concatenate(
            [
                latents[:, k * latent_width : (k + 1) * latent_width],
                jnp.broadcast_to(squares, (rows.shape[0], rest)),
            ],
            axis=1,
        )
        for same, ref in ((True, keep_ref), (False, send_ref)):

            @pl.when((core == k % 2) == same)
            def _(ref=ref, query=query, tail=tail):
                ref[k // 2, :, :query_width] = query
                ref[k // 2, :, query_width:] = tail


def new_sums(blocks, one, other, query_proj, down_proj):
    width = query_proj.shape[1] // blocks + 128
    half = jax.ShapeDtypeStruct((blocks // 2, one.shape[0], width), F32)
    return pl.pallas_call(
        functools.partial(new_sums_kernel, blocks),
        out_shape=(half, half),
        compiler_params=pltpu.CompilerParams(vmem_limit_bytes=20 * 1024 * 1024),
        name="new_sums",
    )(one, other, query_proj, down_proj)


def arrange_kernel(query_width, *refs):
    refs, (query_ref, fresh_ref) = refs[:-2], refs[-2:]
    grid = Grid()
    heads, rows, width = refs[0].shape
    requests = query_ref.shape[0]
    steps = rows // requests
    cut = width // 2
    each = query_width // HD
    latent_width = cut - query_width
    fresh_ref[...] = jnp.zeros_like(fresh_ref)
    for dy, ref in enumerate(refs):
        y = lax.rem(grid.y + grid.ys - dy, grid.ys)
        for dz in range(heads):
            pair = y * heads + lax.rem(grid.z + heads - dz, heads)
            parts = 2 * each
            first = pair * parts
            g = lax.div(first, HQ // KVH)
            place = lax.rem(first, HQ // KVH) * steps
            for r in range(requests):
                own = []
                for h in range(parts):
                    at = h // each * cut + h % each * HD
                    own.append(ref[dz, r * steps : (r + 1) * steps, at : at + HD])
                start = pl.multiple_of(place, parts * steps)
                query_ref[r, g, pl.ds(start, parts * steps), :] = jnp.concatenate(own, axis=0)
            latents = [
                ref[dz, :, core * cut + query_width : (core + 1) * cut] for core in range(2)
            ]
            latents = jnp.concatenate(latents, axis=1)
            for r in range(requests):
                fresh_ref[r, pair, :steps, :] = latents[r * steps : (r + 1) * steps, :]


def arrange(by_y, requests, query_width):
    heads, rows, width = by_y[0].shape
    steps = rows // requests
    latents = width - 2 * query_width
    return pl.pallas_call(
        functools.partial(arrange_kernel, query_width),
        out_shape=(
            jax.ShapeDtypeStruct((requests, KVH, HQ // KVH * steps, HD), BF),
            jax.ShapeDtypeStruct((requests, len(by_y) * heads, FRESH, latents), BF),
        ),
        compiler_params=pltpu.CompilerParams(vmem_limit_bytes=8 * 1024 * 1024),
        name="arrange",
    )(*by_y)


def in_a_box(holds, step, *values):
    shapes = jax.eval_shape(step, *values)

    def otherwise(*_):
        return jax.tree.map(lambda one: jnp.zeros(one.shape, one.dtype), shapes)

    return lax.cond(holds, step, otherwise, *values)


def in_order(parts, mine):
    count = len(parts)
    if count == 2:
        swap = mine == 0
        return jnp.stack([jnp.where(swap, parts[0], parts[1]), jnp.where(swap, parts[1], parts[0])])
    twice = jnp.stack(parts[::-1] * 2)
    return lax.dynamic_slice_in_dim(twice, count - 1 - mine, count, 0)


def local(
    cached_hidden,
    page_order,
    lengths,
    new_ids,
    embedding,
    query_proj,
    down_proj,
    key_up,
    value_up,
    out_proj,
):
    grid = Grid()
    side, y, c, z = grid.side, grid.y, grid.c, grid.z
    ys, heads = grid.ys, grid.heads
    requests, span, width = cached_hidden.shape
    tokens, steps = new_ids.shape
    rows = requests * steps
    depth = down_proj.shape[0]
    hidden = cached_hidden.reshape(requests * span, width)
    hidden = pltpu.with_memory_space_constraint(hidden, pltpu.HBM)
    holds = new_ids[0, 0] >= 0

    def on_cores(*segments):
        return [
            [(rows, dy, dc, dz, base, step) for rows, dy, dz, base, step in segments]
            for dc in range(2)
        ]

    def both(piece, *segments):
        here, there = on_cores(*segments)
        return [(piece, here), (grid.send(piece, core=1), there)]

    def swapped(pieces):
        pairs = []
        for i, piece in enumerate(pieces):
            if i >= 2:
                piece, _ = tie(piece, pairs[i - 2][1])
            pairs.append((piece, grid.send(piece, core=1)))
        return pairs

    def add_pairs(pairs, places, latent):
        batch = []
        for pair, segments in zip(pairs, places):
            batch += list(zip(pair, on_cores(*segments)))
        return add_latents(hidden, depth, batch, latent)

    def project_shared(own, between):
        b = depth // 4

        def edge(piece):
            return piece, b, 0, 2 * b

        embed, over_y, over_head, spread, over_all, lay_out = between
        r0 = first_piece(own, key_up, b)
        r1 = grid.send(r0, head=1)
        y0 = grid.send(r0, y=1)

        extra = in_a_box(holds, lambda ids: over_y(embed(ids)), tie(new_ids, r0)[0])
        r1, y0, extra = tie(r1, y0, extra)

        other = (3 * b, -3 * b)
        at_own = [(4 * b, 0, 0, 0, 0)]
        at_r = [None] + [[(3 * b, 0, k, 0, b)] for k in range(1, heads)]
        at_y = [[(3 * b, 1, k, 0, b)] for k in range(3)] + [[(2 * b, 1, 3, 0, 2 * b)]]
        at_x = [
            None,
            [(b, 0, 1, *other), (b, 1, 0, *other)],
            [(b, 0, 2, *other), (b, 1, 1, *other)],
            [(b, 0, 3, *other), (b, 1, 2, *other)],
            [(2 * b, 1, 3, 2 * b, -2 * b)],
        ]

        r2 = grid.send(r1, head=1)
        y1 = grid.send(r1, y=1)
        (edges,) = assemble([edge(r1), edge(y0)])
        x1 = grid.send(edges, side=1)

        def first_latents(*pieces):
            latent = add_pairs(swapped(pieces), [at_own, at_r[1], at_y[0]], None)
            return latent, r0[3 * b :], r1[3 * b :]

        latent, up0, up1 = in_a_box(holds, first_latents, tie(own, edges)[0], r1, y0)
        tables = make_tables(*tie(lengths, page_order, r1)[:2])
        r2, y1, x1, latent, tables, extra = tie(r2, y1, x1, latent, tables, extra)

        r3 = grid.send(r2, head=1)
        y2 = grid.send(r2, y=1)
        (edges,) = assemble([edge(r2), edge(y1)])
        x2 = grid.send(edges, side=1)

        def second_latents(pieces, latent, extra):
            extra = over_head(extra)
            latent = add_pairs(swapped(pieces), [at_r[2], at_y[1], at_x[1]], latent)
            return latent, extra, pieces[0][3 * b :]

        latent, extra, up2 = in_a_box(holds, second_latents, (r2, y1, x1), latent, extra)
        r3, y2, x2, latent, extra = tie(r3, y2, x2, latent, extra)

        last, edges = assemble([(r3, 2 * b, 0, b)], [edge(r3), edge(y2)])
        y3 = grid.send(last, y=1)
        x3 = grid.send(edges, side=1)
        tables, turns = tables
        extra, last = tie(extra, last)

        def third_latents(pieces, latent, extra, *turns):
            pairs = swapped(pieces)
            extra = spread(extra, *turns, pairs)
            return add_pairs(pairs, [at_r[3], at_y[2]], latent), extra, pieces[0][3 * b :]

        latent, extra, up3 = in_a_box(holds, third_latents, (r3, y2), latent, extra, *turns)
        x2, x3, y3, latent, extra = tie(x2, x3, y3, latent, extra)

        x4 = grid.send(y3, side=1)

        def fourth_latents(pieces, latent, extra):
            extra = over_all(extra)
            latent = add_pairs(swapped(pieces), [at_x[2], at_y[3], at_x[3]], latent)
            return latent, lay_out(extra)

        latent, extra = in_a_box(holds, fourth_latents, (x2, y3, x3), latent, extra)
        x4, latent, extra = tie(x4, latent, extra)
        batch = list(zip((x4, grid.send(x4, core=1)), on_cores(*at_x[4])))
        return batch, latent, (extra, ([up0, up1, up2, up3], 0), tables)

    def project_plain(own, between):
        latent = None
        ring = own
        for k in range(heads):
            if k:
                ring = grid.send(ring, head=1)
            if k:
                latent = add_latents(hidden, depth, batch, latent)
            batch = both(ring, (depth, 0, k, 0, 0))
            for dy in range(1, ys):
                latent = add_latents(hidden, depth, batch, latent)
                batch = both(grid.send(ring, y=dy), (depth, dy, k, 0, 0))
        tables, turns = make_tables(lengths, page_order)
        embed, over_y, over_head, spread, over_all, lay_out = between
        extra = spread(over_head(over_y(embed(new_ids))), *turns)
        extra = lay_out(over_all(extra))
        ups = [pack_up(key_up)]
        ups += [grid.send(ups[0], head=k) for k in range(1, heads)]
        return batch, latent, (extra, (ups, 0), tables)

    blocks = 2 * ys * heads
    query_width = query_proj.shape[1] // blocks
    latent_width = down_proj.shape[1] // blocks
    cut = query_width + latent_width

    def embed(ids):
        keep, rest, weight = pick(ids, embedding, query_proj)
        keep, rest = new_sums(blocks, keep, grid.send(rest, side=1), weight, down_proj)
        packed = keep + grid.send(rest, core=1)
        return packed.reshape(ys, heads, rows, -1)

    def reduce_over_y(packed):
        kept = take(packed, y)
        for dy in range(1, ys):
            kept = kept + grid.send(take(packed, (y + dy) % ys), y=dy)
        return kept

    def reduce_over_head(kept):
        return lax.all_to_all(kept, "head", 0, 0)

    def spread_query(mine, cosine, sines, after=()):
        block = turn_query(mine, cosine, sines, query_width, latent_width)
        pair = in_order([block, grid.send(block, core=1)], c)
        pair, _ = tie(jnp.concatenate([pair[0], pair[1]], axis=-1), after)
        return jnp.stack([pair] + [grid.send(pair, head=k) for k in range(1, heads)])

    def spread_over_y(by_head):
        return [by_head] + [grid.send(by_head, y=k) for k in range(1, ys)]

    def lay_out(by_y):
        return arrange(by_y, requests, query_width)

    def make_tables(lengths, page_order):
        pages = page_order.shape[1]
        logical = jnp.arange(pages, dtype=jnp.int32)
        page_of = jnp.sum(
            jnp.where(page_order[:, :, None] == logical[None, None, :], logical[None, :, None], 0), axis=1
        )
        start = ((y * 2 + c) * heads + z) * span
        positions = (
            start + page_of[:, :, None] * PAGE + jnp.arange(PAGE, dtype=jnp.int32)[None, None, :]
        ).reshape(requests, span)
        new_rows = jnp.arange(FRESH, dtype=jnp.int32)
        row_positions = jnp.concatenate(
            [positions, lengths[:, None] + jnp.minimum(new_rows, steps - 1)[None, :]], axis=1
        )
        cosine, sines = sincos(row_positions)
        lanes = max(128, HQ // KVH * steps)
        step_of = jnp.arange(lanes, dtype=jnp.int32) % steps
        holds_new = (y == 0) & (c == 0) & (z == 0)
        new_seen = (new_rows[:, None] <= step_of[None, :]) & holds_new
        live = jnp.concatenate(
            [
                jnp.broadcast_to((positions < lengths[:, None])[:, :, None], (requests, span, lanes)),
                jnp.broadcast_to(new_seen[None], (requests, FRESH, lanes)),
            ],
            axis=1,
        ).astype(F32)
        fresh_positions = lengths[:, None] + jnp.arange(steps, dtype=jnp.int32)[None, :]
        return (cosine, sines, live), sincos(fresh_positions.reshape(-1))

    between = [embed, reduce_over_y, reduce_over_head, spread_query, spread_over_y, lay_out]
    shared = ys == 2 and heads == 4 and grid.sides == 2 and depth % 512 == 0
    batch, latent, extra = (project_shared if shared else project_plain)(down_proj, between)
    (queries, fresh), (ups, up_row), (cosine, sines, live) = extra
    weight = pltpu.with_memory_space_constraint(out_proj, pltpu.HBM)
    states, weight = finish(
        span, hidden, depth, batch, latent, fresh, cosine, sines, live, queries, ups,
        up_row, weight, heads,
    )
    parts = [take(states, z)]
    for dz in range(1, heads):
        parts.append(grid.send(take(states, (z + dz) % heads), head=dz))
    state = join_parts(parts)
    states = [state]
    for dy in range(ys):
        for dc in range(2):
            if dy or dc:
                states.append(grid.send(state, y=dy, core=dc))
    partial_out = project_out(states, value_up, weight, requests, steps)
    sent = partial_out.astype(BF)
    attended = partial_out
    for dz in range(1, heads):
        attended = attended + grid.send(sent, head=dz).astype(F32)
    return attended.astype(BF).reshape(requests, steps, -1)


def solution(mesh):
    return jax.shard_map(
        local,
        mesh=mesh,
        in_specs=(
            P("side", ("seq", "head"), None),
            P("side", ("seq", "head")),
            P("side"),
            P(),
            P("side", ("seq", "head")),
            P(("seq", "head"), None),
            P(("seq", "head"), None),
            P("head", None, None),
            P("head", None, None),
            P("head", "seq"),
        ),
        out_specs=P("side", None, "seq"),
        check_vma=False,
    )
```

time: 177 us -> 144 us (0.81)
  waiting for transfers between devices: 58.7 us -> 41.5 us
  matrix products: 10.7 us -> 0 us
  local copies, waits for them, and re-layouts: 15.5 us -> 9.3 us
  other arithmetic: 6.37 us -> 4.39 us
    ppermute x40, waiting for transfers between devices: 58.7 us -> 35.6 us  [send(): return lax.ppermute(value, AXES, pairs)]
    dot_general x3 -> x0, matrix products: 10.7 us -> none  [the longest x1 4.61 us: local(): partial_out = jnp.dot(context, out_proj, preferred_element_type=F32)]
    pallas_call x4 -> x8, Pallas kernels: 8.89 us -> 18.9 us  [the longest x1 6.99 us: finish(): pl.pallas_call(functools.partial(finish_kernel, counts, segments, depth,...]
    all_to_all x0 -> x1, waiting for transfers between devices: none -> 5.85 us  [reduce_over_head(): return lax.all_to_all(kept, 'head', 0, 0)]
    unnamed x41 -> x20, local copies, waits for them, and re-layouts: 7.7 us -> 2.41 us
    pallas_call x3, Pallas kernels: 7.49 us -> 3.02 us  [assemble(): pl.pallas_call(functools.partial(assemble_kernel, layout), out_shape=shap...]
    all_to_all x0 -> x1, starting transfers between devices: none -> 4.15 us  [reduce_over_head(): return lax.all_to_all(kept, 'head', 0, 0)]
    pallas_call x4, Pallas kernels: 28.8 us -> 25 us  [add_latents(): pl.pallas_call(functools.partial(latent_kernel, counts, segments, depth,...]
  transfers between devices with their start and end apart: 40 -> 41, of which waited for: 19 -> 20; matrix products, arithmetic and copies ran while one was open for 11% -> 7% of each run, Pallas kernels for 17% -> 25%
where the time goes in v2:
time: 144 us
  Pallas kernels  46.9 us (33%)
  waiting for transfers between devices  41.5 us (29%)
  starting transfers between devices  40.5 us (28%)
  local copies, waits for them, and re-layouts  9.3 us (6%)
  other arithmetic  4.39 us (3%)
    ppermute x40, starting transfers between devices, send(): return lax.ppermute(value, AXES, pairs)  36.3 us
    ppermute x40, waiting for transfers between devices, send(): return lax.ppermute(value, AXES, pairs)  35.6 us
    pallas_call x4, Pallas kernels, add_latents(): pl.pallas_call(functools.partial(latent_kernel, counts, segments, depth,...  25 us
    pallas_call x1, Pallas kernels, finish(): pl.pallas_call(functools.partial(finish_kernel, counts, segments, depth,...  6.99 us
    all_to_all x1, waiting for transfers between devices, reduce_over_head(): return lax.all_to_all(kept, 'head', 0, 0)  5.85 us
    pallas_call x1, Pallas kernels, pick(): pl.pallas_call(pick_kernel, out_shape=(half, half, pltpu.VMEM(weight.shap...  4.59 us
    all_to_all x1, starting transfers between devices, reduce_over_head(): return lax.all_to_all(kept, 'head', 0, 0)  4.15 us
    pallas_call x1, Pallas kernels, new_sums(): pl.pallas_call(functools.partial(new_sums_kernel, blocks), out_shape=(hal...  3.1 us
  transfers between devices with their start and end apart: 41, of which 20 were waited for; matrix products, arithmetic and copies ran while one was open for 7% of the time, Pallas kernels for 25%

profile of v2, /device:TPU:0, one launch (start us, length us, event | category | flops | bytes accessed | tf_op | source)
XLA Modules:
  0.0 143.7 jit_solution(1867351103472129033)
XLA Ops:
  2.0 3.1 %collective-permute-start.19 = (bf16[400,1024]{1,0:T(8,128)(2,1)S(1)}, bf16[400,1024]{1,0:T(8,128)(2,1)}, u32[]{:S(2)}, u32[]{:S(2)}) collective-permute-start(bf16[400,1024]{1,0:T(8,128)(2,1)S(1)} %first_piece.1), channel_id=1, source_target_pairs={{0,1},{1,2},{2,3},{3,0},{4,5},{5,6},{6,7},{7,4},{8,9},{9,10},{10,1... | collective-permute-start | bytes 2457608 | tf_op jit(solution)/shard_map/ppermute | solution.py:57
  8.5 20.3 %conditional.5 = (f32[4,16,640]{2,1,0:T(8,128)S(1)}) conditional(s32[]{:T(128)} %bitcast.8, () %tuple.56, (s32[8,4]{0,1:T(4,128)}, bf16[32256,512]{1,0:T(8,128)(2,1)}, bf16[512,8192]{1,0:T(8,128)(2,1)}, bf16[512,1024]{1,0:T(8,128)(2,1)}, s32[]{:T(128)}) %tuple.58), branch_computations={%region_0.0_spmd, %region_1.2_spmd} | conditional | flops 122898 | bytes 8028769 | solution.py:665
  9.3 4.6 %pick.1 = (bf16[16,512]{1,0:T(8,128)(2,1)S(1)}, bf16[16,512]{1,0:T(8,128)(2,1)S(1)}, bf16[512,8192]{1,0:T(8,128)(2,1)S(1)}) custom-call(s32[8,4]{1,0:T(8,128)S(1)} %copy.15.ids_ref, bf16[32256,512]{1,0:T(8,128)(2,1)} %get-tuple-element.207.table_ref, bf16[512,8192]{1,0:T(8,128)(2,1)} %get-tuple-element.208.weight_ref), custom_call_target="tpu_custom_call" | custom-call | tf_op jit(solution)/shard_map/cond/branch_1_fun/pick/pallas_call | solution.py:550
  15.5 2.2 %collective-permute-done.10.other_ref = bf16[16,512]{1,0:T(8,128)(2,1)S(1)} collective-permute-done((bf16[16,512]{1,0:T(8,128)(2,1)S(1)}, bf16[16,512]{1,0:T(8,128)(2,1)S(1)}, u32[]{:S(2)}, u32[]{:S(2)}) %collective-permute-start.10) | collective-permute-done | bytes 16416 | tf_op jit(solution)/shard_map/cond/branch_1_fun/ppermute | solution.py:57
  17.7 3.1 %new_sums.1 = (f32[8,16,640]{2,1,0:T(8,128)S(1)}, f32[8,16,640]{2,1,0:T(8,128)S(1)}) custom-call(bf16[16,512]{1,0:T(8,128)(2,1)S(1)} %get-tuple-element.71.one_ref, bf16[16,512]{1,0:T(8,128)(2,1)S(1)} %collective-permute-done.10.other_ref, bf16[512,8192]{1,0:T(8,128)(2,1)S(1)} %get-tuple-element.73.query_ref, bf16[512,1024]{1,0:T(8,128)(2,1)S(1)} %copy-done.3), custom_call_target="tpu_custom_call" | custom-call | tf_op jit(solution)/shard_map/cond/branch_1_fun/new_sums/pallas_call | solution.py:603
  23.1 5.7 %collective-permute-done.12 = f32[4,16,640]{2,1,0:T(8,128)S(1)} collective-permute-done((f32[4,16,640]{2,1,0:T(8,128)S(1)}, f32[4,16,640]{2,1,0:T(8,128)S(1)}, u32[]{:S(2)}, u32[]{:S(2)}) %collective-permute-start.12) | collective-permute-done | bytes 163872 | tf_op jit(solution)/shard_map/cond/branch_1_fun/ppermute | solution.py:57
  35.0 12.6 %conditional.6 = (f32[768,1024]{1,0:T(8,128)}, bf16[16,1024]{1,0:T(8,128)(2,1)S(1)}, bf16[16,1024]{1,0:T(8,128)(2,1)S(1)}) conditional(s32[]{:T(128)} %bitcast.8, () %tuple.60, (bf16[512,1024]{1,0:T(8,128)(2,1)}, bf16[400,1024]{1,0:T(8,128)(2,1)}, bf16[400,1024]{1,0:T(8,128)(2,1)S(1)}, bf16[768,8192]{1,0:T(8,128)(2,1)}, ...), branch_computations={%region_2.3_spmd, %region_3.4_spmd} | conditional | flops 1 | bytes 10879121 | solution.py:665
  35.5 2.4 %collective-permute-done.refs_1_ = bf16[512,1024]{1,0:T(8,128)(2,1)S(1)} collective-permute-done((bf16[512,1024]{1,0:T(8,128)(2,1)}, bf16[512,1024]{1,0:T(8,128)(2,1)S(1)}, u32[]{:S(2)}, u32[]{:S(2)}) %collective-permute-start) | collective-permute-done | bytes 1048608 | tf_op jit(solution)/shard_map/cond/branch_1_fun/ppermute | solution.py:57
  40.2 7.3 %latents.4 = f32[768,1024]{1,0:T(8,128)} custom-call(bf16[768,8192]{1,0:T(8,128)(2,1)} %get-tuple-element.78.hidden_ref, bf16[512,1024]{1,0:T(8,128)(2,1)} %get-tuple-element.79.refs_0_, bf16[512,1024]{1,0:T(8,128)(2,1)S(1)} %collective-permute-done.refs_1_, bf16[400,1024]{1,0:T(8,128)(2,1)} %get-tuple-element.80.refs_2_, ...), custom_call_target="tpu_custom_call" | custom-call | flops 1 | bytes 1 | tf_op jit(solution)/shard_map/cond/branch_1_fun/latents/pallas_call | solution.py:156
  55.6 21.7 %conditional.7 = (f32[768,1024]{1,0:T(8,128)}, f32[4,16,640]{2,1,0:T(8,128)}, bf16[16,1024]{1,0:T(8,128)(2,1)}) conditional(s32[]{:T(128)} %bitcast.8, () %tuple.65, (bf16[400,1024]{1,0:T(8,128)(2,1)}, bf16[400,1024]{1,0:T(8,128)(2,1)S(1)}, bf16[256,1024]{1,0:T(8,128)(2,1)}, bf16[768,8192]{1,0:T(8,128)(2,1)}, f32[768,1024]{1,0:T(8,128)}, ...), branch_computations={%region_5.6_spmd, %region_6.7_spmd} | conditional | flops 1 | bytes 12484813 | solution.py:665
  59.2 4.2 %all-to-all-start = ((f32[4,16,640]{2,1,0:T(8,128)}), f32[4,16,640]{2,1,0:T(8,128)}, u32[]{:S(2)}, u32[]{:S(2)}) async-start(f32[4,16,640]{2,1,0:T(8,128)} %get-tuple-element.90), calls=%async_computation | async-start | bytes 327680 | tf_op jit(solution)/shard_map/cond/branch_1_fun/all_to_all | solution.py:840
  64.8 6.7 %latents.5 = f32[768,1024]{1,0:T(8,128)} custom-call(bf16[768,8192]{1,0:T(8,128)(2,1)} %get-tuple-element.84.hidden_ref, bf16[400,1024]{1,0:T(8,128)(2,1)} %get-tuple-element.85.refs_0_, bf16[400,1024]{1,0:T(8,128)(2,1)S(1)} %collective-permute-done.3.refs_1_, bf16[400,1024]{1,0:T(8,128)(2,1)} %copy-done.4, ...), custom_call_target="tpu_custom_call" | custom-call | flops 1 | bytes 1 | tf_op jit(solution)/shard_map/cond/branch_1_fun/latents/pallas_call | solution.py:156
  71.4 5.8 %all-to-all-done = f32[4,16,640]{2,1,0:T(8,128)} async-done(((f32[4,16,640]{2,1,0:T(8,128)}), f32[4,16,640]{2,1,0:T(8,128)}, u32[]{:S(2)}, u32[]{:S(2)}) %all-to-all-start) | async-done | bytes 163872 | tf_op jit(solution)/shard_map/cond/branch_1_fun/all_to_all | solution.py:840
  80.0 13.6 %conditional.8 = (f32[768,1024]{1,0:T(8,128)}, bf16[4,16,1152]{2,1,0:T(8,128)(2,1)S(1)}, bf16[16,1024]{1,0:T(8,128)(2,1)}) conditional(s32[]{:T(128)} %bitcast.8, () %tuple.68, (bf16[400,1024]{1,0:T(8,128)(2,1)S(1)}, bf16[400,1024]{1,0:T(8,128)(2,1)}, bf16[768,8192]{1,0:T(8,128)(2,1)}, f32[768,1024]{1,0:T(8,128)}, s32[]{:T(128)}, ...), branch_computations={%region_7.8_spmd, %region_8.9_spmd} | conditional | flops 313346 | bytes 7577875 | solution.py:665
  84.6 3.0 %collective-permute-start.18 = (bf16[16,1152]{1,0:T(8,128)(2,1)S(1)}, bf16[16,1152]{1,0:T(8,128)(2,1)S(1)}, u32[]{:S(2)}, u32[]{:S(2)}) collective-permute-start(bf16[16,1152]{1,0:T(8,128)(2,1)S(1)} %pad_maximum_fusion.1), channel_id=1, source_target_pairs={{0,3},{1,0},{2,1},{3,2},{4,7},{5,4},{6,5},{7,6},{8,11},{9,8},{10,9... | collective-permute-start | bytes 110600 | tf_op jit(solution)/shard_map/cond/branch_1_fun/ppermute | solution.py:57
  88.2 5.3 %latents.6 = f32[768,1024]{1,0:T(8,128)} custom-call(bf16[768,8192]{1,0:T(8,128)(2,1)} %get-tuple-element.91.hidden_ref, bf16[400,1024]{1,0:T(8,128)(2,1)S(1)} %get-tuple-element.92.refs_0_, bf16[400,1024]{1,0:T(8,128)(2,1)S(1)} %collective-permute-done.13.refs_1_, bf16[400,1024]{1,0:T(8,128)(2,1)} %get-tuple-element.93.refs_2_, ...), custom_call_target="tpu_custom_call" | custom-call | flops 1 | bytes 1 | tf_op jit(solution)/shard_map/cond/branch_1_fun/latents/pallas_call | solution.py:156
  95.2 14.4 %conditional.9 = (f32[768,1024]{1,0:T(8,128)S(1)}, bf16[4,8,32,128]{3,2,1,0:T(8,128)(2,1)S(1)}, bf16[4,8,16,128]{3,2,1,0:T(8,128)(2,1)S(1)}) conditional(s32[]{:T(128)} %bitcast.8, () %tuple.72, (bf16[256,1024]{1,0:T(8,128)(2,1)}, bf16[256,1024]{1,0:T(8,128)(2,1)}, bf16[256,1024]{1,0:T(8,128)(2,1)}, bf16[768,8192]{1,0:T(8,128)(2,1)}, ...), branch_computations={%region_9.10_spmd, %region_10.11_spmd} | conditional | flops 1 | bytes 6881465 | solution.py:665
  98.4 5.1 %collective-permute-done.9.refs_1_ = bf16[4,16,1152]{2,1,0:T(8,128)(2,1)S(1)} collective-permute-done((bf16[4,16,1152]{2,1,0:T(8,128)(2,1)S(1)}, bf16[4,16,1152]{2,1,0:T(8,128)(2,1)S(1)}, u32[]{:S(2)}, u32[]{:S(2)}) %collective-permute-start.9) | collective-permute-done | bytes 147488 | tf_op jit(solution)/shard_map/cond/branch_1_fun/ppermute | solution.py:57
  103.9 5.6 %latents.7 = f32[768,1024]{1,0:T(8,128)S(1)} custom-call(bf16[768,8192]{1,0:T(8,128)(2,1)} %get-tuple-element.100.hidden_ref, bf16[256,1024]{1,0:T(8,128)(2,1)} %get-tuple-element.101.refs_0_, bf16[256,1024]{1,0:T(8,128)(2,1)S(1)} %collective-permute-done.6.refs_1_, bf16[256,1024]{1,0:T(8,128)(2,1)} %get-tuple-element.102.refs_2_, ...), custom_call_target="tpu_custom_call" | custom-call | flops 1 | bytes 1 | tf_op jit(solution)/shard_map/cond/branch_1_fun/latents/pallas_call | solution.py:156
  113.1 7.0 %finish.1 = (bf16[4,144,128]{2,1,0:T(8,128)(2,1)S(1)}, bf16[2048,2048]{1,0:T(8,128)(2,1)S(1)}) custom-call(bf16[768,8192]{1,0:T(8,128)(2,1)} %bitcast.23, bf16[256,1024]{1,0:T(8,128)(2,1)S(1)} %collective-permute-done.29.refs_0_, bf16[256,1024]{1,0:T(8,128)(2,1)S(1)} %collective-permute-done.30.refs_1_, f32[768,1024]{1,0:T(8,128)} %copy-done.2, ...), custom_call_target="tpu_custom_call" | custom-call | flops 1 | bytes 1 | tf_op jit(solution)/shard_map/finish/pallas_call | solution.py:367
  122.3 2.8 %collective-permute-start.33 = (bf16[144,128]{1,0:T(8,128)(2,1)S(1)}, bf16[144,128]{1,0:T(8,128)(2,1)S(1)}, u32[]{:S(2)}, u32[]{:S(2)}) collective-permute-start(bf16[144,128]{1,0:T(8,128)(2,1)S(1)} %get-tuple-element.228), channel_id=1, source_target_pairs={{0,3},{1,0},{2,1},{3,2},{4,7},{5,4},{6,5},{7,6},{8,11},{9,8},{10,9... | collective-permute-start | bytes 110600 | tf_op jit(solution)/shard_map/ppermute | solution.py:57
  134.8 2.9 %collective-permute-start.38 = (bf16[16,2048]{1,0:T(8,128)(2,1)S(1)}, bf16[16,2048]{1,0:T(8,128)(2,1)S(1)}, u32[]{:S(2)}, u32[]{:S(2)}) collective-permute-start(bf16[16,2048]{1,0:T(8,128)(2,1)S(1)} %convert_element_type.51), channel_id=1, source_target_pairs={{0,2},{1,3},{2,0},{3,1},{4,6},{5,7},{6,4},{7,5},{8,10},{9,11},{10,... | collective-permute-start | bytes 196616 | tf_op jit(solution)/shard_map/ppermute | solution.py:57
  137.7 2.4 %collective-permute-done.37 = bf16[16,2048]{1,0:T(8,128)(2,1)S(1)} collective-permute-done((bf16[16,2048]{1,0:T(8,128)(2,1)S(1)}, bf16[16,2048]{1,0:T(8,128)(2,1)S(1)}, u32[]{:S(2)}, u32[]{:S(2)}) %collective-permute-start.37) | collective-permute-done | bytes 65568 | tf_op jit(solution)/shard_map/ppermute | solution.py:57
  140.1 2.4 %collective-permute-done.38 = bf16[16,2048]{1,0:T(8,128)(2,1)S(1)} collective-permute-done((bf16[16,2048]{1,0:T(8,128)(2,1)S(1)}, bf16[16,2048]{1,0:T(8,128)(2,1)S(1)}, u32[]{:S(2)}, u32[]{:S(2)}) %collective-permute-start.38) | collective-permute-done | bytes 65568 | tf_op jit(solution)/shard_map/ppermute | solution.py:57
  (141 shorter events, 60.8 us)
Async XLA Ops:
  2.0 26.9 %collective-permute-start.19 = (bf16[400,1024]{1,0:T(8,128)(2,1)S(1)}, bf16[400,1024]{1,0:T(8,128)(2,1)}, u32[]{:S(2)}, u32[]{:S(2)}) collective-permute-start(bf16[400,1024]{1,0:T(8,128)(2,1)S(1)} %first_piece.1), channel_id=1, source_target_pairs={{0,1},{1,2},{2,3},{3,0},{4,5},{5,6},{6,7},{7,4},{8,9},{9,10},{10,1... | collective-permute-start | bytes 2457608 | tf_op jit(solution)/shard_map/ppermute | solution.py:57
  5.1 23.9 %collective-permute-start.20 = (bf16[400,1024]{1,0:T(8,128)(2,1)S(1)}, bf16[400,1024]{1,0:T(8,128)(2,1)S(1)}, u32[]{:S(2)}, u32[]{:S(2)}) collective-permute-start(bf16[400,1024]{1,0:T(8,128)(2,1)S(1)} %first_piece.1), channel_id=1, source_target_pairs={{0,8},{1,9},{2,10},{3,11},{4,12},{5,13},{6,14},{7,15},{8,0},{9,1},... | collective-permute-start | bytes 2457608 | tf_op jit(solution)/shard_map/ppermute | solution.py:57
  22.5 6.3 %collective-permute-start.12 = (f32[4,16,640]{2,1,0:T(8,128)S(1)}, f32[4,16,640]{2,1,0:T(8,128)S(1)}, u32[]{:S(2)}, u32[]{:S(2)}) collective-permute-start(f32[4,16,640]{2,1,0:T(8,128)S(1)} %dynamic-slice_bitcast_fusion), channel_id=1, source_target_pairs={{0,8},{1,9},{2,10},{3,11},{4,12},{5,13},{6,14},{7,15},{8,0},{9,1},... | collective-permute-start | bytes 491528 | tf_op jit(solution)/shard_map/cond/branch_1_fun/ppermute | solution.py:57
  28.9 22.4 %collective-permute-start.21 = (bf16[400,1024]{1,0:T(8,128)(2,1)}, bf16[400,1024]{1,0:T(8,128)(2,1)}, u32[]{:S(2)}, u32[]{:S(2)}) collective-permute-start(bf16[400,1024]{1,0:T(8,128)(2,1)} %collective-permute-done.19.refs_0_), channel_id=1, source_target_pairs={{0,1},{1,2},{2,3},{3,0},{4,5},{5,6},{6,7},{7,4},{8,9},{9,10},{10,1... | collective-permute-start | bytes 2457608 | tf_op jit(solution)/shard_map/ppermute | solution.py:57
  30.6 20.7 %collective-permute-start.22 = (bf16[400,1024]{1,0:T(8,128)(2,1)}, bf16[400,1024]{1,0:T(8,128)(2,1)S(1)}, u32[]{:S(2)}, u32[]{:S(2)}) collective-permute-start(bf16[400,1024]{1,0:T(8,128)(2,1)} %collective-permute-done.19.refs_0_), channel_id=1, source_target_pairs={{0,8},{1,9},{2,10},{3,11},{4,12},{5,13},{6,14},{7,15},{8,0},{9,1},... | collective-permute-start | bytes 2457608 | tf_op jit(solution)/shard_map/ppermute | solution.py:57
  33.0 18.3 %collective-permute-start.23 = (bf16[256,1024]{1,0:T(8,128)(2,1)S(1)}, bf16[256,1024]{1,0:T(8,128)(2,1)}, u32[]{:S(2)}, u32[]{:S(2)}) collective-permute-start(bf16[256,1024]{1,0:T(8,128)(2,1)S(1)} %assemble.3), channel_id=1, source_target_pairs={{0,16},{1,17},{2,18},{3,19},{4,20},{5,21},{6,22},{7,23},{8,24},{9,... | collective-permute-start | bytes 1572872 | tf_op jit(solution)/shard_map/ppermute | solution.py:57
  51.3 26.0 %collective-permute-start.24 = (bf16[400,1024]{1,0:T(8,128)(2,1)}, bf16[400,1024]{1,0:T(8,128)(2,1)S(1)}, u32[]{:S(2)}, u32[]{:S(2)}) collective-permute-start(bf16[400,1024]{1,0:T(8,128)(2,1)} %collective-permute-done.21.refs_0_), channel_id=1, source_target_pairs={{0,1},{1,2},{2,3},{3,0},{4,5},{5,6},{6,7},{7,4},{8,9},{9,10},{10,1... | collective-permute-start | bytes 2457608 | tf_op jit(solution)/shard_map/ppermute | solution.py:57
  52.9 24.4 %collective-permute-start.25 = (bf16[400,1024]{1,0:T(8,128)(2,1)}, bf16[400,1024]{1,0:T(8,128)(2,1)}, u32[]{:S(2)}, u32[]{:S(2)}) collective-permute-start(bf16[400,1024]{1,0:T(8,128)(2,1)} %collective-permute-done.21.refs_0_), channel_id=1, source_target_pairs={{0,8},{1,9},{2,10},{3,11},{4,12},{5,13},{6,14},{7,15},{8,0},{9,1},... | collective-permute-start | bytes 2457608 | tf_op jit(solution)/shard_map/ppermute | solution.py:57
  55.0 22.3 %collective-permute-start.26 = (bf16[256,1024]{1,0:T(8,128)(2,1)S(1)}, bf16[256,1024]{1,0:T(8,128)(2,1)}, u32[]{:S(2)}, u32[]{:S(2)}) collective-permute-start(bf16[256,1024]{1,0:T(8,128)(2,1)S(1)} %assemble.4), channel_id=1, source_target_pairs={{0,16},{1,17},{2,18},{3,19},{4,20},{5,21},{6,22},{7,23},{8,24},{9,... | collective-permute-start | bytes 1572872 | tf_op jit(solution)/shard_map/ppermute | solution.py:57
  56.5 8.2 %collective-permute-start.4 = (bf16[400,1024]{1,0:T(8,128)(2,1)}, bf16[400,1024]{1,0:T(8,128)(2,1)S(1)}, u32[]{:S(2)}, u32[]{:S(2)}) collective-permute-start(bf16[400,1024]{1,0:T(8,128)(2,1)} %copy-done.4), channel_id=1, source_target_pairs={{0,4},{1,5},{2,6},{3,7},{4,0},{5,1},{6,2},{7,3},{8,12},{9,13},{10,... | collective-permute-start | bytes 2457608 | tf_op jit(solution)/shard_map/cond/branch_1_fun/ppermute | solution.py:57
  59.1 5.7 %collective-permute-start.5 = (bf16[256,1024]{1,0:T(8,128)(2,1)}, bf16[256,1024]{1,0:T(8,128)(2,1)S(1)}, u32[]{:S(2)}, u32[]{:S(2)}) collective-permute-start(bf16[256,1024]{1,0:T(8,128)(2,1)} %get-tuple-element.88.refs_4_), channel_id=1, source_target_pairs={{0,4},{1,5},{2,6},{3,7},{4,0},{5,1},{6,2},{7,3},{8,12},{9,13},{10,... | collective-permute-start | bytes 1572872 | tf_op jit(solution)/shard_map/cond/branch_1_fun/ppermute | solution.py:57
  59.2 18.1 %all-to-all-start = ((f32[4,16,640]{2,1,0:T(8,128)}), f32[4,16,640]{2,1,0:T(8,128)}, u32[]{:S(2)}, u32[]{:S(2)}) async-start(f32[4,16,640]{2,1,0:T(8,128)} %get-tuple-element.90), calls=%async_computation | async-start | bytes 327680 | tf_op jit(solution)/shard_map/cond/branch_1_fun/all_to_all | solution.py:840
  78.4 15.3 %collective-permute-start.27 = (bf16[256,1024]{1,0:T(8,128)(2,1)S(1)}, bf16[256,1024]{1,0:T(8,128)(2,1)}, u32[]{:S(2)}, u32[]{:S(2)}) collective-permute-start(bf16[256,1024]{1,0:T(8,128)(2,1)S(1)} %get-tuple-element.175), channel_id=1, source_target_pairs={{0,16},{1,17},{2,18},{3,19},{4,20},{5,21},{6,22},{7,23},{8,24},{9,... | collective-permute-start | bytes 1572872 | tf_op jit(solution)/shard_map/ppermute | solution.py:57
  79.0 14.7 %collective-permute-start.28 = (bf16[256,1024]{1,0:T(8,128)(2,1)S(1)}, bf16[256,1024]{1,0:T(8,128)(2,1)}, u32[]{:S(2)}, u32[]{:S(2)}) collective-permute-start(bf16[256,1024]{1,0:T(8,128)(2,1)S(1)} %get-tuple-element.176), channel_id=1, source_target_pairs={{0,8},{1,9},{2,10},{3,11},{4,12},{5,13},{6,14},{7,15},{8,0},{9,1},... | collective-permute-start | bytes 1572872 | tf_op jit(solution)/shard_map/ppermute | solution.py:57
  83.8 9.8 %collective-permute-start.16 = (bf16[16,1152]{1,0:T(8,128)(2,1)S(1)}, bf16[16,1152]{1,0:T(8,128)(2,1)S(1)}, u32[]{:S(2)}, u32[]{:S(2)}) collective-permute-start(bf16[16,1152]{1,0:T(8,128)(2,1)S(1)} %pad_maximum_fusion.1), channel_id=1, source_target_pairs={{0,1},{1,2},{2,3},{3,0},{4,5},{5,6},{6,7},{7,4},{8,9},{9,10},{10,1... | collective-permute-start | bytes 110600 | tf_op jit(solution)/shard_map/cond/branch_1_fun/ppermute | solution.py:57
  83.8 9.8 %collective-permute-start.17 = (bf16[16,1152]{1,0:T(8,128)(2,1)S(1)}, bf16[16,1152]{1,0:T(8,128)(2,1)S(1)}, u32[]{:S(2)}, u32[]{:S(2)}) collective-permute-start(bf16[16,1152]{1,0:T(8,128)(2,1)S(1)} %pad_maximum_fusion.1), channel_id=1, source_target_pairs={{0,2},{1,3},{2,0},{3,1},{4,6},{5,7},{6,4},{7,5},{8,10},{9,11},{10,... | collective-permute-start | bytes 110600 | tf_op jit(solution)/shard_map/cond/branch_1_fun/ppermute | solution.py:57
  84.6 9.0 %collective-permute-start.18 = (bf16[16,1152]{1,0:T(8,128)(2,1)S(1)}, bf16[16,1152]{1,0:T(8,128)(2,1)S(1)}, u32[]{:S(2)}, u32[]{:S(2)}) collective-permute-start(bf16[16,1152]{1,0:T(8,128)(2,1)S(1)} %pad_maximum_fusion.1), channel_id=1, source_target_pairs={{0,3},{1,0},{2,1},{3,2},{4,7},{5,4},{6,5},{7,6},{8,11},{9,8},{10,9... | collective-permute-start | bytes 110600 | tf_op jit(solution)/shard_map/cond/branch_1_fun/ppermute | solution.py:57
  93.6 16.0 %collective-permute-start.29 = (bf16[256,1024]{1,0:T(8,128)(2,1)}, bf16[256,1024]{1,0:T(8,128)(2,1)S(1)}, u32[]{:S(2)}, u32[]{:S(2)}) collective-permute-start(bf16[256,1024]{1,0:T(8,128)(2,1)} %collective-permute-done.28), channel_id=1, source_target_pairs={{0,16},{1,17},{2,18},{3,19},{4,20},{5,21},{6,22},{7,23},{8,24},{9,... | collective-permute-start | bytes 1572872 | tf_op jit(solution)/shard_map/ppermute | solution.py:57
  95.2 8.7 %collective-permute-start.7 = (bf16[256,1024]{1,0:T(8,128)(2,1)}, bf16[256,1024]{1,0:T(8,128)(2,1)S(1)}, u32[]{:S(2)}, u32[]{:S(2)}) collective-permute-start(bf16[256,1024]{1,0:T(8,128)(2,1)} %get-tuple-element.102.refs_2_), channel_id=1, source_target_pairs={{0,4},{1,5},{2,6},{3,7},{4,0},{5,1},{6,2},{7,3},{8,12},{9,13},{10,... | collective-permute-start | bytes 1572872 | tf_op jit(solution)/shard_map/cond/branch_1_fun/ppermute | solution.py:57
  97.3 6.6 %collective-permute-start.8 = (bf16[256,1024]{1,0:T(8,128)(2,1)}, bf16[256,1024]{1,0:T(8,128)(2,1)S(1)}, u32[]{:S(2)}, u32[]{:S(2)}) collective-permute-start(bf16[256,1024]{1,0:T(8,128)(2,1)} %get-tuple-element.104.refs_4_), channel_id=1, source_target_pairs={{0,4},{1,5},{2,6},{3,7},{4,0},{5,1},{6,2},{7,3},{8,12},{9,13},{10,... | collective-permute-start | bytes 1572872 | tf_op jit(solution)/shard_map/cond/branch_1_fun/ppermute | solution.py:57
  97.5 6.1 %collective-permute-start.9 = (bf16[4,16,1152]{2,1,0:T(8,128)(2,1)S(1)}, bf16[4,16,1152]{2,1,0:T(8,128)(2,1)S(1)}, u32[]{:S(2)}, u32[]{:S(2)}) collective-permute-start(bf16[4,16,1152]{2,1,0:T(8,128)(2,1)S(1)} %get-tuple-element.106.refs_0_), channel_id=1, source_target_pairs={{0,8},{1,9},{2,10},{3,11},{4,12},{5,13},{6,14},{7,15},{8,0},{9,1},... | collective-permute-start | bytes 442376 | tf_op jit(solution)/shard_map/cond/branch_1_fun/ppermute | solution.py:57
  120.2 6.3 %collective-permute-start.31 = (bf16[144,128]{1,0:T(8,128)(2,1)S(1)}, bf16[144,128]{1,0:T(8,128)(2,1)S(1)}, u32[]{:S(2)}, u32[]{:S(2)}) collective-permute-start(bf16[144,128]{1,0:T(8,128)(2,1)S(1)} %get-tuple-element.230), channel_id=1, source_target_pairs={{0,1},{1,2},{2,3},{3,0},{4,5},{5,6},{6,7},{7,4},{8,9},{9,10},{10,1... | collective-permute-start | bytes 110600 | tf_op jit(solution)/shard_map/ppermute | solution.py:57
  132.9 7.1 %collective-permute-start.37 = (bf16[16,2048]{1,0:T(8,128)(2,1)S(1)}, bf16[16,2048]{1,0:T(8,128)(2,1)S(1)}, u32[]{:S(2)}, u32[]{:S(2)}) collective-permute-start(bf16[16,2048]{1,0:T(8,128)(2,1)S(1)} %convert_element_type.51), channel_id=1, source_target_pairs={{0,1},{1,2},{2,3},{3,0},{4,5},{5,6},{6,7},{7,4},{8,9},{9,10},{10,1... | collective-permute-start | bytes 196616 | tf_op jit(solution)/shard_map/ppermute | solution.py:57
  134.8 7.7 %collective-permute-start.38 = (bf16[16,2048]{1,0:T(8,128)(2,1)S(1)}, bf16[16,2048]{1,0:T(8,128)(2,1)S(1)}, u32[]{:S(2)}, u32[]{:S(2)}) collective-permute-start(bf16[16,2048]{1,0:T(8,128)(2,1)S(1)} %convert_element_type.51), channel_id=1, source_target_pairs={{0,2},{1,3},{2,0},{3,1},{4,6},{5,7},{6,4},{7,5},{8,10},{9,11},{10,... | collective-permute-start | bytes 196616 | tf_op jit(solution)/shard_map/ppermute | solution.py:57
  (29 other events, 190.9 us)

commit v3 on v2

--- a/solution.py
+++ b/solution.py
@@ -166,7 +166,11 @@
             pltpu.SemaphoreType.DMA((4,)),
         ],
         compiler_params=pltpu.CompilerParams(vmem_limit_bytes=28 * 1024 * 1024),
-        cost_estimate=pl.CostEstimate(flops=1, bytes_accessed=1, transcendentals=0),
+        cost_estimate=pl.CostEstimate(
+            flops=2 * rows * deep * columns,
+            bytes_accessed=2 * deep * (rows + columns) + 8 * rows * columns,
+            transcendentals=0,
+        ),
         name="latents",
     )(*operands)
 
@@ -321,14 +325,43 @@
         out_ref[b, each * RANK :, :] = jnp.concatenate(stats, axis=0).astype(BF)
 
 
-def finish_kernel(counts, segments, depth, scale, span, up_row, hidden_ref, *refs):
+def lay_tables(span, steps, start, order_ref, length_ref, small_cos, small_sin, cos_ref, sin_ref, live_ref):
+    requests, rows, lanes = cos_ref.shape
+    pages = order_ref.shape[1]
+    padded = -(-pages // 16) * 16
+    inner_cos, inner_sin = small_cos[padded : padded + PAGE, :], small_sin[padded : padded + PAGE, :]
+    inner = lax.broadcasted_iota(jnp.int32, (PAGE, lanes), 0)
+    grid = Grid()
+    first = grid.place(0, 0, 0) == 0
+    column_step = lax.rem(lax.broadcasted_iota(jnp.int32, (FRESH, lanes), 1), steps)
+    new_row = lax.broadcasted_iota(jnp.int32, (FRESH, lanes), 0)
+    seen = jnp.where(jnp.logical_and(new_row <= column_step, first), 1.0, 0.0)
+    for j in range(pages):
+        page_cos, page_sin = small_cos[j : j + 1, :], small_sin[j : j + 1, :]
+        cosine = page_cos * inner_cos - page_sin * inner_sin
+        sines = page_sin * inner_cos + page_cos * inner_sin
+        for r in range(requests):
+            at = pl.multiple_of(order_ref[r, j] * PAGE, PAGE)
+            cos_ref[r, pl.ds(at, PAGE), :] = cosine
+            sin_ref[r, pl.ds(at, PAGE), :] = sines
+            position = start + j * PAGE + inner
+            live_ref[r, pl.ds(at, PAGE), :] = jnp.where(position < length_ref[r], 1.0, 0.0)
+    fill = jnp.zeros((FRESH - steps, lanes), F32)
+    new = padded + PAGE
+    for r in range(requests):
+        own = slice(new + r * steps, new + (r + 1) * steps)
+        cos_ref[r, span:, :] = jnp.concatenate([small_cos[own, :], fill], axis=0)
+        sin_ref[r, span:, :] = jnp.concatenate([small_sin[own, :], fill], axis=0)
+        live_ref[r, span:, :] = seen
+
+
+def finish_kernel(counts, segments, depth, scale, span, up_row, steps, order_ref, length_ref, *refs):
+    small_cos, small_sin, hidden_ref, refs = refs[0], refs[1], refs[2], refs[3:]
     pieces, refs = refs[: len(counts)], refs[len(counts) :]
-    before_ref, refs = refs[0], refs[1:]
     heads = lax.axis_size("head")
-    tables, ups, weight_ref, refs = refs[:5], refs[5 : 5 + heads], refs[5 + heads], refs[6 + heads :]
-    out_ref, weight_out, hidden_buf, piece_buf, total = refs[:5]
-    held, up_buf, table_sems, weight_sem = refs[5:10], refs[11], refs[12], refs[13]
-    sems = refs[10]
+    before_ref, tables, ups, weight_ref = refs[0], refs[1:3], refs[3 : 3 + heads], refs[3 + heads]
+    out_ref, weight_out, hidden_buf, piece_buf, total, *refs = refs[4 + heads :]
+    held, (cos_ref, sin_ref, live_ref, up_buf, sems, table_sems, weight_sem) = refs[:2], refs[2:]
     loads = [
         pltpu.make_async_copy(table, buf, table_sems.at[i])
         for i, (table, buf) in enumerate(zip(tables, held))
@@ -343,34 +376,48 @@
         )
     for load in loads:
         load.start()
+    grid = Grid()
+    start = grid.place(0, 0, 0) * span
+    lay_tables(
+        span, steps, start, order_ref, length_ref, small_cos, small_sin, cos_ref, sin_ref, live_ref
+    )
     accumulate(counts, segments, depth, hidden_ref, pieces, before_ref, hidden_buf, piece_buf, total, sems)
     for load in loads:
         load.wait()
     bring = pltpu.make_async_copy(weight_ref, weight_out, weight_sem)
     bring.start()
-    attend_part(scale, span, total, *held, up_buf, out_ref)
+    fresh, queries = held
+    attend_part(scale, span, total, fresh, cos_ref, sin_ref, live_ref, queries, up_buf, out_ref)
     bring.wait()
 
 
-def finish(span, hidden, depth, batch, total, fresh, cosine, sines, live, queries, ups, up_row, weight, blocks):
+def finish(
+    span, hidden, depth, batch, total, fresh, cosine, sines, queries, ups, up_row, weight, blocks,
+    page_order, lengths, steps,
+):
     pieces = [piece for piece, _ in batch]
     counts = [sum(part[0] for part in parts) for _, parts in batch]
     segments = [(i, *part) for i, (_, parts) in enumerate(batch) for part in parts]
     deep, columns = sum(counts), pieces[0].shape[1]
     rows = hidden.shape[0]
     requests, groups, lanes, _ = queries.shape
-    tables = (fresh, cosine, sines, live, queries)
-    far = [pltpu.with_memory_space_constraint(t, pltpu.HBM) for t in (cosine, sines, live)]
-    tables = (fresh, *far, queries)
-    operands = [hidden, *pieces, total, *tables, *ups, weight]
+    tables = (fresh, queries)
+    wide = (requests, span + FRESH, HD)
+    total = pltpu.with_memory_space_constraint(total, pltpu.VMEM)
+    operands = [page_order, lengths, cosine, sines, hidden, *pieces, total, *tables, *ups, weight]
+    far = [pl.BlockSpec(memory_space=pl.ANY)] * (len(operands) - 4)
     state_rows = groups // blocks * RANK + 16
     return pl.pallas_call(
-        functools.partial(finish_kernel, counts, segments, depth, 1.0 / math.sqrt(HD), span, up_row),
+        functools.partial(
+            finish_kernel, counts, segments, depth, 1.0 / math.sqrt(HD), span, up_row, steps
+        ),
         out_shape=(
             jax.ShapeDtypeStruct((blocks, state_rows, requests * lanes), BF),
             pltpu.VMEM(weight.shape, weight.dtype),
         ),
-        in_specs=[pl.BlockSpec(memory_space=pl.ANY)] * len(operands),
+        in_specs=[pl.BlockSpec(memory_space=pltpu.SMEM)] * 2
+        + [pl.BlockSpec(memory_space=pltpu.VMEM)] * 2
+        + far,
         out_specs=(pl.BlockSpec(memory_space=pltpu.VMEM), pl.BlockSpec(memory_space=pl.ANY)),
         scratch_shapes=[
             pltpu.VMEM((rows, deep), BF),
@@ -378,13 +425,14 @@
             pltpu.VMEM((rows, columns), F32),
         ]
         + [pltpu.VMEM(table.shape, table.dtype) for table in tables]
+        + [pltpu.VMEM(wide, F32)] * 3
         + [
+            pltpu.VMEM((len(ups), FRESH, ups[0].shape[1]), BF),
             pltpu.SemaphoreType.DMA((len(segments) + len(pieces) + 1,)),
-            pltpu.VMEM((len(ups), FRESH, ups[0].shape[1]), BF),
             pltpu.SemaphoreType.DMA((len(tables) + len(ups),)),
             pltpu.SemaphoreType.DMA,
         ],
-        compiler_params=pltpu.CompilerParams(vmem_limit_bytes=28 * 1024 * 1024),
+        compiler_params=pltpu.CompilerParams(vmem_limit_bytes=18 * 1024 * 1024),
         cost_estimate=pl.CostEstimate(flops=1, bytes_accessed=1, transcendentals=0),
         name="finish",
     )(*operands)
@@ -492,7 +540,8 @@
         sums = sums + sums_ref[k]
     at = query_width + latent_width
     sums = sums * lax.rsqrt(sums[:, at : at + 1] / D + 1e-05)
-    cosine, sines = cos_ref[...], sin_ref[...]
+    own = slice(cos_ref.shape[0] - sums.shape[0], None)
+    cosine, sines = cos_ref[own, :], sin_ref[own, :]
     for h in range(query_width // HD):
         one = sums[:, h * HD : (h + 1) * HD]
         one = one * cosine + pltpu.roll(one, HD // 2, 1) * sines
@@ -509,9 +558,7 @@
     )(sums, cosine, sines)
 
 
-def pick_kernel(ids_ref, table_ref, weight_ref, keep_ref, send_ref, weight_out, buf, sems, weight_sem):
-    bring = pltpu.make_async_copy(weight_ref, weight_out, weight_sem)
-    bring.start()
+def pick_kernel(ids_ref, table_ref, keep_ref, send_ref, buf, sems):
     side = lax.axis_index("side")
     rows = table_ref.shape[0]
     requests, steps = ids_ref.shape
@@ -541,36 +588,34 @@
         def _():
             send_ref[...] = picked
 
-    bring.wait()
-
-
-def pick(ids, table, weight):
+
+def pick(ids, table):
     width = table.shape[1]
     half = jax.ShapeDtypeStruct((ids.size // 2, width), BF)
     return pl.pallas_call(
         pick_kernel,
-        out_shape=(half, half, pltpu.VMEM(weight.shape, weight.dtype)),
-        in_specs=[
-            pl.BlockSpec(memory_space=pltpu.SMEM),
-            pl.BlockSpec(memory_space=pl.ANY),
-            pl.BlockSpec(memory_space=pl.ANY),
-        ],
-        out_specs=[
-            pl.BlockSpec(memory_space=pltpu.VMEM),
-            pl.BlockSpec(memory_space=pltpu.VMEM),
-            pl.BlockSpec(memory_space=pl.ANY),
-        ],
+        out_shape=(half, half),
+        in_specs=[pl.BlockSpec(memory_space=pltpu.SMEM), pl.BlockSpec(memory_space=pl.ANY)],
         scratch_shapes=[
             pltpu.VMEM((ids.size, FRESH, width), BF),
             pltpu.SemaphoreType.DMA((ids.size,)),
-            pltpu.SemaphoreType.DMA,
         ],
-        compiler_params=pltpu.CompilerParams(vmem_limit_bytes=12 * 1024 * 1024),
+        compiler_params=pltpu.CompilerParams(vmem_limit_bytes=4 * 1024 * 1024),
         name="pick",
-    )(ids, table, weight)
-
-
-def new_sums_kernel(blocks, one_ref, other_ref, query_ref, down_ref, keep_ref, send_ref):
+    )(ids, table)
+
+
+def new_sums_kernel(
+    blocks, one_ref, other_ref, query_far, down_ref, keep_ref, send_ref, query_ref, sems
+):
+    wide = query_ref.shape[1] // sems.shape[0]
+    copies = []
+    for k in range(sems.shape[0]):
+        part = pl.ds(k * wide, wide)
+        copies.append(
+            pltpu.make_async_copy(query_far.at[:, part], query_ref.at[:, part], sems.at[k])
+        )
+        copies[-1].start()
     core = lax.rem(lax.axis_index("seq"), 2)
     rows = one_ref[...] + other_ref[...]
     widened = rows.astype(F32)
@@ -581,6 +626,8 @@
     rest = 128 - latent_width
     for k in range(blocks):
         part = slice(k * query_width, (k + 1) * query_width)
+        if k * query_width % wide == 0:
+            copies[k * query_width // wide].wait()
         query = jnp.dot(rows, query_ref[:, part], preferred_element_type=F32)
         tail = jnp.concatenate(
             [
@@ -603,24 +650,31 @@
     return pl.pallas_call(
         functools.partial(new_sums_kernel, blocks),
         out_shape=(half, half),
+        in_specs=[pl.BlockSpec(memory_space=pltpu.VMEM)] * 2
+        + [pl.BlockSpec(memory_space=pl.ANY), pl.BlockSpec(memory_space=pltpu.VMEM)],
+        scratch_shapes=[
+            pltpu.VMEM(query_proj.shape, query_proj.dtype),
+            pltpu.SemaphoreType.DMA((8,)),
+        ],
         compiler_params=pltpu.CompilerParams(vmem_limit_bytes=20 * 1024 * 1024),
         name="new_sums",
-    )(one, other, query_proj, down_proj)
+    )(one, other, pltpu.with_memory_space_constraint(query_proj, pltpu.HBM), down_proj)
 
 
 def arrange_kernel(query_width, *refs):
     refs, (query_ref, fresh_ref) = refs[:-2], refs[-2:]
     grid = Grid()
-    heads, rows, width = refs[0].shape
+    ys, rows, width = refs[0].shape
+    heads = len(refs)
     requests = query_ref.shape[0]
     steps = rows // requests
     cut = width // 2
     each = query_width // HD
     latent_width = cut - query_width
     fresh_ref[...] = jnp.zeros_like(fresh_ref)
-    for dy, ref in enumerate(refs):
-        y = lax.rem(grid.y + grid.ys - dy, grid.ys)
-        for dz in range(heads):
+    for dz, ref in enumerate(refs):
+        for dy in range(ys):
+            y = lax.rem(grid.y + ys - dy, ys)
             pair = y * heads + lax.rem(grid.z + heads - dz, heads)
             parts = 2 * each
             first = pair * parts
@@ -630,30 +684,30 @@
                 own = []
                 for h in range(parts):
                     at = h // each * cut + h % each * HD
-                    own.append(ref[dz, r * steps : (r + 1) * steps, at : at + HD])
+                    own.append(ref[dy, r * steps : (r + 1) * steps, at : at + HD])
                 start = pl.multiple_of(place, parts * steps)
                 query_ref[r, g, pl.ds(start, parts * steps), :] = jnp.concatenate(own, axis=0)
             latents = [
-                ref[dz, :, core * cut + query_width : (core + 1) * cut] for core in range(2)
+                ref[dy, :, core * cut + query_width : (core + 1) * cut] for core in range(2)
             ]
             latents = jnp.concatenate(latents, axis=1)
             for r in range(requests):
                 fresh_ref[r, pair, :steps, :] = latents[r * steps : (r + 1) * steps, :]
 
 
-def arrange(by_y, requests, query_width):
-    heads, rows, width = by_y[0].shape
+def arrange(by_head, requests, query_width):
+    ys, rows, width = by_head[0].shape
     steps = rows // requests
     latents = width - 2 * query_width
     return pl.pallas_call(
         functools.partial(arrange_kernel, query_width),
         out_shape=(
             jax.ShapeDtypeStruct((requests, KVH, HQ // KVH * steps, HD), BF),
-            jax.ShapeDtypeStruct((requests, len(by_y) * heads, FRESH, latents), BF),
+            jax.ShapeDtypeStruct((requests, ys * len(by_head), FRESH, latents), BF),
         ),
         compiler_params=pltpu.CompilerParams(vmem_limit_bytes=8 * 1024 * 1024),
         name="arrange",
-    )(*by_y)
+    )(*by_head)
 
 
 def in_a_box(holds, step, *values):
@@ -707,11 +761,11 @@
         here, there = on_cores(*segments)
         return [(piece, here), (grid.send(piece, core=1), there)]
 
-    def swapped(pieces):
+    def swapped(pieces, at_once=2):
         pairs = []
         for i, piece in enumerate(pieces):
-            if i >= 2:
-                piece, _ = tie(piece, pairs[i - 2][1])
+            if i >= at_once:
+                piece, _ = tie(piece, pairs[i - at_once][1])
             pairs.append((piece, grid.send(piece, core=1)))
         return pairs
 
@@ -727,7 +781,7 @@
         def edge(piece):
             return piece, b, 0, 2 * b
 
-        embed, over_y, over_head, spread, over_all, lay_out = between
+        embed, over_y, over_head, turn, spread_y, spread, lay_out = between
         r0 = first_piece(own, key_up, b)
         r1 = grid.send(r0, head=1)
         y0 = grid.send(r0, y=1)
@@ -757,32 +811,32 @@
             return latent, r0[3 * b :], r1[3 * b :]
 
         latent, up0, up1 = in_a_box(holds, first_latents, tie(own, edges)[0], r1, y0)
-        tables = make_tables(*tie(lengths, page_order, r1)[:2])
-        r2, y1, x1, latent, tables, extra = tie(r2, y1, x1, latent, tables, extra)
+        r2, y1, x1, latent, extra = tie(r2, y1, x1, latent, extra)
 
         r3 = grid.send(r2, head=1)
         y2 = grid.send(r2, y=1)
         (edges,) = assemble([edge(r2), edge(y1)])
         x2 = grid.send(edges, side=1)
 
-        def second_latents(pieces, latent, extra):
-            extra = over_head(extra)
+        def second_latents(pieces, latent, lengths):
             latent = add_pairs(swapped(pieces), [at_r[2], at_y[1], at_x[1]], latent)
-            return latent, extra, pieces[0][3 * b :]
-
-        latent, extra, up2 = in_a_box(holds, second_latents, (r2, y1, x1), latent, extra)
-        r3, y2, x2, latent, extra = tie(r3, y2, x2, latent, extra)
+            return latent, make_turns(lengths), pieces[0][3 * b :]
+
+        latent, turns, up2 = in_a_box(
+            holds, second_latents, (r2, y1, x1), latent, tie(lengths, r2)[0]
+        )
+        r3, y2, x2, latent = tie(r3, y2, x2, latent)
 
         last, edges = assemble([(r3, 2 * b, 0, b)], [edge(r3), edge(y2)])
         y3 = grid.send(last, y=1)
         x3 = grid.send(edges, side=1)
-        tables, turns = tables
         extra, last = tie(extra, last)
 
         def third_latents(pieces, latent, extra, *turns):
-            pairs = swapped(pieces)
-            extra = spread(extra, *turns, pairs)
-            return add_pairs(pairs, [at_r[3], at_y[2]], latent), extra, pieces[0][3 * b :]
+            extra = over_head(extra)
+            latent = add_pairs(swapped(pieces), [at_r[3], at_y[2]], latent)
+            extra, latent = tie(extra, latent)
+            return latent, turn(extra, *turns), pieces[0][3 * b :]
 
         latent, extra, up3 = in_a_box(holds, third_latents, (r3, y2), latent, extra, *turns)
         x2, x3, y3, latent, extra = tie(x2, x3, y3, latent, extra)
@@ -790,14 +844,16 @@
         x4 = grid.send(y3, side=1)
 
         def fourth_latents(pieces, latent, extra):
-            extra = over_all(extra)
-            latent = add_pairs(swapped(pieces), [at_x[2], at_y[3], at_x[3]], latent)
-            return latent, lay_out(extra)
+            extra = spread_y(extra)
+            pairs = swapped(pieces)
+            extra, pairs = tie(extra, pairs)
+            latent = add_pairs(pairs, [at_x[2], at_y[3], at_x[3]], latent)
+            return latent, lay_out(spread(extra))
 
         latent, extra = in_a_box(holds, fourth_latents, (x2, y3, x3), latent, extra)
         x4, latent, extra = tie(x4, latent, extra)
         batch = list(zip((x4, grid.send(x4, core=1)), on_cores(*at_x[4])))
-        return batch, latent, (extra, ([up0, up1, up2, up3], 0), tables)
+        return batch, latent, (extra, ([up0, up1, up2, up3], 0), turns)
 
     def project_plain(own, between):
         latent = None
@@ -811,13 +867,13 @@
             for dy in range(1, ys):
                 latent = add_latents(hidden, depth, batch, latent)
                 batch = both(grid.send(ring, y=dy), (depth, dy, k, 0, 0))
-        tables, turns = make_tables(lengths, page_order)
-        embed, over_y, over_head, spread, over_all, lay_out = between
-        extra = spread(over_head(over_y(embed(new_ids))), *turns)
-        extra = lay_out(over_all(extra))
+        turns = make_turns(lengths)
+        embed, over_y, over_head, turn, spread_y, spread, lay_out = between
+        extra = turn(over_head(over_y(embed(new_ids))), *turns)
+        extra = lay_out(spread(spread_y(extra)))
         ups = [pack_up(key_up)]
         ups += [grid.send(ups[0], head=k) for k in range(1, heads)]
-        return batch, latent, (extra, (ups, 0), tables)
+        return batch, latent, (extra, (ups, 0), turns)
 
     blocks = 2 * ys * heads
     query_width = query_proj.shape[1] // blocks
@@ -825,8 +881,8 @@
     cut = query_width + latent_width
 
     def embed(ids):
-        keep, rest, weight = pick(ids, embedding, query_proj)
-        keep, rest = new_sums(blocks, keep, grid.send(rest, side=1), weight, down_proj)
+        keep, rest = pick(ids, embedding)
+        keep, rest = new_sums(blocks, keep, grid.send(rest, side=1), query_proj, down_proj)
         packed = keep + grid.send(rest, core=1)
         return packed.reshape(ys, heads, rows, -1)
 
@@ -839,55 +895,43 @@
     def reduce_over_head(kept):
         return lax.all_to_all(kept, "head", 0, 0)
 
-    def spread_query(mine, cosine, sines, after=()):
-        block = turn_query(mine, cosine, sines, query_width, latent_width)
+    def turn(sums, cosine, sines):
+        block = turn_query(sums, cosine, sines, query_width, latent_width)
         pair = in_order([block, grid.send(block, core=1)], c)
-        pair, _ = tie(jnp.concatenate([pair[0], pair[1]], axis=-1), after)
-        return jnp.stack([pair] + [grid.send(pair, head=k) for k in range(1, heads)])
-
-    def spread_over_y(by_head):
-        return [by_head] + [grid.send(by_head, y=k) for k in range(1, ys)]
-
-    def lay_out(by_y):
-        return arrange(by_y, requests, query_width)
-
-    def make_tables(lengths, page_order):
-        pages = page_order.shape[1]
-        logical = jnp.arange(pages, dtype=jnp.int32)
-        page_of = jnp.sum(
-            jnp.where(page_order[:, :, None] == logical[None, None, :], logical[None, :, None], 0), axis=1
-        )
-        start = ((y * 2 + c) * heads + z) * span
-        positions = (
-            start + page_of[:, :, None] * PAGE + jnp.arange(PAGE, dtype=jnp.int32)[None, None, :]
-        ).reshape(requests, span)
-        new_rows = jnp.arange(FRESH, dtype=jnp.int32)
-        row_positions = jnp.concatenate(
-            [positions, lengths[:, None] + jnp.minimum(new_rows, steps - 1)[None, :]], axis=1
-        )
-        cosine, sines = sincos(row_positions)
-        lanes = max(128, HQ // KVH * steps)
-        step_of = jnp.arange(lanes, dtype=jnp.int32) % steps
-        holds_new = (y == 0) & (c == 0) & (z == 0)
-        new_seen = (new_rows[:, None] <= step_of[None, :]) & holds_new
-        live = jnp.concatenate(
-            [
-                jnp.broadcast_to((positions < lengths[:, None])[:, :, None], (requests, span, lanes)),
-                jnp.broadcast_to(new_seen[None], (requests, FRESH, lanes)),
-            ],
-            axis=1,
-        ).astype(F32)
+        return jnp.concatenate([pair[0], pair[1]], axis=-1)
+
+    def spread_over_y(pair):
+        return jnp.stack([pair] + [grid.send(pair, y=k) for k in range(1, ys)])
+
+    def spread_over_head(by_y):
+        return [by_y] + [grid.send(by_y, head=k) for k in range(1, heads)]
+
+    def lay_out(by_head):
+        return arrange(by_head, requests, query_width)
+
+    pages = page_order.shape[1]
+    start = ((y * 2 + c) * heads + z) * span
+
+    def make_turns(lengths):
         fresh_positions = lengths[:, None] + jnp.arange(steps, dtype=jnp.int32)[None, :]
-        return (cosine, sines, live), sincos(fresh_positions.reshape(-1))
-
-    between = [embed, reduce_over_y, reduce_over_head, spread_query, spread_over_y, lay_out]
+        positions = [
+            start + PAGE * jnp.arange(pages, dtype=jnp.int32),
+            jnp.arange(16 - pages % 16 if pages % 16 else 0, dtype=jnp.int32),
+            jnp.arange(PAGE, dtype=jnp.int32),
+            fresh_positions.reshape(-1),
+        ]
+        return sincos(jnp.concatenate(positions))
+
+    between = [
+        embed, reduce_over_y, reduce_over_head, turn, spread_over_y, spread_over_head, lay_out,
+    ]
     shared = ys == 2 and heads == 4 and grid.sides == 2 and depth % 512 == 0
     batch, latent, extra = (project_shared if shared else project_plain)(down_proj, between)
-    (queries, fresh), (ups, up_row), (cosine, sines, live) = extra
+    (queries, fresh), (ups, up_row), (cosine, sines) = extra
     weight = pltpu.with_memory_space_constraint(out_proj, pltpu.HBM)
     states, weight = finish(
-        span, hidden, depth, batch, latent, fresh, cosine, sines, live, queries, ups,
-        up_row, weight, heads,
+        span, hidden, depth, batch, latent, fresh, cosine, sines, queries, ups, up_row, weight,
+        heads, page_order, lengths, steps,
     )
     parts = [take(states, z)]
     for dz in range(1, heads):

time: 144 us -> 140 us (0.972)
  other arithmetic: 4.39 us -> 1.92 us
  local copies, waits for them, and re-layouts: 9.3 us -> 7.74 us
    all_to_all x1, waiting for transfers between devices: 5.85 us -> 1.28 us  [reduce_over_head(): return lax.all_to_all(kept, 'head', 0, 0)]
    ppermute x40, waiting for transfers between devices: 35.6 us -> 40.1 us  [send(): return lax.ppermute(value, AXES, pairs)]
    pallas_call x1, Pallas kernels: 4.59 us -> 2.2 us  [pick(): pl.pallas_call(pick_kernel, out_shape=(half, half), in_specs=[pl.BlockSpe...]
    neg x2 -> x1, other arithmetic: 1.67 us -> 0.17 us  [sincos(): -sines]
  transfers between devices with their start and end apart: 41 -> 41, of which waited for: 20 -> 21; matrix products, arithmetic and copies ran while one was open for 7% -> 5% of each run, Pallas kernels for 25% -> 25%
where the time goes in v3:
time: 140 us; the launch traced here: 139 us
  Pallas kernels  46.6 us (33%)
  waiting for transfers between devices  41.4 us (30%)
  starting transfers between devices  40.4 us (29%)
  local copies, waits for them, and re-layouts  7.74 us (6%)
  other arithmetic  1.92 us (1%)
    ppermute x40, waiting for transfers between devices, send(): return lax.ppermute(value, AXES, pairs)  40.1 us
    ppermute x40, starting transfers between devices, send(): return lax.ppermute(value, AXES, pairs)  37.1 us
    pallas_call x4, Pallas kernels, add_latents(): pl.pallas_call(functools.partial(latent_kernel, counts, segments, depth,...  25 us
    pallas_call x1, Pallas kernels, finish(): pl.pallas_call(functools.partial(finish_kernel, counts, segments, depth,...  7.76 us
    pallas_call x1, Pallas kernels, new_sums(): pl.pallas_call(functools.partial(new_sums_kernel, blocks), out_shape=(hal...  4.31 us
    all_to_all x1, starting transfers between devices, reduce_over_head(): return lax.all_to_all(kept, 'head', 0, 0)  3.34 us
    pallas_call x3, Pallas kernels, assemble(): pl.pallas_call(functools.partial(assemble_kernel, layout), out_shape=shap...  3.21 us
  transfers between devices with their start and end apart: 41, of which 21 were waited for; matrix products, arithmetic and copies ran while one was open for 5% of the time, Pallas kernels for 25%

profile of v3, /device:TPU:0, one launch (start us, length us, event | category | flops | bytes accessed | tf_op | source)
XLA Modules:
  0.0 139.4 jit_solution(13959998223892837297)
XLA Ops:
  2.0 3.1 %collective-permute-start.19 = (bf16[400,1024]{1,0:T(8,128)(2,1)S(1)}, bf16[400,1024]{1,0:T(8,128)(2,1)}, u32[]{:S(2)}, u32[]{:S(2)}) collective-permute-start(bf16[400,1024]{1,0:T(8,128)(2,1)S(1)} %first_piece.1), channel_id=1, source_target_pairs={{0,1},{1,2},{2,3},{3,0},{4,5},{5,6},{6,7},{7,4},{8,9},{9,10},{10,1... | collective-permute-start | bytes 2457608 | tf_op jit(solution)/shard_map/ppermute | solution.py:57
  8.5 20.5 %conditional.5 = (f32[4,16,640]{2,1,0:T(8,128)}) conditional(s32[]{:T(128)} %bitcast.5, () %tuple.62, (s32[8,4]{0,1:T(4,128)}, bf16[32256,512]{1,0:T(8,128)(2,1)}, bf16[512,8192]{1,0:T(8,128)(2,1)}, bf16[512,1024]{1,0:T(8,128)(2,1)}, s32[]{:T(128)}) %tuple.64), branch_computations={%region_0.0_spmd, %region_1.2_spmd} | conditional | flops 122898 | bytes 8028769 | solution.py:719
  9.2 2.2 %pick.1 = (bf16[16,512]{1,0:T(8,128)(2,1)S(1)}, bf16[16,512]{1,0:T(8,128)(2,1)S(1)}) custom-call(s32[8,4]{1,0:T(8,128)S(1)} %copy.13.ids_ref, bf16[32256,512]{1,0:T(8,128)(2,1)} %get-tuple-element.219.table_ref), custom_call_target="tpu_custom_call" | custom-call | tf_op jit(solution)/shard_map/cond/branch_1_fun/pick/pallas_call | solution.py:595
  15.2 4.3 %new_sums.1 = (f32[8,16,640]{2,1,0:T(8,128)S(1)}, f32[8,16,640]{2,1,0:T(8,128)S(1)}) custom-call(bf16[16,512]{1,0:T(8,128)(2,1)S(1)} %get-tuple-element.84.one_ref, bf16[16,512]{1,0:T(8,128)(2,1)S(1)} %collective-permute-done.3.other_ref, bf16[512,8192]{1,0:T(8,128)(2,1)} %get-tuple-element.220.query_far, bf16[512,1024]{1,0:T(8,128)(2,1)S(1)} %copy-done.4), custom_call_target="tpu_custom_call" | custom-call | tf_op jit(solution)/shard_map/cond/branch_1_fun/new_sums/pallas_call | solution.py:650
  21.9 6.4 %collective-permute-done.5 = f32[4,16,640]{2,1,0:T(8,128)S(1)} collective-permute-done((f32[4,16,640]{2,1,0:T(8,128)S(1)}, f32[4,16,640]{2,1,0:T(8,128)S(1)}, u32[]{:S(2)}, u32[]{:S(2)}) %collective-permute-start.5) | collective-permute-done | bytes 163872 | tf_op jit(solution)/shard_map/cond/branch_1_fun/ppermute | solution.py:57
  34.7 12.4 %conditional.6 = (f32[768,1024]{1,0:T(8,128)S(1)}, bf16[16,1024]{1,0:T(8,128)(2,1)S(1)}, bf16[16,1024]{1,0:T(8,128)(2,1)S(1)}) conditional(s32[]{:T(128)} %bitcast.5, () %tuple.66, (bf16[512,1024]{1,0:T(8,128)(2,1)}, bf16[400,1024]{1,0:T(8,128)(2,1)}, bf16[400,1024]{1,0:T(8,128)(2,1)S(1)}, bf16[768,8192]{1,0:T(8,128)(2,1)}, ...), branch_computations={%region_2.3_spmd, %region_3.4_spmd} | conditional | flops 4026531840 | bytes 26345616 | solution.py:719
  35.2 2.4 %collective-permute-done.refs_1_ = bf16[512,1024]{1,0:T(8,128)(2,1)S(1)} collective-permute-done((bf16[512,1024]{1,0:T(8,128)(2,1)}, bf16[512,1024]{1,0:T(8,128)(2,1)S(1)}, u32[]{:S(2)}, u32[]{:S(2)}) %collective-permute-start) | collective-permute-done | bytes 1048608 | tf_op jit(solution)/shard_map/cond/branch_1_fun/ppermute | solution.py:57
  39.9 7.2 %latents.4 = f32[768,1024]{1,0:T(8,128)S(1)} custom-call(bf16[768,8192]{1,0:T(8,128)(2,1)} %get-tuple-element.91.hidden_ref, bf16[512,1024]{1,0:T(8,128)(2,1)} %get-tuple-element.92.refs_0_, bf16[512,1024]{1,0:T(8,128)(2,1)S(1)} %collective-permute-done.refs_1_, bf16[400,1024]{1,0:T(8,128)(2,1)} %get-tuple-element.93.refs_2_, ...), custom_call_target="tpu_custom_call" | custom-call | flops 4026531840 | bytes 15466496 | tf_op jit(solution)/shard_map/cond/branch_1_fun/latents/pallas_call | solution.py:156
  47.1 3.6 %collective-permute-done.21.refs_0_ = bf16[400,1024]{1,0:T(8,128)(2,1)} collective-permute-done((bf16[400,1024]{1,0:T(8,128)(2,1)}, bf16[400,1024]{1,0:T(8,128)(2,1)}, u32[]{:S(2)}, u32[]{:S(2)}) %collective-permute-start.21) | collective-permute-done | bytes 819232 | tf_op jit(solution)/shard_map/ppermute | solution.py:57
  55.1 13.3 %conditional.7 = (f32[768,1024]{1,0:T(8,128)}, f32[48,128]{1,0:T(8,128)}, f32[48,128]{1,0:T(8,128)}, bf16[16,1024]{1,0:T(8,128)(2,1)S(1)}) conditional(s32[]{:T(128)} %bitcast.5, () %tuple.61, (bf16[400,1024]{1,0:T(8,128)(2,1)}, bf16[400,1024]{1,0:T(8,128)(2,1)S(1)}, bf16[256,1024]{1,0:T(8,128)(2,1)S(1)}, bf16[768,8192]{1,0:T(8,128)(2,1)}, ...), branch_computations={%region_4.5_spmd, %region_5.6_spmd} | conditional | flops 3221244160 | bytes 24569476 | solution.py:719
  57.3 2.2 %collective-permute-done.6.refs_1_ = bf16[400,1024]{1,0:T(8,128)(2,1)S(1)} collective-permute-done((bf16[400,1024]{1,0:T(8,128)(2,1)}, bf16[400,1024]{1,0:T(8,128)(2,1)S(1)}, u32[]{:S(2)}, u32[]{:S(2)}) %collective-permute-start.6) | collective-permute-done | bytes 819232 | tf_op jit(solution)/shard_map/cond/branch_1_fun/ppermute | solution.py:57
  61.7 6.7 %latents.5 = f32[768,1024]{1,0:T(8,128)} custom-call(bf16[768,8192]{1,0:T(8,128)(2,1)} %get-tuple-element.97.hidden_ref, bf16[400,1024]{1,0:T(8,128)(2,1)} %get-tuple-element.98.refs_0_, bf16[400,1024]{1,0:T(8,128)(2,1)S(1)} %collective-permute-done.6.refs_1_, bf16[400,1024]{1,0:T(8,128)(2,1)S(1)} %get-tuple-element.99.refs_2_, ...), custom_call_target="tpu_custom_call" | custom-call | flops 3221225472 | bytes 13631488 | tf_op jit(solution)/shard_map/cond/branch_1_fun/latents/pallas_call | solution.py:156
  68.4 3.2 %collective-permute-done.24.refs_0_.refs_1_ = bf16[400,1024]{1,0:T(8,128)(2,1)} collective-permute-done((bf16[400,1024]{1,0:T(8,128)(2,1)}, bf16[400,1024]{1,0:T(8,128)(2,1)}, u32[]{:S(2)}, u32[]{:S(2)}) %collective-permute-start.24) | collective-permute-done | bytes 819232 | tf_op jit(solution)/shard_map/ppermute | solution.py:57
  74.9 13.1 %conditional.8 = (f32[768,1024]{1,0:T(8,128)}, bf16[16,1152]{1,0:T(8,128)(2,1)S(1)}, bf16[16,1024]{1,0:T(8,128)(2,1)S(1)}) conditional(s32[]{:T(128)} %bitcast.5, () %tuple.73, (f32[4,16,640]{2,1,0:T(8,128)}, bf16[400,1024]{1,0:T(8,128)(2,1)}, bf16[400,1024]{1,0:T(8,128)(2,1)}, bf16[768,8192]{1,0:T(8,128)(2,1)}, f32[768,1024]{1,0:T(8,128)}, ...), branch_computations={%region_6.7_spmd, %region_7.8_spmd} | conditional | flops 2416011264 | bytes 19128504 | solution.py:719
  75.4 3.3 %all-to-all-start = ((f32[4,16,640]{2,1,0:T(8,128)}), f32[4,16,640]{2,1,0:T(8,128)S(1)}, u32[]{:S(2)}, u32[]{:S(2)}) async-start(f32[4,16,640]{2,1,0:T(8,128)} %get-tuple-element.107), calls=%async_computation | async-start | bytes 327680 | tf_op jit(solution)/shard_map/cond/branch_1_fun/all_to_all | solution.py:896
  78.8 5.5 %latents.6 = f32[768,1024]{1,0:T(8,128)} custom-call(bf16[768,8192]{1,0:T(8,128)(2,1)} %get-tuple-element.108.hidden_ref, bf16[400,1024]{1,0:T(8,128)(2,1)} %get-tuple-element.109.refs_0_, bf16[400,1024]{1,0:T(8,128)(2,1)S(1)} %collective-permute-done.9.refs_1_, bf16[400,1024]{1,0:T(8,128)(2,1)} %get-tuple-element.110.refs_2_, ...), custom_call_target="tpu_custom_call" | custom-call | flops 2415919104 | bytes 11796480 | tf_op jit(solution)/shard_map/cond/branch_1_fun/latents/pallas_call | solution.py:156
  88.6 16.9 %conditional.9 = (f32[768,1024]{1,0:T(8,128)S(1)}, bf16[4,8,32,128]{3,2,1,0:T(8,128)(2,1)S(1)}, bf16[4,8,16,128]{3,2,1,0:T(8,128)(2,1)S(1)}) conditional(s32[]{:T(128)} %bitcast.5, () %tuple.77, (bf16[16,1152]{1,0:T(8,128)(2,1)S(1)}, bf16[256,1024]{1,0:T(8,128)(2,1)}, bf16[256,1024]{1,0:T(8,128)(2,1)}, bf16[256,1024]{1,0:T(8,128)(2,1)S(1)}, ...), branch_computations={%region_8.9_spmd, %region_9.10_spmd} | conditional | flops 2415955968 | bytes 21365068 | solution.py:719
  95.9 2.1 %collective-permute-start.17 = (bf16[2,16,1152]{2,1,0:T(8,128)(2,1)S(1)}, bf16[2,16,1152]{2,1,0:T(8,128)(2,1)S(1)}, u32[]{:S(2)}, u32[]{:S(2)}) collective-permute-start(bf16[2,16,1152]{2,1,0:T(8,128)(2,1)S(1)} %pad_maximum_fusion.3.refs_0_), channel_id=1, source_target_pairs={{0,2},{1,3},{2,0},{3,1},{4,6},{5,7},{6,4},{7,5},{8,10},{9,11},{10,... | collective-permute-start | bytes 221192 | tf_op jit(solution)/shard_map/cond/branch_1_fun/ppermute | solution.py:57
  99.5 5.6 %latents.7 = f32[768,1024]{1,0:T(8,128)S(1)} custom-call(bf16[768,8192]{1,0:T(8,128)(2,1)} %get-tuple-element.117.hidden_ref, bf16[256,1024]{1,0:T(8,128)(2,1)} %get-tuple-element.123.refs_0_, bf16[256,1024]{1,0:T(8,128)(2,1)S(1)} %collective-permute-done.13.refs_1_, bf16[256,1024]{1,0:T(8,128)(2,1)} %get-tuple-element.125.refs_2_, ...), custom_call_target="tpu_custom_call" | custom-call | flops 2415919104 | bytes 11796480 | tf_op jit(solution)/shard_map/cond/branch_1_fun/latents/pallas_call | solution.py:156
  105.6 2.2 %collective-permute-done.30.refs_4_ = bf16[256,1024]{1,0:T(8,128)(2,1)} collective-permute-done((bf16[256,1024]{1,0:T(8,128)(2,1)}, bf16[256,1024]{1,0:T(8,128)(2,1)}, u32[]{:S(2)}, u32[]{:S(2)}) %collective-permute-start.30) | collective-permute-done | bytes 524320 | tf_op jit(solution)/shard_map/ppermute | solution.py:57
  107.8 7.8 %finish.1 = (bf16[4,144,128]{2,1,0:T(8,128)(2,1)S(1)}, bf16[2048,2048]{1,0:T(8,128)(2,1)S(1)}) custom-call(s32[4,12]{1,0:T(4,128)S(1)} %copy-done.2, s32[4]{0:T(128)S(1)} %copy-done.12, f32[48,128]{1,0:T(8,128)} %get-tuple-element.186.refs_0_, f32[48,128]{1,0:T(8,128)} %get-tuple-element.187.refs_1_, bf16[768,8192]{1,0:T(8,128)(2,1)} %bitcast.21, ...), custom_call_target="tpu_custom_call" | custom-call | flops 1 | bytes 1 | tf_op jit(solution)/shard_map/finish/pallas_call | solution.py:410
  117.7 2.2 %collective-permute-start.33 = (bf16[144,128]{1,0:T(8,128)(2,1)S(1)}, bf16[144,128]{1,0:T(8,128)(2,1)S(1)}, u32[]{:S(2)}, u32[]{:S(2)}) collective-permute-start(bf16[144,128]{1,0:T(8,128)(2,1)S(1)} %get-tuple-element.233), channel_id=1, source_target_pairs={{0,3},{1,0},{2,1},{3,2},{4,7},{5,4},{6,5},{7,6},{8,11},{9,8},{10,9... | collective-permute-start | bytes 110600 | tf_op jit(solution)/shard_map/ppermute | solution.py:57
  131.2 2.2 %collective-permute-start.38 = (bf16[16,2048]{1,0:T(8,128)(2,1)S(1)}, bf16[16,2048]{1,0:T(8,128)(2,1)S(1)}, u32[]{:S(2)}, u32[]{:S(2)}) collective-permute-start(bf16[16,2048]{1,0:T(8,128)(2,1)S(1)} %convert_element_type.34), channel_id=1, source_target_pairs={{0,2},{1,3},{2,0},{3,1},{4,6},{5,7},{6,4},{7,5},{8,10},{9,11},{10,... | collective-permute-start | bytes 196616 | tf_op jit(solution)/shard_map/ppermute | solution.py:57
  133.7 2.5 %collective-permute-done.37 = bf16[16,2048]{1,0:T(8,128)(2,1)S(1)} collective-permute-done((bf16[16,2048]{1,0:T(8,128)(2,1)S(1)}, bf16[16,2048]{1,0:T(8,128)(2,1)S(1)}, u32[]{:S(2)}, u32[]{:S(2)}) %collective-permute-start.37) | collective-permute-done | bytes 65568 | tf_op jit(solution)/shard_map/ppermute | solution.py:57
  (129 shorter events, 63.2 us)
Async XLA Ops:
  2.0 27.0 %collective-permute-start.19 = (bf16[400,1024]{1,0:T(8,128)(2,1)S(1)}, bf16[400,1024]{1,0:T(8,128)(2,1)}, u32[]{:S(2)}, u32[]{:S(2)}) collective-permute-start(bf16[400,1024]{1,0:T(8,128)(2,1)S(1)} %first_piece.1), channel_id=1, source_target_pairs={{0,1},{1,2},{2,3},{3,0},{4,5},{5,6},{6,7},{7,4},{8,9},{9,10},{10,1... | collective-permute-start | bytes 2457608 | tf_op jit(solution)/shard_map/ppermute | solution.py:57
  5.1 23.9 %collective-permute-start.20 = (bf16[400,1024]{1,0:T(8,128)(2,1)S(1)}, bf16[400,1024]{1,0:T(8,128)(2,1)S(1)}, u32[]{:S(2)}, u32[]{:S(2)}) collective-permute-start(bf16[400,1024]{1,0:T(8,128)(2,1)S(1)} %first_piece.1), channel_id=1, source_target_pairs={{0,8},{1,9},{2,10},{3,11},{4,12},{5,13},{6,14},{7,15},{8,0},{9,1},... | collective-permute-start | bytes 2457608 | tf_op jit(solution)/shard_map/ppermute | solution.py:57
  21.3 7.0 %collective-permute-start.5 = (f32[4,16,640]{2,1,0:T(8,128)S(1)}, f32[4,16,640]{2,1,0:T(8,128)S(1)}, u32[]{:S(2)}, u32[]{:S(2)}) collective-permute-start(f32[4,16,640]{2,1,0:T(8,128)S(1)} %dynamic-slice_bitcast_fusion), channel_id=1, source_target_pairs={{0,8},{1,9},{2,10},{3,11},{4,12},{5,13},{6,14},{7,15},{8,0},{9,1},... | collective-permute-start | bytes 491528 | tf_op jit(solution)/shard_map/cond/branch_1_fun/ppermute | solution.py:57
  29.0 21.8 %collective-permute-start.21 = (bf16[400,1024]{1,0:T(8,128)(2,1)}, bf16[400,1024]{1,0:T(8,128)(2,1)}, u32[]{:S(2)}, u32[]{:S(2)}) collective-permute-start(bf16[400,1024]{1,0:T(8,128)(2,1)} %collective-permute-done.19.refs_0_), channel_id=1, source_target_pairs={{0,1},{1,2},{2,3},{3,0},{4,5},{5,6},{6,7},{7,4},{8,9},{9,10},{10,1... | collective-permute-start | bytes 2457608 | tf_op jit(solution)/shard_map/ppermute | solution.py:57
  30.6 20.2 %collective-permute-start.22 = (bf16[400,1024]{1,0:T(8,128)(2,1)}, bf16[400,1024]{1,0:T(8,128)(2,1)S(1)}, u32[]{:S(2)}, u32[]{:S(2)}) collective-permute-start(bf16[400,1024]{1,0:T(8,128)(2,1)} %collective-permute-done.19.refs_0_), channel_id=1, source_target_pairs={{0,8},{1,9},{2,10},{3,11},{4,12},{5,13},{6,14},{7,15},{8,0},{9,1},... | collective-permute-start | bytes 2457608 | tf_op jit(solution)/shard_map/ppermute | solution.py:57
  33.1 14.0 %collective-permute-start.23 = (bf16[256,1024]{1,0:T(8,128)(2,1)S(1)}, bf16[256,1024]{1,0:T(8,128)(2,1)S(1)}, u32[]{:S(2)}, u32[]{:S(2)}) collective-permute-start(bf16[256,1024]{1,0:T(8,128)(2,1)S(1)} %assemble.3), channel_id=1, source_target_pairs={{0,16},{1,17},{2,18},{3,19},{4,20},{5,21},{6,22},{7,23},{8,24},{9,... | collective-permute-start | bytes 1572872 | tf_op jit(solution)/shard_map/ppermute | solution.py:57
  50.8 20.9 %collective-permute-start.24 = (bf16[400,1024]{1,0:T(8,128)(2,1)}, bf16[400,1024]{1,0:T(8,128)(2,1)}, u32[]{:S(2)}, u32[]{:S(2)}) collective-permute-start(bf16[400,1024]{1,0:T(8,128)(2,1)} %collective-permute-done.21.refs_0_), channel_id=1, source_target_pairs={{0,1},{1,2},{2,3},{3,0},{4,5},{5,6},{6,7},{7,4},{8,9},{9,10},{10,1... | collective-permute-start | bytes 2457608 | tf_op jit(solution)/shard_map/ppermute | solution.py:57
  51.8 19.9 %collective-permute-start.25 = (bf16[400,1024]{1,0:T(8,128)(2,1)}, bf16[400,1024]{1,0:T(8,128)(2,1)}, u32[]{:S(2)}, u32[]{:S(2)}) collective-permute-start(bf16[400,1024]{1,0:T(8,128)(2,1)} %collective-permute-done.21.refs_0_), channel_id=1, source_target_pairs={{0,8},{1,9},{2,10},{3,11},{4,12},{5,13},{6,14},{7,15},{8,0},{9,1},... | collective-permute-start | bytes 2457608 | tf_op jit(solution)/shard_map/ppermute | solution.py:57
  53.4 15.0 %collective-permute-start.26 = (bf16[256,1024]{1,0:T(8,128)(2,1)S(1)}, bf16[256,1024]{1,0:T(8,128)(2,1)}, u32[]{:S(2)}, u32[]{:S(2)}) collective-permute-start(bf16[256,1024]{1,0:T(8,128)(2,1)S(1)} %assemble.4), channel_id=1, source_target_pairs={{0,16},{1,17},{2,18},{3,19},{4,20},{5,21},{6,22},{7,23},{8,24},{9,... | collective-permute-start | bytes 1572872 | tf_op jit(solution)/shard_map/ppermute | solution.py:57
  55.9 4.8 %collective-permute-start.7 = (bf16[400,1024]{1,0:T(8,128)(2,1)S(1)}, bf16[400,1024]{1,0:T(8,128)(2,1)S(1)}, u32[]{:S(2)}, u32[]{:S(2)}) collective-permute-start(bf16[400,1024]{1,0:T(8,128)(2,1)S(1)} %get-tuple-element.99.refs_2_), channel_id=1, source_target_pairs={{0,4},{1,5},{2,6},{3,7},{4,0},{5,1},{6,2},{7,3},{8,12},{9,13},{10,... | collective-permute-start | bytes 2457608 | tf_op jit(solution)/shard_map/cond/branch_1_fun/ppermute | solution.py:57
  72.9 15.1 %collective-permute-start.27 = (bf16[256,1024]{1,0:T(8,128)(2,1)S(1)}, bf16[256,1024]{1,0:T(8,128)(2,1)S(1)}, u32[]{:S(2)}, u32[]{:S(2)}) collective-permute-start(bf16[256,1024]{1,0:T(8,128)(2,1)S(1)} %get-tuple-element.192), channel_id=1, source_target_pairs={{0,16},{1,17},{2,18},{3,19},{4,20},{5,21},{6,22},{7,23},{8,24},{9,... | collective-permute-start | bytes 1572872 | tf_op jit(solution)/shard_map/ppermute | solution.py:57
  74.9 13.1 %collective-permute-start.28 = (bf16[256,1024]{1,0:T(8,128)(2,1)S(1)}, bf16[256,1024]{1,0:T(8,128)(2,1)}, u32[]{:S(2)}, u32[]{:S(2)}) collective-permute-start(bf16[256,1024]{1,0:T(8,128)(2,1)S(1)} %get-tuple-element.193), channel_id=1, source_target_pairs={{0,8},{1,9},{2,10},{3,11},{4,12},{5,13},{6,14},{7,15},{8,0},{9,1},... | collective-permute-start | bytes 1572872 | tf_op jit(solution)/shard_map/ppermute | solution.py:57
  75.4 10.2 %all-to-all-start = ((f32[4,16,640]{2,1,0:T(8,128)}), f32[4,16,640]{2,1,0:T(8,128)S(1)}, u32[]{:S(2)}, u32[]{:S(2)}) async-start(f32[4,16,640]{2,1,0:T(8,128)} %get-tuple-element.107), calls=%async_computation | async-start | bytes 327680 | tf_op jit(solution)/shard_map/cond/branch_1_fun/all_to_all | solution.py:896
  88.0 17.5 %collective-permute-start.29 = (bf16[256,1024]{1,0:T(8,128)(2,1)}, bf16[256,1024]{1,0:T(8,128)(2,1)}, u32[]{:S(2)}, u32[]{:S(2)}) collective-permute-start(bf16[256,1024]{1,0:T(8,128)(2,1)} %collective-permute-done.28), channel_id=1, source_target_pairs={{0,16},{1,17},{2,18},{3,19},{4,20},{5,21},{6,22},{7,23},{8,24},{9,... | collective-permute-start | bytes 1572872 | tf_op jit(solution)/shard_map/ppermute | solution.py:57
  88.8 6.1 %collective-permute-start.14 = (bf16[256,1024]{1,0:T(8,128)(2,1)}, bf16[256,1024]{1,0:T(8,128)(2,1)S(1)}, u32[]{:S(2)}, u32[]{:S(2)}) collective-permute-start(bf16[256,1024]{1,0:T(8,128)(2,1)} %get-tuple-element.125.refs_2_), channel_id=1, source_target_pairs={{0,4},{1,5},{2,6},{3,7},{4,0},{5,1},{6,2},{7,3},{8,12},{9,13},{10,... | collective-permute-start | bytes 1572872 | tf_op jit(solution)/shard_map/cond/branch_1_fun/ppermute | solution.py:57
  94.9 10.3 %collective-permute-start.16 = (bf16[2,16,1152]{2,1,0:T(8,128)(2,1)S(1)}, bf16[2,16,1152]{2,1,0:T(8,128)(2,1)S(1)}, u32[]{:S(2)}, u32[]{:S(2)}) collective-permute-start(bf16[2,16,1152]{2,1,0:T(8,128)(2,1)S(1)} %pad_maximum_fusion.3.refs_0_), channel_id=1, source_target_pairs={{0,1},{1,2},{2,3},{3,0},{4,5},{5,6},{6,7},{7,4},{8,9},{9,10},{10,1... | collective-permute-start | bytes 221192 | tf_op jit(solution)/shard_map/cond/branch_1_fun/ppermute | solution.py:57
  95.9 9.2 %collective-permute-start.17 = (bf16[2,16,1152]{2,1,0:T(8,128)(2,1)S(1)}, bf16[2,16,1152]{2,1,0:T(8,128)(2,1)S(1)}, u32[]{:S(2)}, u32[]{:S(2)}) collective-permute-start(bf16[2,16,1152]{2,1,0:T(8,128)(2,1)S(1)} %pad_maximum_fusion.3.refs_0_), channel_id=1, source_target_pairs={{0,2},{1,3},{2,0},{3,1},{4,6},{5,7},{6,4},{7,5},{8,10},{9,11},{10,... | collective-permute-start | bytes 221192 | tf_op jit(solution)/shard_map/cond/branch_1_fun/ppermute | solution.py:57
  98.0 7.1 %collective-permute-start.18 = (bf16[2,16,1152]{2,1,0:T(8,128)(2,1)S(1)}, bf16[2,16,1152]{2,1,0:T(8,128)(2,1)S(1)}, u32[]{:S(2)}, u32[]{:S(2)}) collective-permute-start(bf16[2,16,1152]{2,1,0:T(8,128)(2,1)S(1)} %pad_maximum_fusion.3.refs_0_), channel_id=1, source_target_pairs={{0,3},{1,0},{2,1},{3,2},{4,7},{5,4},{6,5},{7,6},{8,11},{9,8},{10,9... | collective-permute-start | bytes 221192 | tf_op jit(solution)/shard_map/cond/branch_1_fun/ppermute | solution.py:57
  115.6 6.2 %collective-permute-start.31 = (bf16[144,128]{1,0:T(8,128)(2,1)S(1)}, bf16[144,128]{1,0:T(8,128)(2,1)S(1)}, u32[]{:S(2)}, u32[]{:S(2)}) collective-permute-start(bf16[144,128]{1,0:T(8,128)(2,1)S(1)} %get-tuple-element.235), channel_id=1, source_target_pairs={{0,1},{1,2},{2,3},{3,0},{4,5},{5,6},{6,7},{7,4},{8,9},{9,10},{10,1... | collective-permute-start | bytes 110600 | tf_op jit(solution)/shard_map/ppermute | solution.py:57
  116.4 5.9 %collective-permute-start.32 = (bf16[144,128]{1,0:T(8,128)(2,1)S(1)}, bf16[144,128]{1,0:T(8,128)(2,1)S(1)}, u32[]{:S(2)}, u32[]{:S(2)}) collective-permute-start(bf16[144,128]{1,0:T(8,128)(2,1)S(1)} %get-tuple-element.234), channel_id=1, source_target_pairs={{0,2},{1,3},{2,0},{3,1},{4,6},{5,7},{6,4},{7,5},{8,10},{9,11},{10,... | collective-permute-start | bytes 110600 | tf_op jit(solution)/shard_map/ppermute | solution.py:57
  117.7 4.6 %collective-permute-start.33 = (bf16[144,128]{1,0:T(8,128)(2,1)S(1)}, bf16[144,128]{1,0:T(8,128)(2,1)S(1)}, u32[]{:S(2)}, u32[]{:S(2)}) collective-permute-start(bf16[144,128]{1,0:T(8,128)(2,1)S(1)} %get-tuple-element.233), channel_id=1, source_target_pairs={{0,3},{1,0},{2,1},{3,2},{4,7},{5,4},{6,5},{7,6},{8,11},{9,8},{10,9... | collective-permute-start | bytes 110600 | tf_op jit(solution)/shard_map/ppermute | solution.py:57
  129.4 6.8 %collective-permute-start.37 = (bf16[16,2048]{1,0:T(8,128)(2,1)S(1)}, bf16[16,2048]{1,0:T(8,128)(2,1)S(1)}, u32[]{:S(2)}, u32[]{:S(2)}) collective-permute-start(bf16[16,2048]{1,0:T(8,128)(2,1)S(1)} %convert_element_type.34), channel_id=1, source_target_pairs={{0,1},{1,2},{2,3},{3,0},{4,5},{5,6},{6,7},{7,4},{8,9},{9,10},{10,1... | collective-permute-start | bytes 196616 | tf_op jit(solution)/shard_map/ppermute | solution.py:57
  131.2 7.1 %collective-permute-start.38 = (bf16[16,2048]{1,0:T(8,128)(2,1)S(1)}, bf16[16,2048]{1,0:T(8,128)(2,1)S(1)}, u32[]{:S(2)}, u32[]{:S(2)}) collective-permute-start(bf16[16,2048]{1,0:T(8,128)(2,1)S(1)} %convert_element_type.34), channel_id=1, source_target_pairs={{0,2},{1,3},{2,0},{3,1},{4,6},{5,7},{6,4},{7,5},{8,10},{9,11},{10,... | collective-permute-start | bytes 196616 | tf_op jit(solution)/shard_map/ppermute | solution.py:57
  133.4 5.3 %collective-permute-start.39 = (bf16[16,2048]{1,0:T(8,128)(2,1)S(1)}, bf16[16,2048]{1,0:T(8,128)(2,1)S(1)}, u32[]{:S(2)}, u32[]{:S(2)}) collective-permute-start(bf16[16,2048]{1,0:T(8,128)(2,1)S(1)} %convert_element_type.34), channel_id=1, source_target_pairs={{0,3},{1,0},{2,1},{3,2},{4,7},{5,4},{6,5},{7,6},{8,11},{9,8},{10,9... | collective-permute-start | bytes 196616 | tf_op jit(solution)/shard_map/ppermute | solution.py:57
  (30 other events, 165.6 us)

commit v4 on v3

--- a/solution.py
+++ b/solution.py
@@ -55,6 +55,12 @@
                         )
                         pairs.append((self.flat(a, b, c, d), self.flat(*to)))
         return lax.ppermute(value, AXES, pairs)
+
+    def along_heads(self, value_for):
+        sent = {}
+        for k in sorted(range(1, self.heads), key=lambda k: -min(k, self.heads - k)):
+            sent[k] = self.send(value_for(k), head=k)
+        return [sent[k] for k in range(1, self.heads)]
 
     def place(self, dy, dc, dz):
         seq = lax.rem(self.y + self.ys - dy, self.ys) * 2 + (1 - self.c if dc else self.c)
@@ -561,11 +567,11 @@
 def pick_kernel(ids_ref, table_ref, keep_ref, send_ref, buf, sems):
     side = lax.axis_index("side")
     rows = table_ref.shape[0]
-    requests, steps = ids_ref.shape
+    steps, requests = ids_ref.shape
     count = requests * steps
     places = []
     for i in range(count):
-        place = ids_ref[i // steps, i % steps] - side * rows
+        place = ids_ref[i % steps, i // steps] - side * rows
         inside = jnp.logical_and(place >= 0, place < rows)
         place = jnp.where(inside, place, 0)
         start = pl.multiple_of(lax.div(place, FRESH) * FRESH, FRESH)
@@ -749,7 +755,8 @@
     depth = down_proj.shape[0]
     hidden = cached_hidden.reshape(requests * span, width)
     hidden = pltpu.with_memory_space_constraint(hidden, pltpu.HBM)
-    holds = new_ids[0, 0] >= 0
+    ids_by_step = new_ids.T
+    holds = ids_by_step[0, 0] >= 0
 
     def on_cores(*segments):
         return [
@@ -786,7 +793,7 @@
         r1 = grid.send(r0, head=1)
         y0 = grid.send(r0, y=1)
 
-        extra = in_a_box(holds, lambda ids: over_y(embed(ids)), tie(new_ids, r0)[0])
+        extra = in_a_box(holds, lambda ids: over_y(embed(ids)), tie(ids_by_step, r0)[0])
         r1, y0, extra = tie(r1, y0, extra)
 
         other = (3 * b, -3 * b)
@@ -869,7 +876,7 @@
                 batch = both(grid.send(ring, y=dy), (depth, dy, k, 0, 0))
         turns = make_turns(lengths)
         embed, over_y, over_head, turn, spread_y, spread, lay_out = between
-        extra = turn(over_head(over_y(embed(new_ids))), *turns)
+        extra = turn(over_head(over_y(embed(ids_by_step))), *turns)
         extra = lay_out(spread(spread_y(extra)))
         ups = [pack_up(key_up)]
         ups += [grid.send(ups[0], head=k) for k in range(1, heads)]
@@ -904,7 +911,7 @@
         return jnp.stack([pair] + [grid.send(pair, y=k) for k in range(1, ys)])
 
     def spread_over_head(by_y):
-        return [by_y] + [grid.send(by_y, head=k) for k in range(1, heads)]
+        return [by_y] + grid.along_heads(lambda k: by_y)
 
     def lay_out(by_head):
         return arrange(by_head, requests, query_width)
@@ -933,20 +940,18 @@
         span, hidden, depth, batch, latent, fresh, cosine, sines, queries, ups, up_row, weight,
         heads, page_order, lengths, steps,
     )
-    parts = [take(states, z)]
-    for dz in range(1, heads):
-        parts.append(grid.send(take(states, (z + dz) % heads), head=dz))
+    parts = [take(states, z)] + grid.along_heads(lambda k: take(states, (z + k) % heads))
     state = join_parts(parts)
     states = [state]
-    for dy in range(ys):
-        for dc in range(2):
+    for dy in range(ys - 1, -1, -1):
+        for dc in (1, 0):
             if dy or dc:
                 states.append(grid.send(state, y=dy, core=dc))
     partial_out = project_out(states, value_up, weight, requests, steps)
     sent = partial_out.astype(BF)
     attended = partial_out
-    for dz in range(1, heads):
-        attended = attended + grid.send(sent, head=dz).astype(F32)
+    for part in grid.along_heads(lambda k: sent):
+        attended = attended + part.astype(F32)
     return attended.astype(BF).reshape(requests, steps, -1)
 
 

time: 140 us -> 138 us (0.986)
  transfers between devices with their start and end apart: 41 -> 41, of which waited for: 21 -> 21; matrix products, arithmetic and copies ran while one was open for 5% -> 5% of each run, Pallas kernels for 25% -> 26%
where the time goes in v4:
time: 138 us; the launch traced here: 137 us
  Pallas kernels  46.9 us (34%)
  waiting for transfers between devices  40.4 us (29%)
  starting transfers between devices  40.2 us (29%)
  local copies, waits for them, and re-layouts  6.65 us (5%)
  other arithmetic  1.92 us (1%)
    ppermute x40, waiting for transfers between devices, send(): return lax.ppermute(value, AXES, pairs)  39.2 us
    ppermute x40, starting transfers between devices, send(): return lax.ppermute(value, AXES, pairs)  36.8 us
    pallas_call x4, Pallas kernels, add_latents(): pl.pallas_call(functools.partial(latent_kernel, counts, segments, depth,...  25 us
    pallas_call x1, Pallas kernels, finish(): pl.pallas_call(functools.partial(finish_kernel, counts, segments, depth,...  7.76 us
    pallas_call x1, Pallas kernels, new_sums(): pl.pallas_call(functools.partial(new_sums_kernel, blocks), out_shape=(hal...  4.31 us
    all_to_all x1, starting transfers between devices, reduce_over_head(): return lax.all_to_all(kept, 'head', 0, 0)  3.34 us
    pallas_call x3, Pallas kernels, assemble(): pl.pallas_call(functools.partial(assemble_kernel, layout), out_shape=shap...  3.21 us
  transfers between devices with their start and end apart: 41, of which 21 were waited for; matrix products, arithmetic and copies ran while one was open for 5% of the time, Pallas kernels for 26%

profile of v4, /device:TPU:0, one launch (start us, length us, event | category | flops | bytes accessed | tf_op | source)
XLA Modules:
  0.0 137.3 jit_solution(18145592001379575500)
XLA Ops:
  2.0 3.1 %collective-permute-start.19 = (bf16[400,1024]{1,0:T(8,128)(2,1)S(1)}, bf16[400,1024]{1,0:T(8,128)(2,1)}, u32[]{:S(2)}, u32[]{:S(2)}) collective-permute-start(bf16[400,1024]{1,0:T(8,128)(2,1)S(1)} %first_piece.1), channel_id=1, source_target_pairs={{0,1},{1,2},{2,3},{3,0},{4,5},{5,6},{6,7},{7,4},{8,9},{9,10},{10,1... | collective-permute-start | bytes 2457608 | tf_op jit(solution)/shard_map/ppermute | solution.py:57
  8.5 20.5 %conditional.5 = (f32[4,16,640]{2,1,0:T(8,128)}) conditional(s32[]{:T(128)} %bitcast.6, () %tuple.62, (s32[4,8]{1,0:T(4,128)}, bf16[32256,512]{1,0:T(8,128)(2,1)}, bf16[512,8192]{1,0:T(8,128)(2,1)}, bf16[512,1024]{1,0:T(8,128)(2,1)}, s32[]{:T(128)}) %tuple.104), branch_computations={%region_0.0_spmd, %region_1.2_spmd} | conditional | flops 122898 | bytes 8028513 | solution.py:725
  8.5 2.6 %pick.1 = (bf16[16,512]{1,0:T(8,128)(2,1)S(1)}, bf16[16,512]{1,0:T(8,128)(2,1)S(1)}) custom-call(s32[4,8]{1,0:T(4,128)} %get-tuple-element.82.ids_ref, bf16[32256,512]{1,0:T(8,128)(2,1)} %get-tuple-element.219.table_ref), custom_call_target="tpu_custom_call" | custom-call | tf_op jit(solution)/shard_map/cond/branch_1_fun/pick/pallas_call | solution.py:601
  12.6 2.3 %collective-permute-done.3.other_ref = bf16[16,512]{1,0:T(8,128)(2,1)S(1)} collective-permute-done((bf16[16,512]{1,0:T(8,128)(2,1)S(1)}, bf16[16,512]{1,0:T(8,128)(2,1)S(1)}, u32[]{:S(2)}, u32[]{:S(2)}) %collective-permute-start.3) | collective-permute-done | bytes 16416 | tf_op jit(solution)/shard_map/cond/branch_1_fun/ppermute | solution.py:57
  14.9 4.3 %new_sums.1 = (f32[8,16,640]{2,1,0:T(8,128)S(1)}, f32[8,16,640]{2,1,0:T(8,128)S(1)}) custom-call(bf16[16,512]{1,0:T(8,128)(2,1)S(1)} %get-tuple-element.84.one_ref, bf16[16,512]{1,0:T(8,128)(2,1)S(1)} %collective-permute-done.3.other_ref, bf16[512,8192]{1,0:T(8,128)(2,1)} %get-tuple-element.220.query_far, bf16[512,1024]{1,0:T(8,128)(2,1)S(1)} %copy-done.4), custom_call_target="tpu_custom_call" | custom-call | tf_op jit(solution)/shard_map/cond/branch_1_fun/new_sums/pallas_call | solution.py:656
  21.5 6.8 %collective-permute-done.5 = f32[4,16,640]{2,1,0:T(8,128)S(1)} collective-permute-done((f32[4,16,640]{2,1,0:T(8,128)S(1)}, f32[4,16,640]{2,1,0:T(8,128)S(1)}, u32[]{:S(2)}, u32[]{:S(2)}) %collective-permute-start.5) | collective-permute-done | bytes 163872 | tf_op jit(solution)/shard_map/cond/branch_1_fun/ppermute | solution.py:57
  34.7 12.4 %conditional.6 = (f32[768,1024]{1,0:T(8,128)S(1)}, bf16[16,1024]{1,0:T(8,128)(2,1)S(1)}, bf16[16,1024]{1,0:T(8,128)(2,1)S(1)}) conditional(s32[]{:T(128)} %bitcast.6, () %tuple.66, (bf16[512,1024]{1,0:T(8,128)(2,1)}, bf16[400,1024]{1,0:T(8,128)(2,1)}, bf16[400,1024]{1,0:T(8,128)(2,1)S(1)}, bf16[768,8192]{1,0:T(8,128)(2,1)}, ...), branch_computations={%region_2.3_spmd, %region_3.4_spmd} | conditional | flops 4026531840 | bytes 26345616 | solution.py:725
  35.2 2.4 %collective-permute-done.refs_1_ = bf16[512,1024]{1,0:T(8,128)(2,1)S(1)} collective-permute-done((bf16[512,1024]{1,0:T(8,128)(2,1)}, bf16[512,1024]{1,0:T(8,128)(2,1)S(1)}, u32[]{:S(2)}, u32[]{:S(2)}) %collective-permute-start) | collective-permute-done | bytes 1048608 | tf_op jit(solution)/shard_map/cond/branch_1_fun/ppermute | solution.py:57
  39.9 7.2 %latents.4 = f32[768,1024]{1,0:T(8,128)S(1)} custom-call(bf16[768,8192]{1,0:T(8,128)(2,1)} %get-tuple-element.91.hidden_ref, bf16[512,1024]{1,0:T(8,128)(2,1)} %get-tuple-element.92.refs_0_, bf16[512,1024]{1,0:T(8,128)(2,1)S(1)} %collective-permute-done.refs_1_, bf16[400,1024]{1,0:T(8,128)(2,1)} %get-tuple-element.93.refs_2_, ...), custom_call_target="tpu_custom_call" | custom-call | flops 4026531840 | bytes 15466496 | tf_op jit(solution)/shard_map/cond/branch_1_fun/latents/pallas_call | solution.py:162
  47.1 3.2 %collective-permute-done.21.refs_0_ = bf16[400,1024]{1,0:T(8,128)(2,1)} collective-permute-done((bf16[400,1024]{1,0:T(8,128)(2,1)}, bf16[400,1024]{1,0:T(8,128)(2,1)}, u32[]{:S(2)}, u32[]{:S(2)}) %collective-permute-start.21) | collective-permute-done | bytes 819232 | tf_op jit(solution)/shard_map/ppermute | solution.py:57
  55.0 13.3 %conditional.7 = (f32[768,1024]{1,0:T(8,128)}, f32[48,128]{1,0:T(8,128)}, f32[48,128]{1,0:T(8,128)}, bf16[16,1024]{1,0:T(8,128)(2,1)S(1)}) conditional(s32[]{:T(128)} %bitcast.6, () %tuple.61, (bf16[400,1024]{1,0:T(8,128)(2,1)}, bf16[400,1024]{1,0:T(8,128)(2,1)S(1)}, bf16[256,1024]{1,0:T(8,128)(2,1)S(1)}, bf16[768,8192]{1,0:T(8,128)(2,1)}, ...), branch_computations={%region_4.5_spmd, %region_5.6_spmd} | conditional | flops 3221244160 | bytes 24569476 | solution.py:725
  57.3 2.2 %collective-permute-done.6.refs_1_ = bf16[400,1024]{1,0:T(8,128)(2,1)S(1)} collective-permute-done((bf16[400,1024]{1,0:T(8,128)(2,1)}, bf16[400,1024]{1,0:T(8,128)(2,1)S(1)}, u32[]{:S(2)}, u32[]{:S(2)}) %collective-permute-start.6) | collective-permute-done | bytes 819232 | tf_op jit(solution)/shard_map/cond/branch_1_fun/ppermute | solution.py:57
  61.6 6.7 %latents.5 = f32[768,1024]{1,0:T(8,128)} custom-call(bf16[768,8192]{1,0:T(8,128)(2,1)} %get-tuple-element.97.hidden_ref, bf16[400,1024]{1,0:T(8,128)(2,1)} %get-tuple-element.98.refs_0_, bf16[400,1024]{1,0:T(8,128)(2,1)S(1)} %collective-permute-done.6.refs_1_, bf16[400,1024]{1,0:T(8,128)(2,1)S(1)} %get-tuple-element.99.refs_2_, ...), custom_call_target="tpu_custom_call" | custom-call | flops 3221225472 | bytes 13631488 | tf_op jit(solution)/shard_map/cond/branch_1_fun/latents/pallas_call | solution.py:162
  68.3 2.5 %collective-permute-done.24.refs_0_.refs_1_ = bf16[400,1024]{1,0:T(8,128)(2,1)} collective-permute-done((bf16[400,1024]{1,0:T(8,128)(2,1)}, bf16[400,1024]{1,0:T(8,128)(2,1)}, u32[]{:S(2)}, u32[]{:S(2)}) %collective-permute-start.24) | collective-permute-done | bytes 819232 | tf_op jit(solution)/shard_map/ppermute | solution.py:57
  74.2 13.0 %conditional.8 = (f32[768,1024]{1,0:T(8,128)}, bf16[16,1152]{1,0:T(8,128)(2,1)S(1)}, bf16[16,1024]{1,0:T(8,128)(2,1)S(1)}) conditional(s32[]{:T(128)} %bitcast.6, () %tuple.73, (f32[4,16,640]{2,1,0:T(8,128)}, bf16[400,1024]{1,0:T(8,128)(2,1)}, bf16[400,1024]{1,0:T(8,128)(2,1)}, bf16[768,8192]{1,0:T(8,128)(2,1)}, f32[768,1024]{1,0:T(8,128)}, ...), branch_computations={%region_6.7_spmd, %region_7.8_spmd} | conditional | flops 2416011264 | bytes 19128504 | solution.py:725
  74.7 3.3 %all-to-all-start = ((f32[4,16,640]{2,1,0:T(8,128)}), f32[4,16,640]{2,1,0:T(8,128)S(1)}, u32[]{:S(2)}, u32[]{:S(2)}) async-start(f32[4,16,640]{2,1,0:T(8,128)} %get-tuple-element.107), calls=%async_computation | async-start | bytes 327680 | tf_op jit(solution)/shard_map/cond/branch_1_fun/all_to_all | solution.py:903
  78.1 5.5 %latents.6 = f32[768,1024]{1,0:T(8,128)} custom-call(bf16[768,8192]{1,0:T(8,128)(2,1)} %get-tuple-element.108.hidden_ref, bf16[400,1024]{1,0:T(8,128)(2,1)} %get-tuple-element.109.refs_0_, bf16[400,1024]{1,0:T(8,128)(2,1)S(1)} %collective-permute-done.9.refs_1_, bf16[400,1024]{1,0:T(8,128)(2,1)} %get-tuple-element.110.refs_2_, ...), custom_call_target="tpu_custom_call" | custom-call | flops 2415919104 | bytes 11796480 | tf_op jit(solution)/shard_map/cond/branch_1_fun/latents/pallas_call | solution.py:162
  87.9 16.9 %conditional.9 = (f32[768,1024]{1,0:T(8,128)S(1)}, bf16[4,8,32,128]{3,2,1,0:T(8,128)(2,1)S(1)}, bf16[4,8,16,128]{3,2,1,0:T(8,128)(2,1)S(1)}) conditional(s32[]{:T(128)} %bitcast.6, () %tuple.77, (bf16[16,1152]{1,0:T(8,128)(2,1)S(1)}, bf16[256,1024]{1,0:T(8,128)(2,1)}, bf16[256,1024]{1,0:T(8,128)(2,1)}, bf16[256,1024]{1,0:T(8,128)(2,1)S(1)}, ...), branch_computations={%region_8.9_spmd, %region_9.10_spmd} | conditional | flops 2415955968 | bytes 21365068 | solution.py:725
  91.6 2.5 %collective-permute-done.12 = bf16[16,1152]{1,0:T(8,128)(2,1)S(1)} collective-permute-done((bf16[16,1152]{1,0:T(8,128)(2,1)S(1)}, bf16[16,1152]{1,0:T(8,128)(2,1)S(1)}, u32[]{:S(2)}, u32[]{:S(2)}) %collective-permute-start.12) | collective-permute-done | bytes 36896 | tf_op jit(solution)/shard_map/cond/branch_1_fun/ppermute | solution.py:57
  98.8 5.6 %latents.7 = f32[768,1024]{1,0:T(8,128)S(1)} custom-call(bf16[768,8192]{1,0:T(8,128)(2,1)} %get-tuple-element.117.hidden_ref, bf16[256,1024]{1,0:T(8,128)(2,1)} %get-tuple-element.123.refs_0_, bf16[256,1024]{1,0:T(8,128)(2,1)S(1)} %collective-permute-done.13.refs_1_, bf16[256,1024]{1,0:T(8,128)(2,1)} %get-tuple-element.125.refs_2_, ...), custom_call_target="tpu_custom_call" | custom-call | flops 2415919104 | bytes 11796480 | tf_op jit(solution)/shard_map/cond/branch_1_fun/latents/pallas_call | solution.py:162
  104.9 2.2 %collective-permute-done.30.refs_4_ = bf16[256,1024]{1,0:T(8,128)(2,1)} collective-permute-done((bf16[256,1024]{1,0:T(8,128)(2,1)}, bf16[256,1024]{1,0:T(8,128)(2,1)}, u32[]{:S(2)}, u32[]{:S(2)}) %collective-permute-start.30) | collective-permute-done | bytes 524320 | tf_op jit(solution)/shard_map/ppermute | solution.py:57
  107.1 7.8 %finish.1 = (bf16[4,144,128]{2,1,0:T(8,128)(2,1)S(1)}, bf16[2048,2048]{1,0:T(8,128)(2,1)S(1)}) custom-call(s32[4,12]{1,0:T(4,128)S(1)} %copy-done.2, s32[4]{0:T(128)S(1)} %copy-done.12, f32[48,128]{1,0:T(8,128)} %get-tuple-element.186.refs_0_, f32[48,128]{1,0:T(8,128)} %get-tuple-element.187.refs_1_, bf16[768,8192]{1,0:T(8,128)(2,1)} %bitcast.22, ...), custom_call_target="tpu_custom_call" | custom-call | flops 1 | bytes 1 | tf_op jit(solution)/shard_map/finish/pallas_call | solution.py:416
  117.0 2.2 %collective-permute-start.33 = (bf16[144,128]{1,0:T(8,128)(2,1)S(1)}, bf16[144,128]{1,0:T(8,128)(2,1)S(1)}, u32[]{:S(2)}, u32[]{:S(2)}) collective-permute-start(bf16[144,128]{1,0:T(8,128)(2,1)S(1)} %get-tuple-element.228), channel_id=1, source_target_pairs={{0,3},{1,0},{2,1},{3,2},{4,7},{5,4},{6,5},{7,6},{8,11},{9,8},{10,9... | collective-permute-start | bytes 110600 | tf_op jit(solution)/shard_map/ppermute | solution.py:57
  131.6 2.6 %collective-permute-done.37 = bf16[16,2048]{1,0:T(8,128)(2,1)S(1)} collective-permute-done((bf16[16,2048]{1,0:T(8,128)(2,1)S(1)}, bf16[16,2048]{1,0:T(8,128)(2,1)S(1)}, u32[]{:S(2)}, u32[]{:S(2)}) %collective-permute-start.37) | collective-permute-done | bytes 65568 | tf_op jit(solution)/shard_map/ppermute | solution.py:57
  (128 shorter events, 61.0 us)
Async XLA Ops:
  2.0 27.0 %collective-permute-start.19 = (bf16[400,1024]{1,0:T(8,128)(2,1)S(1)}, bf16[400,1024]{1,0:T(8,128)(2,1)}, u32[]{:S(2)}, u32[]{:S(2)}) collective-permute-start(bf16[400,1024]{1,0:T(8,128)(2,1)S(1)} %first_piece.1), channel_id=1, source_target_pairs={{0,1},{1,2},{2,3},{3,0},{4,5},{5,6},{6,7},{7,4},{8,9},{9,10},{10,1... | collective-permute-start | bytes 2457608 | tf_op jit(solution)/shard_map/ppermute | solution.py:57
  5.1 23.9 %collective-permute-start.20 = (bf16[400,1024]{1,0:T(8,128)(2,1)S(1)}, bf16[400,1024]{1,0:T(8,128)(2,1)S(1)}, u32[]{:S(2)}, u32[]{:S(2)}) collective-permute-start(bf16[400,1024]{1,0:T(8,128)(2,1)S(1)} %first_piece.1), channel_id=1, source_target_pairs={{0,8},{1,9},{2,10},{3,11},{4,12},{5,13},{6,14},{7,15},{8,0},{9,1},... | collective-permute-start | bytes 2457608 | tf_op jit(solution)/shard_map/ppermute | solution.py:57
  20.9 7.3 %collective-permute-start.5 = (f32[4,16,640]{2,1,0:T(8,128)S(1)}, f32[4,16,640]{2,1,0:T(8,128)S(1)}, u32[]{:S(2)}, u32[]{:S(2)}) collective-permute-start(f32[4,16,640]{2,1,0:T(8,128)S(1)} %dynamic-slice_bitcast_fusion), channel_id=1, source_target_pairs={{0,8},{1,9},{2,10},{3,11},{4,12},{5,13},{6,14},{7,15},{8,0},{9,1},... | collective-permute-start | bytes 491528 | tf_op jit(solution)/shard_map/cond/branch_1_fun/ppermute | solution.py:57
  29.0 21.4 %collective-permute-start.21 = (bf16[400,1024]{1,0:T(8,128)(2,1)}, bf16[400,1024]{1,0:T(8,128)(2,1)}, u32[]{:S(2)}, u32[]{:S(2)}) collective-permute-start(bf16[400,1024]{1,0:T(8,128)(2,1)} %collective-permute-done.19.refs_0_), channel_id=1, source_target_pairs={{0,1},{1,2},{2,3},{3,0},{4,5},{5,6},{6,7},{7,4},{8,9},{9,10},{10,1... | collective-permute-start | bytes 2457608 | tf_op jit(solution)/shard_map/ppermute | solution.py:57
  30.6 19.8 %collective-permute-start.22 = (bf16[400,1024]{1,0:T(8,128)(2,1)}, bf16[400,1024]{1,0:T(8,128)(2,1)S(1)}, u32[]{:S(2)}, u32[]{:S(2)}) collective-permute-start(bf16[400,1024]{1,0:T(8,128)(2,1)} %collective-permute-done.19.refs_0_), channel_id=1, source_target_pairs={{0,8},{1,9},{2,10},{3,11},{4,12},{5,13},{6,14},{7,15},{8,0},{9,1},... | collective-permute-start | bytes 2457608 | tf_op jit(solution)/shard_map/ppermute | solution.py:57
  33.1 14.0 %collective-permute-start.23 = (bf16[256,1024]{1,0:T(8,128)(2,1)S(1)}, bf16[256,1024]{1,0:T(8,128)(2,1)S(1)}, u32[]{:S(2)}, u32[]{:S(2)}) collective-permute-start(bf16[256,1024]{1,0:T(8,128)(2,1)S(1)} %assemble.3), channel_id=1, source_target_pairs={{0,16},{1,17},{2,18},{3,19},{4,20},{5,21},{6,22},{7,23},{8,24},{9,... | collective-permute-start | bytes 1572872 | tf_op jit(solution)/shard_map/ppermute | solution.py:57
  50.4 20.5 %collective-permute-start.24 = (bf16[400,1024]{1,0:T(8,128)(2,1)}, bf16[400,1024]{1,0:T(8,128)(2,1)}, u32[]{:S(2)}, u32[]{:S(2)}) collective-permute-start(bf16[400,1024]{1,0:T(8,128)(2,1)} %collective-permute-done.21.refs_0_), channel_id=1, source_target_pairs={{0,1},{1,2},{2,3},{3,0},{4,5},{5,6},{6,7},{7,4},{8,9},{9,10},{10,1... | collective-permute-start | bytes 2457608 | tf_op jit(solution)/shard_map/ppermute | solution.py:57
  51.4 19.5 %collective-permute-start.25 = (bf16[400,1024]{1,0:T(8,128)(2,1)}, bf16[400,1024]{1,0:T(8,128)(2,1)}, u32[]{:S(2)}, u32[]{:S(2)}) collective-permute-start(bf16[400,1024]{1,0:T(8,128)(2,1)} %collective-permute-done.21.refs_0_), channel_id=1, source_target_pairs={{0,8},{1,9},{2,10},{3,11},{4,12},{5,13},{6,14},{7,15},{8,0},{9,1},... | collective-permute-start | bytes 2457608 | tf_op jit(solution)/shard_map/ppermute | solution.py:57
  53.4 14.9 %collective-permute-start.26 = (bf16[256,1024]{1,0:T(8,128)(2,1)S(1)}, bf16[256,1024]{1,0:T(8,128)(2,1)}, u32[]{:S(2)}, u32[]{:S(2)}) collective-permute-start(bf16[256,1024]{1,0:T(8,128)(2,1)S(1)} %assemble.4), channel_id=1, source_target_pairs={{0,16},{1,17},{2,18},{3,19},{4,20},{5,21},{6,22},{7,23},{8,24},{9,... | collective-permute-start | bytes 1572872 | tf_op jit(solution)/shard_map/ppermute | solution.py:57
  55.8 4.8 %collective-permute-start.7 = (bf16[400,1024]{1,0:T(8,128)(2,1)S(1)}, bf16[400,1024]{1,0:T(8,128)(2,1)S(1)}, u32[]{:S(2)}, u32[]{:S(2)}) collective-permute-start(bf16[400,1024]{1,0:T(8,128)(2,1)S(1)} %get-tuple-element.99.refs_2_), channel_id=1, source_target_pairs={{0,4},{1,5},{2,6},{3,7},{4,0},{5,1},{6,2},{7,3},{8,12},{9,13},{10,... | collective-permute-start | bytes 2457608 | tf_op jit(solution)/shard_map/cond/branch_1_fun/ppermute | solution.py:57
  72.1 15.1 %collective-permute-start.27 = (bf16[256,1024]{1,0:T(8,128)(2,1)S(1)}, bf16[256,1024]{1,0:T(8,128)(2,1)S(1)}, u32[]{:S(2)}, u32[]{:S(2)}) collective-permute-start(bf16[256,1024]{1,0:T(8,128)(2,1)S(1)} %get-tuple-element.192), channel_id=1, source_target_pairs={{0,16},{1,17},{2,18},{3,19},{4,20},{5,21},{6,22},{7,23},{8,24},{9,... | collective-permute-start | bytes 1572872 | tf_op jit(solution)/shard_map/ppermute | solution.py:57
  73.6 13.7 %collective-permute-start.28 = (bf16[256,1024]{1,0:T(8,128)(2,1)S(1)}, bf16[256,1024]{1,0:T(8,128)(2,1)}, u32[]{:S(2)}, u32[]{:S(2)}) collective-permute-start(bf16[256,1024]{1,0:T(8,128)(2,1)S(1)} %get-tuple-element.193), channel_id=1, source_target_pairs={{0,8},{1,9},{2,10},{3,11},{4,12},{5,13},{6,14},{7,15},{8,0},{9,1},... | collective-permute-start | bytes 1572872 | tf_op jit(solution)/shard_map/ppermute | solution.py:57
  74.7 10.1 %all-to-all-start = ((f32[4,16,640]{2,1,0:T(8,128)}), f32[4,16,640]{2,1,0:T(8,128)S(1)}, u32[]{:S(2)}, u32[]{:S(2)}) async-start(f32[4,16,640]{2,1,0:T(8,128)} %get-tuple-element.107), calls=%async_computation | async-start | bytes 327680 | tf_op jit(solution)/shard_map/cond/branch_1_fun/all_to_all | solution.py:903
  87.2 17.5 %collective-permute-start.29 = (bf16[256,1024]{1,0:T(8,128)(2,1)}, bf16[256,1024]{1,0:T(8,128)(2,1)}, u32[]{:S(2)}, u32[]{:S(2)}) collective-permute-start(bf16[256,1024]{1,0:T(8,128)(2,1)} %collective-permute-done.28), channel_id=1, source_target_pairs={{0,16},{1,17},{2,18},{3,19},{4,20},{5,21},{6,22},{7,23},{8,24},{9,... | collective-permute-start | bytes 1572872 | tf_op jit(solution)/shard_map/ppermute | solution.py:57
  88.0 6.1 %collective-permute-start.14 = (bf16[256,1024]{1,0:T(8,128)(2,1)}, bf16[256,1024]{1,0:T(8,128)(2,1)S(1)}, u32[]{:S(2)}, u32[]{:S(2)}) collective-permute-start(bf16[256,1024]{1,0:T(8,128)(2,1)} %get-tuple-element.125.refs_2_), channel_id=1, source_target_pairs={{0,4},{1,5},{2,6},{3,7},{4,0},{5,1},{6,2},{7,3},{8,12},{9,13},{10,... | collective-permute-start | bytes 1572872 | tf_op jit(solution)/shard_map/cond/branch_1_fun/ppermute | solution.py:57
  94.1 10.3 %collective-permute-start.16 = (bf16[2,16,1152]{2,1,0:T(8,128)(2,1)S(1)}, bf16[2,16,1152]{2,1,0:T(8,128)(2,1)S(1)}, u32[]{:S(2)}, u32[]{:S(2)}) collective-permute-start(bf16[2,16,1152]{2,1,0:T(8,128)(2,1)S(1)} %pad_maximum_fusion.3.refs_0_), channel_id=1, source_target_pairs={{0,1},{1,2},{2,3},{3,0},{4,5},{5,6},{6,7},{7,4},{8,9},{9,10},{10,1... | collective-permute-start | bytes 221192 | tf_op jit(solution)/shard_map/cond/branch_1_fun/ppermute | solution.py:57
  95.2 9.2 %collective-permute-start.17 = (bf16[2,16,1152]{2,1,0:T(8,128)(2,1)S(1)}, bf16[2,16,1152]{2,1,0:T(8,128)(2,1)S(1)}, u32[]{:S(2)}, u32[]{:S(2)}) collective-permute-start(bf16[2,16,1152]{2,1,0:T(8,128)(2,1)S(1)} %pad_maximum_fusion.3.refs_0_), channel_id=1, source_target_pairs={{0,2},{1,3},{2,0},{3,1},{4,6},{5,7},{6,4},{7,5},{8,10},{9,11},{10,... | collective-permute-start | bytes 221192 | tf_op jit(solution)/shard_map/cond/branch_1_fun/ppermute | solution.py:57
  97.3 7.1 %collective-permute-start.18 = (bf16[2,16,1152]{2,1,0:T(8,128)(2,1)S(1)}, bf16[2,16,1152]{2,1,0:T(8,128)(2,1)S(1)}, u32[]{:S(2)}, u32[]{:S(2)}) collective-permute-start(bf16[2,16,1152]{2,1,0:T(8,128)(2,1)S(1)} %pad_maximum_fusion.3.refs_0_), channel_id=1, source_target_pairs={{0,3},{1,0},{2,1},{3,2},{4,7},{5,4},{6,5},{7,6},{8,11},{9,8},{10,9... | collective-permute-start | bytes 221192 | tf_op jit(solution)/shard_map/cond/branch_1_fun/ppermute | solution.py:57
  114.9 6.2 %collective-permute-start.31 = (bf16[144,128]{1,0:T(8,128)(2,1)S(1)}, bf16[144,128]{1,0:T(8,128)(2,1)S(1)}, u32[]{:S(2)}, u32[]{:S(2)}) collective-permute-start(bf16[144,128]{1,0:T(8,128)(2,1)S(1)} %get-tuple-element.230), channel_id=1, source_target_pairs={{0,1},{1,2},{2,3},{3,0},{4,5},{5,6},{6,7},{7,4},{8,9},{9,10},{10,1... | collective-permute-start | bytes 110600 | tf_op jit(solution)/shard_map/ppermute | solution.py:57
  115.5 6.0 %collective-permute-start.32 = (bf16[144,128]{1,0:T(8,128)(2,1)S(1)}, bf16[144,128]{1,0:T(8,128)(2,1)S(1)}, u32[]{:S(2)}, u32[]{:S(2)}) collective-permute-start(bf16[144,128]{1,0:T(8,128)(2,1)S(1)} %get-tuple-element.229), channel_id=1, source_target_pairs={{0,2},{1,3},{2,0},{3,1},{4,6},{5,7},{6,4},{7,5},{8,10},{9,11},{10,... | collective-permute-start | bytes 110600 | tf_op jit(solution)/shard_map/ppermute | solution.py:57
  117.0 4.6 %collective-permute-start.33 = (bf16[144,128]{1,0:T(8,128)(2,1)S(1)}, bf16[144,128]{1,0:T(8,128)(2,1)S(1)}, u32[]{:S(2)}, u32[]{:S(2)}) collective-permute-start(bf16[144,128]{1,0:T(8,128)(2,1)S(1)} %get-tuple-element.228), channel_id=1, source_target_pairs={{0,3},{1,0},{2,1},{3,2},{4,7},{5,4},{6,5},{7,6},{8,11},{9,8},{10,9... | collective-permute-start | bytes 110600 | tf_op jit(solution)/shard_map/ppermute | solution.py:57
  127.4 6.9 %collective-permute-start.37 = (bf16[16,2048]{1,0:T(8,128)(2,1)S(1)}, bf16[16,2048]{1,0:T(8,128)(2,1)S(1)}, u32[]{:S(2)}, u32[]{:S(2)}) collective-permute-start(bf16[16,2048]{1,0:T(8,128)(2,1)S(1)} %convert_element_type.34), channel_id=1, source_target_pairs={{0,1},{1,2},{2,3},{3,0},{4,5},{5,6},{6,7},{7,4},{8,9},{9,10},{10,1... | collective-permute-start | bytes 196616 | tf_op jit(solution)/shard_map/ppermute | solution.py:57
  129.2 7.2 %collective-permute-start.38 = (bf16[16,2048]{1,0:T(8,128)(2,1)S(1)}, bf16[16,2048]{1,0:T(8,128)(2,1)S(1)}, u32[]{:S(2)}, u32[]{:S(2)}) collective-permute-start(bf16[16,2048]{1,0:T(8,128)(2,1)S(1)} %convert_element_type.34), channel_id=1, source_target_pairs={{0,2},{1,3},{2,0},{3,1},{4,6},{5,7},{6,4},{7,5},{8,10},{9,11},{10,... | collective-permute-start | bytes 196616 | tf_op jit(solution)/shard_map/ppermute | solution.py:57
  131.3 5.3 %collective-permute-start.39 = (bf16[16,2048]{1,0:T(8,128)(2,1)S(1)}, bf16[16,2048]{1,0:T(8,128)(2,1)S(1)}, u32[]{:S(2)}, u32[]{:S(2)}) collective-permute-start(bf16[16,2048]{1,0:T(8,128)(2,1)S(1)} %convert_element_type.34), channel_id=1, source_target_pairs={{0,3},{1,0},{2,1},{3,2},{4,7},{5,4},{6,5},{7,6},{8,11},{9,8},{10,9... | collective-permute-start | bytes 196616 | tf_op jit(solution)/shard_map/ppermute | solution.py:57
  (30 other events, 164.3 us)

commit v5 on v4

--- a/solution.py
+++ b/solution.py
@@ -513,15 +513,17 @@
             order, one, (((0,), (1,)), ((), ())), preferred_element_type=F32
         ).astype(BF)
         context += [one[j * rows : (j + 1) * rows, :] for j in range(heads)]
-    out_ref[...] = jnp.dot(
+    total = jnp.dot(
         jnp.concatenate(context, axis=1), weight_ref[...], preferred_element_type=F32
     )
+    for r in range(requests):
+        out_ref[r] = total[r * steps : (r + 1) * steps, :]
 
 
 def project_out(parts, value_up, out_proj, requests, steps):
     return pl.pallas_call(
         functools.partial(project_out_kernel, requests, steps),
-        out_shape=jax.ShapeDtypeStruct((requests * steps, out_proj.shape[1]), F32),
+        out_shape=jax.ShapeDtypeStruct((requests, steps, out_proj.shape[1]), F32),
         compiler_params=pltpu.CompilerParams(vmem_limit_bytes=24 * 1024 * 1024),
         cost_estimate=pl.CostEstimate(flops=1, bytes_accessed=1, transcendentals=0),
         name="project_out",
@@ -952,7 +954,7 @@
     attended = partial_out
     for part in grid.along_heads(lambda k: sent):
         attended = attended + part.astype(F32)
-    return attended.astype(BF).reshape(requests, steps, -1)
+    return attended.astype(BF)
 
 
 def solution(mesh):

time: 138 us -> 138 us (level)
  no operation moved by 1% of the time
where the time goes in v5:
time: 138 us; the launch traced here: 137 us
  Pallas kernels  46.9 us (34%)
  waiting for transfers between devices  40.4 us (29%)
  starting transfers between devices  40.1 us (29%)
  local copies, waits for them, and re-layouts  5.99 us (4%)
  other arithmetic  2.6 us (2%)
    ppermute x40, waiting for transfers between devices, send(): return lax.ppermute(value, AXES, pairs)  39.2 us
    ppermute x40, starting transfers between devices, send(): return lax.ppermute(value, AXES, pairs)  36.8 us
    pallas_call x4, Pallas kernels, add_latents(): pl.pallas_call(functools.partial(latent_kernel, counts, segments, depth,...  25 us
    pallas_call x1, Pallas kernels, finish(): pl.pallas_call(functools.partial(finish_kernel, counts, segments, depth,...  7.76 us
    pallas_call x1, Pallas kernels, new_sums(): pl.pallas_call(functools.partial(new_sums_kernel, blocks), out_shape=(hal...  4.31 us
    all_to_all x1, starting transfers between devices, reduce_over_head(): return lax.all_to_all(kept, 'head', 0, 0)  3.34 us
    pallas_call x3, Pallas kernels, assemble(): pl.pallas_call(functools.partial(assemble_kernel, layout), out_shape=shap...  3.21 us
  transfers between devices with their start and end apart: 41, of which 21 were waited for; matrix products, arithmetic and copies ran while one was open for 5% of the time, Pallas kernels for 26%

profile of v5, /device:TPU:0, one launch (start us, length us, event | category | flops | bytes accessed | tf_op | source)
XLA Modules:
  0.0 137.3 jit_solution(403277575803379390)
XLA Ops:
  2.0 3.1 %collective-permute-start.19 = (bf16[400,1024]{1,0:T(8,128)(2,1)S(1)}, bf16[400,1024]{1,0:T(8,128)(2,1)}, u32[]{:S(2)}, u32[]{:S(2)}) collective-permute-start(bf16[400,1024]{1,0:T(8,128)(2,1)S(1)} %first_piece.1), channel_id=1, source_target_pairs={{0,1},{1,2},{2,3},{3,0},{4,5},{5,6},{6,7},{7,4},{8,9},{9,10},{10,1... | collective-permute-start | bytes 2457608 | tf_op jit(solution)/shard_map/ppermute | solution.py:57
  8.5 20.5 %conditional.5 = (f32[4,16,640]{2,1,0:T(8,128)}) conditional(s32[]{:T(128)} %bitcast.6, () %tuple.62, (s32[4,8]{1,0:T(4,128)}, bf16[32256,512]{1,0:T(8,128)(2,1)}, bf16[512,8192]{1,0:T(8,128)(2,1)}, bf16[512,1024]{1,0:T(8,128)(2,1)}, s32[]{:T(128)}) %tuple.104), branch_computations={%region_0.0_spmd, %region_1.2_spmd} | conditional | flops 122898 | bytes 8028513 | solution.py:727
  8.5 2.5 %pick.1 = (bf16[16,512]{1,0:T(8,128)(2,1)S(1)}, bf16[16,512]{1,0:T(8,128)(2,1)S(1)}) custom-call(s32[4,8]{1,0:T(4,128)} %get-tuple-element.82.ids_ref, bf16[32256,512]{1,0:T(8,128)(2,1)} %get-tuple-element.219.table_ref), custom_call_target="tpu_custom_call" | custom-call | tf_op jit(solution)/shard_map/cond/branch_1_fun/pick/pallas_call | solution.py:603
  12.5 2.3 %collective-permute-done.3.other_ref = bf16[16,512]{1,0:T(8,128)(2,1)S(1)} collective-permute-done((bf16[16,512]{1,0:T(8,128)(2,1)S(1)}, bf16[16,512]{1,0:T(8,128)(2,1)S(1)}, u32[]{:S(2)}, u32[]{:S(2)}) %collective-permute-start.3) | collective-permute-done | bytes 16416 | tf_op jit(solution)/shard_map/cond/branch_1_fun/ppermute | solution.py:57
  14.8 4.3 %new_sums.1 = (f32[8,16,640]{2,1,0:T(8,128)S(1)}, f32[8,16,640]{2,1,0:T(8,128)S(1)}) custom-call(bf16[16,512]{1,0:T(8,128)(2,1)S(1)} %get-tuple-element.84.one_ref, bf16[16,512]{1,0:T(8,128)(2,1)S(1)} %collective-permute-done.3.other_ref, bf16[512,8192]{1,0:T(8,128)(2,1)} %get-tuple-element.220.query_far, bf16[512,1024]{1,0:T(8,128)(2,1)S(1)} %copy-done.4), custom_call_target="tpu_custom_call" | custom-call | tf_op jit(solution)/shard_map/cond/branch_1_fun/new_sums/pallas_call | solution.py:658
  21.5 6.8 %collective-permute-done.5 = f32[4,16,640]{2,1,0:T(8,128)S(1)} collective-permute-done((f32[4,16,640]{2,1,0:T(8,128)S(1)}, f32[4,16,640]{2,1,0:T(8,128)S(1)}, u32[]{:S(2)}, u32[]{:S(2)}) %collective-permute-start.5) | collective-permute-done | bytes 163872 | tf_op jit(solution)/shard_map/cond/branch_1_fun/ppermute | solution.py:57
  34.7 12.4 %conditional.6 = (f32[768,1024]{1,0:T(8,128)S(1)}, bf16[16,1024]{1,0:T(8,128)(2,1)S(1)}, bf16[16,1024]{1,0:T(8,128)(2,1)S(1)}) conditional(s32[]{:T(128)} %bitcast.6, () %tuple.66, (bf16[512,1024]{1,0:T(8,128)(2,1)}, bf16[400,1024]{1,0:T(8,128)(2,1)}, bf16[400,1024]{1,0:T(8,128)(2,1)S(1)}, bf16[768,8192]{1,0:T(8,128)(2,1)}, ...), branch_computations={%region_2.3_spmd, %region_3.4_spmd} | conditional | flops 4026531840 | bytes 26345616 | solution.py:727
  35.2 2.4 %collective-permute-done.refs_1_ = bf16[512,1024]{1,0:T(8,128)(2,1)S(1)} collective-permute-done((bf16[512,1024]{1,0:T(8,128)(2,1)}, bf16[512,1024]{1,0:T(8,128)(2,1)S(1)}, u32[]{:S(2)}, u32[]{:S(2)}) %collective-permute-start) | collective-permute-done | bytes 1048608 | tf_op jit(solution)/shard_map/cond/branch_1_fun/ppermute | solution.py:57
  39.9 7.2 %latents.4 = f32[768,1024]{1,0:T(8,128)S(1)} custom-call(bf16[768,8192]{1,0:T(8,128)(2,1)} %get-tuple-element.91.hidden_ref, bf16[512,1024]{1,0:T(8,128)(2,1)} %get-tuple-element.92.refs_0_, bf16[512,1024]{1,0:T(8,128)(2,1)S(1)} %collective-permute-done.refs_1_, bf16[400,1024]{1,0:T(8,128)(2,1)} %get-tuple-element.93.refs_2_, ...), custom_call_target="tpu_custom_call" | custom-call | flops 4026531840 | bytes 15466496 | tf_op jit(solution)/shard_map/cond/branch_1_fun/latents/pallas_call | solution.py:162
  47.1 3.2 %collective-permute-done.21.refs_0_ = bf16[400,1024]{1,0:T(8,128)(2,1)} collective-permute-done((bf16[400,1024]{1,0:T(8,128)(2,1)}, bf16[400,1024]{1,0:T(8,128)(2,1)}, u32[]{:S(2)}, u32[]{:S(2)}) %collective-permute-start.21) | collective-permute-done | bytes 819232 | tf_op jit(solution)/shard_map/ppermute | solution.py:57
  55.0 13.3 %conditional.7 = (f32[768,1024]{1,0:T(8,128)}, f32[48,128]{1,0:T(8,128)}, f32[48,128]{1,0:T(8,128)}, bf16[16,1024]{1,0:T(8,128)(2,1)S(1)}) conditional(s32[]{:T(128)} %bitcast.6, () %tuple.61, (bf16[400,1024]{1,0:T(8,128)(2,1)}, bf16[400,1024]{1,0:T(8,128)(2,1)S(1)}, bf16[256,1024]{1,0:T(8,128)(2,1)S(1)}, bf16[768,8192]{1,0:T(8,128)(2,1)}, ...), branch_computations={%region_4.5_spmd, %region_5.6_spmd} | conditional | flops 3221244160 | bytes 24569476 | solution.py:727
  57.3 2.2 %collective-permute-done.6.refs_1_ = bf16[400,1024]{1,0:T(8,128)(2,1)S(1)} collective-permute-done((bf16[400,1024]{1,0:T(8,128)(2,1)}, bf16[400,1024]{1,0:T(8,128)(2,1)S(1)}, u32[]{:S(2)}, u32[]{:S(2)}) %collective-permute-start.6) | collective-permute-done | bytes 819232 | tf_op jit(solution)/shard_map/cond/branch_1_fun/ppermute | solution.py:57
  61.6 6.7 %latents.5 = f32[768,1024]{1,0:T(8,128)} custom-call(bf16[768,8192]{1,0:T(8,128)(2,1)} %get-tuple-element.97.hidden_ref, bf16[400,1024]{1,0:T(8,128)(2,1)} %get-tuple-element.98.refs_0_, bf16[400,1024]{1,0:T(8,128)(2,1)S(1)} %collective-permute-done.6.refs_1_, bf16[400,1024]{1,0:T(8,128)(2,1)S(1)} %get-tuple-element.99.refs_2_, ...), custom_call_target="tpu_custom_call" | custom-call | flops 3221225472 | bytes 13631488 | tf_op jit(solution)/shard_map/cond/branch_1_fun/latents/pallas_call | solution.py:162
  68.3 2.5 %collective-permute-done.24.refs_0_.refs_1_ = bf16[400,1024]{1,0:T(8,128)(2,1)} collective-permute-done((bf16[400,1024]{1,0:T(8,128)(2,1)}, bf16[400,1024]{1,0:T(8,128)(2,1)}, u32[]{:S(2)}, u32[]{:S(2)}) %collective-permute-start.24) | collective-permute-done | bytes 819232 | tf_op jit(solution)/shard_map/ppermute | solution.py:57
  74.2 13.0 %conditional.8 = (f32[768,1024]{1,0:T(8,128)}, bf16[16,1152]{1,0:T(8,128)(2,1)S(1)}, bf16[16,1024]{1,0:T(8,128)(2,1)S(1)}) conditional(s32[]{:T(128)} %bitcast.6, () %tuple.73, (f32[4,16,640]{2,1,0:T(8,128)}, bf16[400,1024]{1,0:T(8,128)(2,1)}, bf16[400,1024]{1,0:T(8,128)(2,1)}, bf16[768,8192]{1,0:T(8,128)(2,1)}, f32[768,1024]{1,0:T(8,128)}, ...), branch_computations={%region_6.7_spmd, %region_7.8_spmd} | conditional | flops 2416011264 | bytes 19128504 | solution.py:727
  74.7 3.3 %all-to-all-start = ((f32[4,16,640]{2,1,0:T(8,128)}), f32[4,16,640]{2,1,0:T(8,128)S(1)}, u32[]{:S(2)}, u32[]{:S(2)}) async-start(f32[4,16,640]{2,1,0:T(8,128)} %get-tuple-element.107), calls=%async_computation | async-start | bytes 327680 | tf_op jit(solution)/shard_map/cond/branch_1_fun/all_to_all | solution.py:905
  78.1 5.5 %latents.6 = f32[768,1024]{1,0:T(8,128)} custom-call(bf16[768,8192]{1,0:T(8,128)(2,1)} %get-tuple-element.108.hidden_ref, bf16[400,1024]{1,0:T(8,128)(2,1)} %get-tuple-element.109.refs_0_, bf16[400,1024]{1,0:T(8,128)(2,1)S(1)} %collective-permute-done.9.refs_1_, bf16[400,1024]{1,0:T(8,128)(2,1)} %get-tuple-element.110.refs_2_, ...), custom_call_target="tpu_custom_call" | custom-call | flops 2415919104 | bytes 11796480 | tf_op jit(solution)/shard_map/cond/branch_1_fun/latents/pallas_call | solution.py:162
  87.9 16.9 %conditional.9 = (f32[768,1024]{1,0:T(8,128)S(1)}, bf16[4,8,32,128]{3,2,1,0:T(8,128)(2,1)S(1)}, bf16[4,8,16,128]{3,2,1,0:T(8,128)(2,1)S(1)}) conditional(s32[]{:T(128)} %bitcast.6, () %tuple.77, (bf16[16,1152]{1,0:T(8,128)(2,1)S(1)}, bf16[256,1024]{1,0:T(8,128)(2,1)}, bf16[256,1024]{1,0:T(8,128)(2,1)}, bf16[256,1024]{1,0:T(8,128)(2,1)S(1)}, ...), branch_computations={%region_8.9_spmd, %region_9.10_spmd} | conditional | flops 2415955968 | bytes 21365068 | solution.py:727
  91.6 2.5 %collective-permute-done.12 = bf16[16,1152]{1,0:T(8,128)(2,1)S(1)} collective-permute-done((bf16[16,1152]{1,0:T(8,128)(2,1)S(1)}, bf16[16,1152]{1,0:T(8,128)(2,1)S(1)}, u32[]{:S(2)}, u32[]{:S(2)}) %collective-permute-start.12) | collective-permute-done | bytes 36896 | tf_op jit(solution)/shard_map/cond/branch_1_fun/ppermute | solution.py:57
  98.8 5.6 %latents.7 = f32[768,1024]{1,0:T(8,128)S(1)} custom-call(bf16[768,8192]{1,0:T(8,128)(2,1)} %get-tuple-element.117.hidden_ref, bf16[256,1024]{1,0:T(8,128)(2,1)} %get-tuple-element.123.refs_0_, bf16[256,1024]{1,0:T(8,128)(2,1)S(1)} %collective-permute-done.13.refs_1_, bf16[256,1024]{1,0:T(8,128)(2,1)} %get-tuple-element.125.refs_2_, ...), custom_call_target="tpu_custom_call" | custom-call | flops 2415919104 | bytes 11796480 | tf_op jit(solution)/shard_map/cond/branch_1_fun/latents/pallas_call | solution.py:162
  104.9 2.2 %collective-permute-done.30.refs_4_ = bf16[256,1024]{1,0:T(8,128)(2,1)} collective-permute-done((bf16[256,1024]{1,0:T(8,128)(2,1)}, bf16[256,1024]{1,0:T(8,128)(2,1)}, u32[]{:S(2)}, u32[]{:S(2)}) %collective-permute-start.30) | collective-permute-done | bytes 524320 | tf_op jit(solution)/shard_map/ppermute | solution.py:57
  107.1 7.8 %finish.1 = (bf16[4,144,128]{2,1,0:T(8,128)(2,1)S(1)}, bf16[2048,2048]{1,0:T(8,128)(2,1)S(1)}) custom-call(s32[4,12]{1,0:T(4,128)S(1)} %copy-done.2, s32[4]{0:T(128)S(1)} %copy-done.12, f32[48,128]{1,0:T(8,128)} %get-tuple-element.186.refs_0_, f32[48,128]{1,0:T(8,128)} %get-tuple-element.187.refs_1_, bf16[768,8192]{1,0:T(8,128)(2,1)} %bitcast.22, ...), custom_call_target="tpu_custom_call" | custom-call | flops 1 | bytes 1 | tf_op jit(solution)/shard_map/finish/pallas_call | solution.py:416
  117.0 2.2 %collective-permute-start.33 = (bf16[144,128]{1,0:T(8,128)(2,1)S(1)}, bf16[144,128]{1,0:T(8,128)(2,1)S(1)}, u32[]{:S(2)}, u32[]{:S(2)}) collective-permute-start(bf16[144,128]{1,0:T(8,128)(2,1)S(1)} %get-tuple-element.228), channel_id=1, source_target_pairs={{0,3},{1,0},{2,1},{3,2},{4,7},{5,4},{6,5},{7,6},{8,11},{9,8},{10,9... | collective-permute-start | bytes 110600 | tf_op jit(solution)/shard_map/ppermute | solution.py:57
  131.7 2.6 %collective-permute-done.37 = bf16[4,4,2048]{2,1,0:T(4,128)(2,1)S(1)} collective-permute-done((bf16[4,4,2048]{2,1,0:T(4,128)(2,1)S(1)}, bf16[4,4,2048]{2,1,0:T(4,128)(2,1)S(1)}, u32[]{:S(2)}, u32[]{:S(2)}) %collective-permute-start.37) | collective-permute-done | bytes 65568 | tf_op jit(solution)/shard_map/ppermute | solution.py:57
  (127 shorter events, 61.0 us)
Async XLA Ops:
  2.0 27.0 %collective-permute-start.19 = (bf16[400,1024]{1,0:T(8,128)(2,1)S(1)}, bf16[400,1024]{1,0:T(8,128)(2,1)}, u32[]{:S(2)}, u32[]{:S(2)}) collective-permute-start(bf16[400,1024]{1,0:T(8,128)(2,1)S(1)} %first_piece.1), channel_id=1, source_target_pairs={{0,1},{1,2},{2,3},{3,0},{4,5},{5,6},{6,7},{7,4},{8,9},{9,10},{10,1... | collective-permute-start | bytes 2457608 | tf_op jit(solution)/shard_map/ppermute | solution.py:57
  5.1 23.9 %collective-permute-start.20 = (bf16[400,1024]{1,0:T(8,128)(2,1)S(1)}, bf16[400,1024]{1,0:T(8,128)(2,1)S(1)}, u32[]{:S(2)}, u32[]{:S(2)}) collective-permute-start(bf16[400,1024]{1,0:T(8,128)(2,1)S(1)} %first_piece.1), channel_id=1, source_target_pairs={{0,8},{1,9},{2,10},{3,11},{4,12},{5,13},{6,14},{7,15},{8,0},{9,1},... | collective-permute-start | bytes 2457608 | tf_op jit(solution)/shard_map/ppermute | solution.py:57
  20.9 7.4 %collective-permute-start.5 = (f32[4,16,640]{2,1,0:T(8,128)S(1)}, f32[4,16,640]{2,1,0:T(8,128)S(1)}, u32[]{:S(2)}, u32[]{:S(2)}) collective-permute-start(f32[4,16,640]{2,1,0:T(8,128)S(1)} %dynamic-slice_bitcast_fusion), channel_id=1, source_target_pairs={{0,8},{1,9},{2,10},{3,11},{4,12},{5,13},{6,14},{7,15},{8,0},{9,1},... | collective-permute-start | bytes 491528 | tf_op jit(solution)/shard_map/cond/branch_1_fun/ppermute | solution.py:57
  29.0 21.4 %collective-permute-start.21 = (bf16[400,1024]{1,0:T(8,128)(2,1)}, bf16[400,1024]{1,0:T(8,128)(2,1)}, u32[]{:S(2)}, u32[]{:S(2)}) collective-permute-start(bf16[400,1024]{1,0:T(8,128)(2,1)} %collective-permute-done.19.refs_0_), channel_id=1, source_target_pairs={{0,1},{1,2},{2,3},{3,0},{4,5},{5,6},{6,7},{7,4},{8,9},{9,10},{10,1... | collective-permute-start | bytes 2457608 | tf_op jit(solution)/shard_map/ppermute | solution.py:57
  30.6 19.8 %collective-permute-start.22 = (bf16[400,1024]{1,0:T(8,128)(2,1)}, bf16[400,1024]{1,0:T(8,128)(2,1)S(1)}, u32[]{:S(2)}, u32[]{:S(2)}) collective-permute-start(bf16[400,1024]{1,0:T(8,128)(2,1)} %collective-permute-done.19.refs_0_), channel_id=1, source_target_pairs={{0,8},{1,9},{2,10},{3,11},{4,12},{5,13},{6,14},{7,15},{8,0},{9,1},... | collective-permute-start | bytes 2457608 | tf_op jit(solution)/shard_map/ppermute | solution.py:57
  33.1 14.0 %collective-permute-start.23 = (bf16[256,1024]{1,0:T(8,128)(2,1)S(1)}, bf16[256,1024]{1,0:T(8,128)(2,1)S(1)}, u32[]{:S(2)}, u32[]{:S(2)}) collective-permute-start(bf16[256,1024]{1,0:T(8,128)(2,1)S(1)} %assemble.3), channel_id=1, source_target_pairs={{0,16},{1,17},{2,18},{3,19},{4,20},{5,21},{6,22},{7,23},{8,24},{9,... | collective-permute-start | bytes 1572872 | tf_op jit(solution)/shard_map/ppermute | solution.py:57
  50.4 20.5 %collective-permute-start.24 = (bf16[400,1024]{1,0:T(8,128)(2,1)}, bf16[400,1024]{1,0:T(8,128)(2,1)}, u32[]{:S(2)}, u32[]{:S(2)}) collective-permute-start(bf16[400,1024]{1,0:T(8,128)(2,1)} %collective-permute-done.21.refs_0_), channel_id=1, source_target_pairs={{0,1},{1,2},{2,3},{3,0},{4,5},{5,6},{6,7},{7,4},{8,9},{9,10},{10,1... | collective-permute-start | bytes 2457608 | tf_op jit(solution)/shard_map/ppermute | solution.py:57
  51.4 19.5 %collective-permute-start.25 = (bf16[400,1024]{1,0:T(8,128)(2,1)}, bf16[400,1024]{1,0:T(8,128)(2,1)}, u32[]{:S(2)}, u32[]{:S(2)}) collective-permute-start(bf16[400,1024]{1,0:T(8,128)(2,1)} %collective-permute-done.21.refs_0_), channel_id=1, source_target_pairs={{0,8},{1,9},{2,10},{3,11},{4,12},{5,13},{6,14},{7,15},{8,0},{9,1},... | collective-permute-start | bytes 2457608 | tf_op jit(solution)/shard_map/ppermute | solution.py:57
  53.4 14.9 %collective-permute-start.26 = (bf16[256,1024]{1,0:T(8,128)(2,1)S(1)}, bf16[256,1024]{1,0:T(8,128)(2,1)}, u32[]{:S(2)}, u32[]{:S(2)}) collective-permute-start(bf16[256,1024]{1,0:T(8,128)(2,1)S(1)} %assemble.4), channel_id=1, source_target_pairs={{0,16},{1,17},{2,18},{3,19},{4,20},{5,21},{6,22},{7,23},{8,24},{9,... | collective-permute-start | bytes 1572872 | tf_op jit(solution)/shard_map/ppermute | solution.py:57
  55.8 4.8 %collective-permute-start.7 = (bf16[400,1024]{1,0:T(8,128)(2,1)S(1)}, bf16[400,1024]{1,0:T(8,128)(2,1)S(1)}, u32[]{:S(2)}, u32[]{:S(2)}) collective-permute-start(bf16[400,1024]{1,0:T(8,128)(2,1)S(1)} %get-tuple-element.99.refs_2_), channel_id=1, source_target_pairs={{0,4},{1,5},{2,6},{3,7},{4,0},{5,1},{6,2},{7,3},{8,12},{9,13},{10,... | collective-permute-start | bytes 2457608 | tf_op jit(solution)/shard_map/cond/branch_1_fun/ppermute | solution.py:57
  72.1 15.2 %collective-permute-start.27 = (bf16[256,1024]{1,0:T(8,128)(2,1)S(1)}, bf16[256,1024]{1,0:T(8,128)(2,1)S(1)}, u32[]{:S(2)}, u32[]{:S(2)}) collective-permute-start(bf16[256,1024]{1,0:T(8,128)(2,1)S(1)} %get-tuple-element.192), channel_id=1, source_target_pairs={{0,16},{1,17},{2,18},{3,19},{4,20},{5,21},{6,22},{7,23},{8,24},{9,... | collective-permute-start | bytes 1572872 | tf_op jit(solution)/shard_map/ppermute | solution.py:57
  73.5 13.8 %collective-permute-start.28 = (bf16[256,1024]{1,0:T(8,128)(2,1)S(1)}, bf16[256,1024]{1,0:T(8,128)(2,1)}, u32[]{:S(2)}, u32[]{:S(2)}) collective-permute-start(bf16[256,1024]{1,0:T(8,128)(2,1)S(1)} %get-tuple-element.193), channel_id=1, source_target_pairs={{0,8},{1,9},{2,10},{3,11},{4,12},{5,13},{6,14},{7,15},{8,0},{9,1},... | collective-permute-start | bytes 1572872 | tf_op jit(solution)/shard_map/ppermute | solution.py:57
  74.7 10.1 %all-to-all-start = ((f32[4,16,640]{2,1,0:T(8,128)}), f32[4,16,640]{2,1,0:T(8,128)S(1)}, u32[]{:S(2)}, u32[]{:S(2)}) async-start(f32[4,16,640]{2,1,0:T(8,128)} %get-tuple-element.107), calls=%async_computation | async-start | bytes 327680 | tf_op jit(solution)/shard_map/cond/branch_1_fun/all_to_all | solution.py:905
  87.2 17.5 %collective-permute-start.29 = (bf16[256,1024]{1,0:T(8,128)(2,1)}, bf16[256,1024]{1,0:T(8,128)(2,1)}, u32[]{:S(2)}, u32[]{:S(2)}) collective-permute-start(bf16[256,1024]{1,0:T(8,128)(2,1)} %collective-permute-done.28), channel_id=1, source_target_pairs={{0,16},{1,17},{2,18},{3,19},{4,20},{5,21},{6,22},{7,23},{8,24},{9,... | collective-permute-start | bytes 1572872 | tf_op jit(solution)/shard_map/ppermute | solution.py:57
  88.0 6.1 %collective-permute-start.14 = (bf16[256,1024]{1,0:T(8,128)(2,1)}, bf16[256,1024]{1,0:T(8,128)(2,1)S(1)}, u32[]{:S(2)}, u32[]{:S(2)}) collective-permute-start(bf16[256,1024]{1,0:T(8,128)(2,1)} %get-tuple-element.125.refs_2_), channel_id=1, source_target_pairs={{0,4},{1,5},{2,6},{3,7},{4,0},{5,1},{6,2},{7,3},{8,12},{9,13},{10,... | collective-permute-start | bytes 1572872 | tf_op jit(solution)/shard_map/cond/branch_1_fun/ppermute | solution.py:57
  94.1 10.3 %collective-permute-start.16 = (bf16[2,16,1152]{2,1,0:T(8,128)(2,1)S(1)}, bf16[2,16,1152]{2,1,0:T(8,128)(2,1)S(1)}, u32[]{:S(2)}, u32[]{:S(2)}) collective-permute-start(bf16[2,16,1152]{2,1,0:T(8,128)(2,1)S(1)} %pad_maximum_fusion.3.refs_0_), channel_id=1, source_target_pairs={{0,1},{1,2},{2,3},{3,0},{4,5},{5,6},{6,7},{7,4},{8,9},{9,10},{10,1... | collective-permute-start | bytes 221192 | tf_op jit(solution)/shard_map/cond/branch_1_fun/ppermute | solution.py:57
  95.2 9.2 %collective-permute-start.17 = (bf16[2,16,1152]{2,1,0:T(8,128)(2,1)S(1)}, bf16[2,16,1152]{2,1,0:T(8,128)(2,1)S(1)}, u32[]{:S(2)}, u32[]{:S(2)}) collective-permute-start(bf16[2,16,1152]{2,1,0:T(8,128)(2,1)S(1)} %pad_maximum_fusion.3.refs_0_), channel_id=1, source_target_pairs={{0,2},{1,3},{2,0},{3,1},{4,6},{5,7},{6,4},{7,5},{8,10},{9,11},{10,... | collective-permute-start | bytes 221192 | tf_op jit(solution)/shard_map/cond/branch_1_fun/ppermute | solution.py:57
  97.3 7.1 %collective-permute-start.18 = (bf16[2,16,1152]{2,1,0:T(8,128)(2,1)S(1)}, bf16[2,16,1152]{2,1,0:T(8,128)(2,1)S(1)}, u32[]{:S(2)}, u32[]{:S(2)}) collective-permute-start(bf16[2,16,1152]{2,1,0:T(8,128)(2,1)S(1)} %pad_maximum_fusion.3.refs_0_), channel_id=1, source_target_pairs={{0,3},{1,0},{2,1},{3,2},{4,7},{5,4},{6,5},{7,6},{8,11},{9,8},{10,9... | collective-permute-start | bytes 221192 | tf_op jit(solution)/shard_map/cond/branch_1_fun/ppermute | solution.py:57
  114.9 6.2 %collective-permute-start.31 = (bf16[144,128]{1,0:T(8,128)(2,1)S(1)}, bf16[144,128]{1,0:T(8,128)(2,1)S(1)}, u32[]{:S(2)}, u32[]{:S(2)}) collective-permute-start(bf16[144,128]{1,0:T(8,128)(2,1)S(1)} %get-tuple-element.230), channel_id=1, source_target_pairs={{0,1},{1,2},{2,3},{3,0},{4,5},{5,6},{6,7},{7,4},{8,9},{9,10},{10,1... | collective-permute-start | bytes 110600 | tf_op jit(solution)/shard_map/ppermute | solution.py:57
  115.5 6.0 %collective-permute-start.32 = (bf16[144,128]{1,0:T(8,128)(2,1)S(1)}, bf16[144,128]{1,0:T(8,128)(2,1)S(1)}, u32[]{:S(2)}, u32[]{:S(2)}) collective-permute-start(bf16[144,128]{1,0:T(8,128)(2,1)S(1)} %get-tuple-element.229), channel_id=1, source_target_pairs={{0,2},{1,3},{2,0},{3,1},{4,6},{5,7},{6,4},{7,5},{8,10},{9,11},{10,... | collective-permute-start | bytes 110600 | tf_op jit(solution)/shard_map/ppermute | solution.py:57
  117.0 4.6 %collective-permute-start.33 = (bf16[144,128]{1,0:T(8,128)(2,1)S(1)}, bf16[144,128]{1,0:T(8,128)(2,1)S(1)}, u32[]{:S(2)}, u32[]{:S(2)}) collective-permute-start(bf16[144,128]{1,0:T(8,128)(2,1)S(1)} %get-tuple-element.228), channel_id=1, source_target_pairs={{0,3},{1,0},{2,1},{3,2},{4,7},{5,4},{6,5},{7,6},{8,11},{9,8},{10,9... | collective-permute-start | bytes 110600 | tf_op jit(solution)/shard_map/ppermute | solution.py:57
  127.4 6.9 %collective-permute-start.37 = (bf16[4,4,2048]{2,1,0:T(4,128)(2,1)S(1)}, bf16[4,4,2048]{2,1,0:T(4,128)(2,1)S(1)}, u32[]{:S(2)}, u32[]{:S(2)}) collective-permute-start(bf16[4,4,2048]{2,1,0:T(4,128)(2,1)S(1)} %convert_element_type.34), channel_id=1, source_target_pairs={{0,1},{1,2},{2,3},{3,0},{4,5},{5,6},{6,7},{7,4},{8,9},{9,10},{10,1... | collective-permute-start | bytes 196616 | tf_op jit(solution)/shard_map/ppermute | solution.py:57
  129.2 7.1 %collective-permute-start.38 = (bf16[4,4,2048]{2,1,0:T(4,128)(2,1)S(1)}, bf16[4,4,2048]{2,1,0:T(4,128)(2,1)S(1)}, u32[]{:S(2)}, u32[]{:S(2)}) collective-permute-start(bf16[4,4,2048]{2,1,0:T(4,128)(2,1)S(1)} %convert_element_type.34), channel_id=1, source_target_pairs={{0,2},{1,3},{2,0},{3,1},{4,6},{5,7},{6,4},{7,5},{8,10},{9,11},{10,... | collective-permute-start | bytes 196616 | tf_op jit(solution)/shard_map/ppermute | solution.py:57
  131.4 5.3 %collective-permute-start.39 = (bf16[4,4,2048]{2,1,0:T(4,128)(2,1)S(1)}, bf16[4,4,2048]{2,1,0:T(4,128)(2,1)S(1)}, u32[]{:S(2)}, u32[]{:S(2)}) collective-permute-start(bf16[4,4,2048]{2,1,0:T(4,128)(2,1)S(1)} %convert_element_type.34), channel_id=1, source_target_pairs={{0,3},{1,0},{2,1},{3,2},{4,7},{5,4},{6,5},{7,6},{8,11},{9,8},{10,9... | collective-permute-start | bytes 196616 | tf_op jit(solution)/shard_map/ppermute | solution.py:57
  (30 other events, 164.3 us)
